TPU v7x, 32 devices: a whole 2x2x4 slice. The times are simulated.
32 devices in a mesh: tm: 2 (over x), rows: 16 (over z, y, core).
Axes of the slice: x: 2, y: 2, z: 4, core: 2. Of those that a mesh axis runs over, the one named last changes fastest.
Arguments:
- inverse_block: bfloat16 [2, 2048, 2048], P('tm', 'rows'), may hold values from -6 to 6
- coupling_tiles: bfloat16 [2, 64, 128, 128], P('tm', 'rows'), may hold values from -0.005859375 to 0.005859375
- tile_pos: int32 [2, 64, 2], P('tm', 'rows'), may hold values from 0 to 31
- sep_diag: bfloat16 [2, 2048, 2048], P('tm', 'rows'), as said below
- sep_cross: bfloat16 [2, 2048, 2048], P('tm', 'rows')
Outputs:
- sigma_es: float32 [2, 2048, 4096], P('tm', 'rows')
- sigma_tiles: float32 [2, 2048, 128], P('tm', 'rows')
Inputs may be any that keep to these rules, and one draw needn't show every extreme that they name: `sep_diag`: each block is symmetric.
All inputs are finite; a program needn't handle non-finite values.
Results may differ from a plain program's by a relative error of at most 0.0034.
Values may be sent and summed in bfloat16 or wider, within the bound.
No kernel may reach another device: no remote copies, remote signals or barrier semaphores. Data moves between devices by JAX's collectives and lax.ppermute only.
A program may use at most 128 MiB of HBM per device.

v0:
```python
import jax
import jax.numpy as jnp
from jax import lax
from jax.sharding import PartitionSpec as P

TILE = 128


def from_behind(array, axis, by):
    size = lax.axis_size(axis)
    pairs = [(i, i + by) for i in range(size) if 0 <= i + by < size]
    return lax.ppermute(array, axis, pairs)


def swapped(array, axis, stride):
    return lax.ppermute(array, axis, [(i, i ^ 1 << stride) for i in range(lax.axis_size(axis))])


def contract_last(left, right):
    return lax.dot_general(
        left, right, (((1,), (1,)), ((), ())), preferred_element_type=jnp.float32
    )


def shards(inverse_block, coupling_tiles, tile_pos, sep_diag, sep_cross):
    wrows = inverse_block[0]
    local_rows = wrows.shape[0]
    width = wrows.shape[1]
    tiles = coupling_tiles[0]
    positions = tile_pos[0]
    diag_left = sep_diag[0]
    cross = sep_cross[0]
    index = lax.axis_index("rows")
    row_tiles = width // TILE
    col_tiles = 2 * width // TILE
    wview = wrows.reshape(local_rows, row_tiles, TILE)
    piece_tiles = lax.all_gather(tiles, "rows", axis=0, tiled=True)
    piece_pos = lax.all_gather(positions, "rows", axis=0, tiled=True)
    wsel = jnp.take(wview, piece_pos[:, 0], axis=1)
    contrib = jnp.einsum("rkt,ktc->krc", wsel, piece_tiles, preferred_element_type=jnp.float32)
    onehot = (piece_pos[:, 1][:, None] == jnp.arange(col_tiles, dtype=jnp.int32)[None, :]).astype(
        jnp.float32
    )
    placed = jnp.einsum("krc,kj->rjc", contrib, onehot, precision=lax.Precision.HIGHEST)
    factor = placed.reshape(local_rows, 2 * width).astype(jnp.bfloat16)
    diag_right = from_behind(diag_left, "tm", -1)
    factor_left = factor[:, :width]
    factor_right = factor[:, width:]
    start = jnp.int32(0)
    piece_left = lax.all_gather(diag_left, "rows", axis=0, tiled=True)
    piece_cross = lax.all_gather(cross, "rows", axis=0, tiled=True)
    piece_right = lax.all_gather(diag_right, "rows", axis=0, tiled=True)
    span = piece_left.shape[0]
    part_left = jnp.dot(factor_left, piece_left, preferred_element_type=jnp.float32)
    part_right = jnp.dot(factor_left, piece_cross, preferred_element_type=jnp.float32)
    part_right = part_right + jnp.dot(factor_right, piece_right, preferred_element_type=jnp.float32)
    updated = jnp.concatenate([part_left, part_right], axis=1)
    extra = contract_last(factor_right, piece_cross)
    current = lax.dynamic_slice_in_dim(updated, start, span, 1)
    summed = lax.dynamic_update_slice_in_dim(updated, current + extra, start, 1)
    sigma = -summed
    rounded = sigma.astype(jnp.bfloat16)
    if local_rows < TILE:
        steps_count = (TILE // local_rows).bit_length() - 1
        block = factor
        for bit in range(steps_count):
            other = swapped(block, "rows", bit)
            lower = index >> bit & 1 == 0
            block = jnp.where(
                lower,
                jnp.concatenate([block, other], axis=0),
                jnp.concatenate([other, block], axis=0),
            )
        product = contract_last(rounded, block)
        tile_start = index * local_rows // TILE * TILE
        wtile = lax.dynamic_slice_in_dim(wrows, tile_start, TILE, 1).astype(jnp.float32)
        result_tiles = wtile - product
    else:
        many = local_rows // TILE
        product = jnp.einsum(
            "mrk,mck->mrc",
            rounded.reshape(many, TILE, 2 * width),
            factor.reshape(many, TILE, 2 * width),
            preferred_element_type=jnp.float32,
        )
        square = lax.dynamic_slice_in_dim(wrows, index * local_rows, local_rows, 1).reshape(
            many, TILE, many, TILE
        )
        wtile = jnp.stack([square[i, :, i, :] for i in range(many)]).astype(jnp.float32)
        result_tiles = (wtile - product).reshape(local_rows, TILE)
    return (sigma[None], result_tiles[None])


def solution(mesh):
    placed = (
        P("tm", "rows", None),
        P("tm", "rows", None, None),
        P("tm", "rows", None),
        P("tm", "rows", None),
        P("tm", "rows", None),
    )
    return jax.shard_map(
        shards,
        mesh=mesh,
        in_specs=placed,
        out_specs=(P("tm", "rows", None), P("tm", "rows", None)),
        check_vma=False,
    )
```

profile of v0, /device:TPU:0, one launch (start us, length us, event | category | flops | bytes accessed | tf_op | source)
XLA Modules:
  0.0 302.2 jit_solution(2456924817742031261)
XLA Ops:
  7.2 0.0 copy-start
  7.2 0.0 all-gather.11.cloned.1.call-start
  7.2 0.7 all-gather.11.cloned.1.call-update
  7.9 0.0 all-gather.15.cloned.1.call-start
  8.0 0.7 all-gather.15.cloned.1.call-update
  8.7 0.0 all-gather.13.cloned.1.call-start
  8.7 0.7 all-gather.13.cloned.1.call-update
  9.4 0.0 all-gather.9.cloned.1.call-start
  9.4 1.3 collective-permute-start
  10.7 15.1 %collective-permute-done = bf16[128,2048]{1,0:T(8,128)(2,1)S(1)} collective-permute-done((bf16[128,2048]{1,0:T(8,128)(2,1)}, bf16[128,2048]{1,0:T(8,128)(2,1)S(1)}, u32[]{:S(2)}, u32[]{:S(2)}) %collective-permute-start) | collective-permute-done | bytes 524320 | tf_op jit(solution)/shard_map/ppermute | solution.py:12
  25.8 0.0 copy-start.1
  25.8 0.8 copy-done.1
  26.6 0.0 all-gather.9.cloned.1.call-update
  26.6 0.8 copy.10
  27.4 22.9 %all-gather = s32[1,64,2]{2,0,1:T(1,128)S(1)} all-gather(s32[1,4,2]{2,0,1:T(1,128)S(1)} %copy.10), channel_id=2, replica_groups=mesh['tm'=2,'rows'=16] {'rows'}, dimensions={1}, use_global_device_ids=true | all-gather | bytes 544 | tf_op jit(solution)/shard_map/all_gather | solution.py:38
  50.3 0.1 copy.11
  50.4 0.0 copy-done
  50.4 0.3 copy.12
  50.6 0.3 copy.13
  51.0 1.0 gather_fusion
  51.9 2.3 all-gather.11.cloned.1.call-done
  54.2 2.4 fusion.14
  56.6 4.1 %fusion.19 = bf16[32,128,128]{2,0,1:T(8,128)(2,1)S(1)} fusion(f32[64,128,128]{2,1,0:T(8,128)S(1)} %fusion.14, s32[64]{0:T(128)S(1)} %get-tuple-element.2), kind=kOutput, calls=%fused_computation.20 | convolution fusion | flops 403179520 | bytes 5243136 | tf_op jit(solution)/shard_map/krc,kj->rjc/dot_general | solution.py:44
  60.7 0.5 copy.23
  61.1 69.1 %all-gather.15.cloned.1.call-done = bf16[1,2048,2048]{2,1,0:T(8,128)(2,1)} async-done(((bf16[1,128,2048]{2,1,0:T(8,128)(2,1)}), bf16[1,2048,2048]{2,1,0:T(8,128)(2,1)}) %all-gather.15.cloned.1.call-update) | async-done | bytes 8388624 | tf_op jit(solution)/shard_map/all_gather | solution.py:51
  130.2 5.6 %fusion.2 = f32[128,2048]{1,0:T(8,128)} fusion(bf16[1,2048,2048]{2,1,0:T(8,128)(2,1)} %all-gather.15.cloned.1.call-done, bf16[128,4096]{1,0:T(8,128)(2,1)S(1)} %bitcast.45), kind=kOutput, calls=%fused_computation.3 | convolution fusion | flops 1073741824 | bytes 9961472 | tf_op jit(solution)/shard_map/dot_general | solution.py:55
  135.8 69.7 %all-gather.13.cloned.1.call-done = bf16[1,2048,2048]{2,1,0:T(8,128)(2,1)} async-done(((bf16[1,128,2048]{2,1,0:T(8,128)(2,1)}), bf16[1,2048,2048]{2,1,0:T(8,128)(2,1)}) %all-gather.13.cloned.1.call-update) | async-done | bytes 8388624 | tf_op jit(solution)/shard_map/all_gather | solution.py:50
  205.6 4.6 %fusion.4 = f32[128,2048]{1,0:T(8,128)S(1)} fusion(bf16[1,2048,2048]{2,1,0:T(8,128)(2,1)} %all-gather.13.cloned.1.call-done, bf16[128,4096]{1,0:T(8,128)(2,1)S(1)} %bitcast.46), kind=kOutput, calls=%fused_computation.5 | convolution fusion | flops 1073741824 | bytes 9961472 | tf_op jit(solution)/shard_map/dot_general | solution.py:54
  210.2 70.6 %all-gather.9.cloned.1.call-done = bf16[2048,2048]{1,0:T(8,128)(2,1)} async-done(((bf16[128,2048]{1,0:T(8,128)(2,1)}), bf16[2048,2048]{1,0:T(8,128)(2,1)}) %all-gather.9.cloned.1.call-update) | async-done | bytes 8388624 | tf_op jit(solution)/shard_map/all_gather | solution.py:52
  280.8 4.9 %convolution_add_fusion = f32[128,2048]{1,0:T(8,128)S(1)} fusion(f32[128,2048]{1,0:T(8,128)} %fusion.2, bf16[2048,2048]{1,0:T(8,128)(2,1)} %all-gather.9.cloned.1.call-done, bf16[128,4096]{1,0:T(8,128)(2,1)S(1)} %bitcast.47), kind=kOutput, calls=%fused_computation.11 | convolution fusion | flops 1074003968 | bytes 11010048 | tf_op jit(solution)/shard_map/dot_general | solution.py:56
  285.6 0.2 pad_maximum_fusion
  285.8 6.3 %fusion.11 = f32[128,4096]{1,0:T(8,128)S(1)} fusion(f32[128,4096]{1,0:T(8,128)S(1)} %pad_maximum_fusion, f32[128,2048]{1,0:T(8,128)S(1)} %fusion.4, bf16[1,2048,2048]{2,1,0:T(8,128)(2,1)} %all-gather.15.cloned.1.call-done, bf16[128,4096]{1,0:T(8,128)(2,1)S(1)} %bitcast.48), kind=kOutput, calls=%fused_computation.10 | convolution fusion | flops 1074003968 | bytes 11010048 | tf_op jit(solution)/shard_map/dot_general | solution.py:20
  292.1 1.5 negate_bitcast_fusion
  293.6 2.1 fusion.22
  (3 shorter events, 0.0 us)
Async XLA Ops:
  7.2 43.2 %copy-start = (bf16[1,128,2048]{2,1,0:T(8,128)(2,1)S(1)}, bf16[1,128,2048]{2,1,0:T(8,128)(2,1)}, u32[]{:S(2)}) copy-start(bf16[1,128,2048]{2,1,0:T(8,128)(2,1)} %param.5) | copy-start | bytes 1572868
  7.2 47.1 %all-gather.11.cloned.1.call-start = ((), (), s32[]{:S(2)}) async-start(), calls=%async_computation.1 | async-start | bytes 2228224 | tf_op jit(solution)/shard_map/all_gather | solution.py:37
  7.9 122.3 %all-gather.15.cloned.1.call-start = ((), (), s32[]{:S(2)}) async-start(), calls=%async_computation.3 | async-start | bytes 8912896 | tf_op jit(solution)/shard_map/all_gather | solution.py:51
  8.7 196.9 %all-gather.13.cloned.1.call-start = ((), (), s32[]{:S(2)}) async-start(), calls=%async_computation.2 | async-start | bytes 8912896 | tf_op jit(solution)/shard_map/all_gather | solution.py:50
  9.4 271.4 %all-gather.9.cloned.1.call-start = ((), (), s32[]{:S(2)}) async-start(), calls=%async_computation | async-start | bytes 8912896 | tf_op jit(solution)/shard_map/all_gather | solution.py:52
  9.4 16.4 %collective-permute-start = (bf16[128,2048]{1,0:T(8,128)(2,1)}, bf16[128,2048]{1,0:T(8,128)(2,1)S(1)}, u32[]{:S(2)}, u32[]{:S(2)}) collective-permute-start(bf16[128,2048]{1,0:T(8,128)(2,1)} %bitcast.52), channel_id=1, source_target_pairs={{16,0},{17,1},{18,2},{19,3},{20,4},{21,5},{22,6},{23,7},{24,8},{25... | collective-permute-start | bytes 1572872 | tf_op jit(solution)/shard_map/ppermute | solution.py:12
  25.8 0.8 copy-start.1
Sparse Core Ops, SparseCore 0:
  10.2 44.0 all-gather.10
  56.4 73.7 all-gather.14
  132.4 73.1 all-gather.12
  207.6 73.1 all-gather.8
where the time goes:
time: 303 us; the launch traced here: 302 us
  waiting for transfers between devices  229 us (76%)
  matrix products  29.9 us (10%)
  blocking collectives  22.9 us (8%)
  between operations  13.9 us (5%)
  local copies, waits for them, and re-layouts  3.6 us (1%)
    all_gather x1, waiting for transfers between devices, shards(): piece_right = lax.all_gather(diag_right, 'rows', axis=0, tiled=True)  70.6 us
    all_gather x1, waiting for transfers between devices, shards(): piece_left = lax.all_gather(diag_left, 'rows', axis=0, tiled=True)  69.7 us
    all_gather x1, waiting for transfers between devices, shards(): piece_cross = lax.all_gather(cross, 'rows', axis=0, tiled=True)  69.1 us
    all_gather x1, blocking collectives, shards(): piece_pos = lax.all_gather(positions, 'rows', axis=0, tiled=True)  22.9 us
    ppermute x1, waiting for transfers between devices, from_behind(): return lax.ppermute(array, axis, pairs)  15.1 us
    dot_general x1, matrix products, contract_last(): lax.dot_general(left, right, (((1,), (1,)), ((), ())), preferred_element_...  6.27 us
  transfers between devices with their start and end apart: 5, of which 5 were waited for; matrix products, arithmetic and copies ran while one was open for 6% of the time, Pallas kernels for 0%

commit v1 on v0

v1 whole, which is shorter than its diff:
```python
import functools

import jax
import jax.numpy as jnp
from jax import lax
from jax.experimental import pallas as pl
from jax.experimental.pallas import tpu as pltpu
from jax.sharding import PartitionSpec as P

TILE = 128
PAD = 32
SIDES = 2
CORES = 2
QUAD = SIDES * CORES


def contract_last(left, right):
    return lax.dot_general(
        left, right, (((1,), (1,)), ((), ())), preferred_element_type=jnp.float32
    )


def place(z, y, c):
    return (z * SIDES + y) * CORES + c


def sent(array, line, move):
    pairs = []
    for z in range(line):
        for y in range(SIDES):
            for c in range(CORES):
                target = move(z, y, c)
                if target is not None:
                    pairs.append((place(z, y, c), place(*target)))
    return lax.ppermute(array, "rows", pairs)


def to_core(array, line):
    return sent(array, line, lambda z, y, c: (z, y, 1 - c))


def to_side(array, line):
    return sent(array, line, lambda z, y, c: (z, 1 - y, c))


def hop(array, line, by, low, high):
    def move(z, y, c):
        if low <= z <= high and 0 <= z + by < line:
            return (z + by, y, c)
        return None

    return sent(array, line, move)


def ring_gather(array, line):
    cycle = [(z, 0) for z in range(line)] + [(z, 1) for z in reversed(range(line))]
    where_at = {chip: i for i, chip in enumerate(cycle)}
    count = len(cycle)

    def turn(part, by):
        return sent(
            part, line, lambda z, y, c: (*cycle[(where_at[(z, y)] + by) % count], c)
        )

    pieces = [array]
    ahead = behind = array
    for _ in range(count // 2 - 1):
        ahead = turn(ahead, 1)
        behind = turn(behind, -1)
        pieces += [ahead, behind]
    half = array.shape[0] // 2
    pieces.append(jnp.concatenate([turn(ahead[:half], 1), turn(behind[half:], -1)], axis=0))
    return pieces


def factors_kernel(
    per_shard,
    shards_each,
    pos_ref,
    side_ref,
    near_ref,
    far_ref,
    wrows_ref,
    diag_ref,
    diag_other_ref,
    cross_ref,
    cross_other_ref,
    cols_ref,
    cols_other_ref,
    next_ref,
    next_other_ref,
    updated_ref,
    factor_ref,
    sep_ref,
    wtile_ref,
    sum_ref,
    fac_ref,
):
    rows = wrows_ref.shape[0]
    count = wrows_ref.shape[1] // TILE
    side = side_ref[0]
    mine = pl.ds(pl.multiple_of(side * rows, rows), rows)
    other = pl.ds(pl.multiple_of((1 - side) * rows, rows), rows)
    mine_low = pl.ds(pl.multiple_of((2 + side) * rows, rows), rows)
    other_low = pl.ds(pl.multiple_of((3 - side) * rows, rows), rows)
    for j in range(count):
        lanes = pl.ds(j * TILE, TILE)
        sep_ref[j, mine, :] = diag_ref[:, lanes]
        sep_ref[j, other, :] = diag_other_ref[:, lanes]
        sep_ref[j, mine_low, :] = cols_ref[:, lanes]
        sep_ref[j, other_low, :] = cols_other_ref[:, lanes]
        sep_ref[count + j, mine, :] = cross_ref[:, lanes]
        sep_ref[count + j, other, :] = cross_other_ref[:, lanes]
        sep_ref[count + j, mine_low, :] = next_ref[:, lanes]
        sep_ref[count + j, other_low, :] = next_other_ref[:, lanes]
        wtile_ref[j] = wrows_ref[:, lanes]
    sum_ref[...] = jnp.zeros_like(sum_ref)
    fac_ref[...] = jnp.zeros_like(fac_ref)

    def add(tile, k):
        i = pos_ref[2 * k]
        j = pos_ref[2 * k + 1]
        sum_ref[i] += contract_last(sep_ref[j], tile)
        fac_ref[j] += jnp.dot(wtile_ref[i], tile, preferred_element_type=jnp.float32)

    stride = per_shard * TILE + PAD

    @pl.loop(0, shards_each)
    def _(s):
        for half, ref in enumerate((near_ref, far_ref)):
            for t in range(per_shard):
                start = pl.multiple_of(s * stride + t * TILE, 16)
                add(ref[pl.ds(start, TILE), :], (half * shards_each + s) * per_shard + t)

    for i in range(count):
        updated_ref[:, i * TILE : (i + 1) * TILE] = sum_ref[i].astype(jnp.bfloat16)
    for j in range(2 * count):
        factor_ref[:, j * TILE : (j + 1) * TILE] = fac_ref[j].astype(jnp.bfloat16)


def factors(positions, side, near, far, wrows, seps, per_shard):
    rows, width = wrows.shape
    count = width // TILE
    shards_each = near.shape[0] // (per_shard * TILE + PAD)
    tiles = 2 * shards_each * per_shard
    whole = pl.BlockSpec(memory_space=pltpu.VMEM)
    scalar = pl.BlockSpec(memory_space=pltpu.SMEM)
    return pl.pallas_call(
        functools.partial(factors_kernel, per_shard, shards_each),
        out_shape=(
            jax.ShapeDtypeStruct((4 * rows, width), jnp.bfloat16),
            jax.ShapeDtypeStruct((rows, 2 * width), jnp.bfloat16),
        ),
        in_specs=[scalar, scalar] + [whole] * (3 + len(seps)),
        out_specs=(whole, whole),
        scratch_shapes=[
            pltpu.VMEM((2 * count, 4 * rows, TILE), jnp.bfloat16),
            pltpu.VMEM((count, rows, TILE), jnp.bfloat16),
            pltpu.VMEM((count, 4 * rows, TILE), jnp.float32),
            pltpu.VMEM((2 * count, rows, TILE), jnp.float32),
        ],
        compiler_params=pltpu.CompilerParams(vmem_limit_bytes=48 * 1024 * 1024),
        cost_estimate=pl.CostEstimate(
            flops=2 * tiles * TILE * TILE * rows * 5,
            bytes_accessed=2 * (13 * rows * width + tiles * TILE * TILE),
            transcendentals=0,
        ),
    )(positions, side, near, far, wrows, *seps)


def shards(line, inverse_block, coupling_tiles, tile_pos, sep_diag, sep_cross):
    wrows = inverse_block[0]
    rows, width = wrows.shape
    tiles = coupling_tiles[0]
    per_shard = tiles.shape[0]
    diag = sep_diag[0]
    cross = sep_cross[0]
    index = lax.axis_index("rows")
    z = index // QUAD
    y = index // CORES % SIDES
    c = index % CORES

    marks = tile_pos[0].astype(jnp.bfloat16).reshape(1, -1)
    marks = jnp.pad(marks, ((0, PAD - 1), (0, TILE - marks.shape[1])))
    packed = jnp.concatenate([tiles.reshape(-1, TILE), marks], axis=0)
    near = jnp.concatenate(ring_gather(packed, line), axis=0)
    far = to_core(near, line)

    cols = lax.all_to_all(cross.T, "rows", 0, 1, tiled=True)
    cols_other = to_side(cols, line)

    diag_other = to_side(diag, line)
    cross_other = to_side(cross, line)
    size = lax.axis_size("tm")
    back = [(i + 1, i) for i in range(size - 1)]
    following = lax.ppermute(diag, "tm", back)
    following_other = lax.ppermute(diag_other, "tm", back)

    def marked(part):
        rows_each = per_shard * TILE + PAD
        return part.reshape(-1, rows_each, TILE)[:, per_shard * TILE, : 2 * per_shard]

    positions = jnp.concatenate([marked(near), marked(far)], axis=0)
    positions = positions.astype(jnp.int32).reshape(-1)
    seps = (diag, diag_other, cross, cross_other, cols, cols_other, following, following_other)
    updated, factor = factors(
        positions, y.astype(jnp.int32).reshape(1), near, far, wrows, seps, per_shard
    )
    updated_far = to_core(updated, line)

    both = jnp.stack(
        [
            jnp.where(c == 0, updated, updated_far).reshape(2, SIDES, rows, width),
            jnp.where(c == 0, updated_far, updated).reshape(2, SIDES, rows, width),
        ],
        axis=2,
    ).reshape(2 * QUAD * rows, width)

    def block(part):
        return (-contract_last(part, both)).astype(jnp.bfloat16)

    results = {0: block(wrows)}
    up = down = wrows
    for s in range(1, line):
        if 2 * s < line:
            up = hop(up, line, 1, s - 1, line - 2)
            down = hop(down, line, -1, 1, line - s)
            results[s] = hop(block(up), line, -s, s, line - 1)
            results[-s] = hop(block(down), line, s, 0, line - 1 - s)
            continue
        if 2 * (s - 1) < line:
            up = hop(up, line, 1, s - 1, line - 2)
            down = hop(down, line, -1, 1, line - s)
            one = jnp.where(z >= s, up, down)
        else:
            last = s

            def outward(zz, yy, cc):
                if last - 1 <= zz < line - 1:
                    return (zz + 1, yy, cc)
                if 1 <= zz <= line - last:
                    return (zz - 1, yy, cc)
                return None

            one = sent(one, line, outward)
        span = s

        def home(zz, yy, cc):
            if zz >= span:
                return (zz - span, yy, cc)
            if zz + span < line:
                return (zz + span, yy, cc)
            return None

        results[s] = results[-s] = sent(block(one), line, home)

    quads = []
    for q in range(line):
        piece = results[0]
        for d in range(-q, line - q):
            if d:
                piece = jnp.where(z == q + d, results[-d], piece)
        quads.append(piece.reshape(rows, 2, QUAD * rows))
    rounded = jnp.stack(quads, axis=2).reshape(rows, 2 * width)
    sigma = rounded.astype(jnp.float32)

    if rows < TILE:
        whole = factor
        for bit in range((TILE // rows).bit_length() - 1):
            pairs = [(i, i ^ 1 << bit) for i in range(lax.axis_size("rows"))]
            partner = lax.ppermute(whole, "rows", pairs)
            whole = jnp.where(
                index >> bit & 1 == 0,
                jnp.concatenate([whole, partner], axis=0),
                jnp.concatenate([partner, whole], axis=0),
            )
        product = contract_last(rounded, whole)
        start = index * rows // TILE * TILE
        wtile = lax.dynamic_slice_in_dim(wrows, start, TILE, 1).astype(jnp.float32)
        result_tiles = wtile - product
    else:
        many = rows // TILE
        product = jnp.einsum(
            "mrk,mck->mrc",
            rounded.reshape(many, TILE, 2 * width),
            factor.reshape(many, TILE, 2 * width),
            preferred_element_type=jnp.float32,
        )
        square = lax.dynamic_slice_in_dim(wrows, index * rows, rows, 1).reshape(
            many, TILE, many, TILE
        )
        wtile = jnp.stack([square[i, :, i, :] for i in range(many)]).astype(jnp.float32)
        result_tiles = (wtile - product).reshape(rows, TILE)
    return (sigma[None], result_tiles[None])


def solution(mesh):
    placed = (
        P("tm", "rows", None),
        P("tm", "rows", None, None),
        P("tm", "rows", None),
        P("tm", "rows", None),
        P("tm", "rows", None),
    )
    return jax.shard_map(
        functools.partial(shards, mesh.shape["rows"] // QUAD),
        mesh=mesh,
        in_specs=placed,
        out_specs=(P("tm", "rows", None), P("tm", "rows", None)),
        check_vma=False,
    )
```

time: 303 us -> 170 us (0.56)
  waiting for transfers between devices: 229 us -> 81.9 us
  starting transfers between devices: 1.44 us -> 42.9 us
  blocking collectives: 22.9 us -> 0 us
  matrix products: 29.9 us -> 9.72 us
  local copies, waits for them, and re-layouts: 3.6 us -> 18.2 us
  between operations: 13.9 us -> 0.94 us
  Pallas kernels: 0 us -> 9.81 us
  other arithmetic: 1.68 us -> 5.74 us
    all_gather x4 -> x0, waiting for transfers between devices: 212 us -> none  [the longest x1 70.6 us: shards(): piece_right = lax.all_gather(diag_right, 'rows', axis=0, tiled=True)]
    ppermute x1 -> x24, waiting for transfers between devices: 15.1 us -> 81.9 us  [the longest x22 62.6 us: sent(): return lax.ppermute(array, 'rows', pairs)]
    ppermute x1 -> x24, starting transfers between devices: 1.29 us -> 37.8 us  [the longest x22 35.3 us: sent(): return lax.ppermute(array, 'rows', pairs)]
    all_gather x1 -> x0, blocking collectives: 22.9 us -> none  [shards(): piece_pos = lax.all_gather(positions, 'rows', axis=0, tiled=True)]
    dot_general x5 -> x0, matrix products: 21.5 us -> none  [the longest x1 5.61 us: shards(): jnp.dot(factor_left, piece_cross, preferred_element_type=jnp.float32)]
    pallas_call x0 -> x1, Pallas kernels: none -> 9.81 us  [factors(): pl.pallas_call(functools.partial(factors_kernel, per_shard, shards_each),...]
    unnamed x7 -> x23, local copies, waits for them, and re-layouts: 2.29 us -> 10.7 us
    all_to_all x0 -> x1, starting transfers between devices: none -> 5.03 us  [shards(): cols = lax.all_to_all(cross.T, 'rows', 0, 1, tiled=True)]
  transfers between devices with their start and end apart: 5 -> 25, of which waited for: 5 -> 13; matrix products, arithmetic and copies ran while one was open for 6% -> 12% of each run, Pallas kernels for 0% -> 0%
where the time goes in v1:
time: 170 us; the launch traced here: 169 us
  waiting for transfers between devices  81.9 us (48%)
  starting transfers between devices  42.9 us (25%)
  local copies, waits for them, and re-layouts  18.2 us (11%)
  Pallas kernels  9.81 us (6%)
  matrix products  9.72 us (6%)
  other arithmetic  5.74 us (3%)
    ppermute x22, waiting for transfers between devices, sent(): return lax.ppermute(array, 'rows', pairs)  62.6 us
    ppermute x22, starting transfers between devices, sent(): return lax.ppermute(array, 'rows', pairs)  35.3 us
    unnamed x23, local copies, waits for them, and re-layouts  10.7 us
    ppermute x1, waiting for transfers between devices, shards(): following_other = lax.ppermute(diag_other, 'tm', back)  10.1 us
    pallas_call x1, Pallas kernels, factors(): pl.pallas_call(functools.partial(factors_kernel, per_shard, shards_each),...  9.81 us
    ppermute x1, waiting for transfers between devices, shards(): following = lax.ppermute(diag, 'tm', back)  9.16 us
    dot_general x5, matrix products, contract_last(): lax.dot_general(left, right, (((1,), (1,)), ((), ())), preferred_element_...  8.62 us
    all_to_all x1, starting transfers between devices, shards(): cols = lax.all_to_all(cross.T, 'rows', 0, 1, tiled=True)  5.03 us
  transfers between devices with their start and end apart: 25, of which 13 were waited for; matrix products, arithmetic and copies ran while one was open for 12% of the time, Pallas kernels for 0%

profile of v1, /device:TPU:0, one launch (start us, length us, event | category | flops | bytes accessed | tf_op | source)
XLA Modules:
  0.0 169.2 jit_solution(4890823981365328609)
XLA Ops:
  0.6 1.6 constant_dynamic-update-slice_fusion.9
  3.7 0.9 pad_maximum_fusion.2
  4.6 3.1 %collective-permute-start.5 = (bf16[544,128]{1,0:T(8,128)(2,1)S(1)}, bf16[544,128]{1,0:T(8,128)(2,1)S(1)}, u32[]{:S(2)}, u32[]{:S(2)}) collective-permute-start(bf16[544,128]{1,0:T(8,128)(2,1)S(1)} %pad_maximum_fusion.2), channel_id=1, source_target_pairs={{0,4},{1,5},{2,0},{3,1},{4,8},{5,9},{6,2},{7,3},{8,12},{9,13},{10,... | collective-permute-start | bytes 417800 | tf_op jit(solution)/shard_map/ppermute | solution.py:35
  7.7 2.0 %collective-permute-start.14 = (bf16[128,2048]{1,0:T(8,128)(2,1)}, bf16[128,2048]{1,0:T(8,128)(2,1)S(1)}, u32[]{:S(2)}, u32[]{:S(2)}) collective-permute-start(bf16[128,2048]{1,0:T(8,128)(2,1)} %bitcast.64), channel_id=1, source_target_pairs={{0,2},{1,3},{2,0},{3,1},{4,6},{5,7},{6,4},{7,5},{8,10},{9,11},{10,... | collective-permute-start | bytes 1572872 | tf_op jit(solution)/shard_map/ppermute | solution.py:35
  9.6 2.1 %copy.47 = bf16[2048,128]{1,0:T(8,128)(2,1)} copy(bf16[2048,128]{0,1:T(8,128)(2,1)} %bitcast.58) | data formatting | bytes 1048576 | tf_op jit(solution)/shard_map/all_to_all | solution.py:189
  11.7 5.0 %all-to-all-start = ((bf16[16,128,128]{2,1,0:T(8,128)(2,1)}), bf16[16,128,128]{2,1,0:T(8,128)(2,1)}, u32[]{:S(2)}, u32[]{:S(2)}) async-start(bf16[16,128,128]{2,1,0:T(8,128)(2,1)} %bitcast.10), calls=%async_computation | async-start | bytes 1048576 | tf_op jit(solution)/shard_map/all_to_all | solution.py:189
  16.8 1.9 %collective-permute-start.7 = (bf16[544,128]{1,0:T(8,128)(2,1)S(1)}, bf16[544,128]{1,0:T(8,128)(2,1)S(1)}, u32[]{:S(2)}, u32[]{:S(2)}) collective-permute-start(bf16[544,128]{1,0:T(8,128)(2,1)S(1)} %collective-permute-done.5), channel_id=1, source_target_pairs={{0,4},{1,5},{2,0},{3,1},{4,8},{5,9},{6,2},{7,3},{8,12},{9,13},{10,... | collective-permute-start | bytes 417800 | tf_op jit(solution)/shard_map/ppermute | solution.py:35
  20.2 10.1 %collective-permute-done.7 = bf16[544,128]{1,0:T(8,128)(2,1)S(1)} collective-permute-done((bf16[544,128]{1,0:T(8,128)(2,1)S(1)}, bf16[544,128]{1,0:T(8,128)(2,1)S(1)}, u32[]{:S(2)}, u32[]{:S(2)}) %collective-permute-start.7) | collective-permute-done | bytes 139296 | tf_op jit(solution)/shard_map/ppermute | solution.py:35
  30.3 3.4 %collective-permute-start.9 = (bf16[544,128]{1,0:T(8,128)(2,1)S(1)}, bf16[544,128]{1,0:T(8,128)(2,1)S(1)}, u32[]{:S(2)}, u32[]{:S(2)}) collective-permute-start(bf16[544,128]{1,0:T(8,128)(2,1)S(1)} %collective-permute-done.7), channel_id=1, source_target_pairs={{0,4},{1,5},{2,0},{3,1},{4,8},{5,9},{6,2},{7,3},{8,12},{9,13},{10,... | collective-permute-start | bytes 417800 | tf_op jit(solution)/shard_map/ppermute | solution.py:35
  35.0 1.4 collective-permute-done.9
  36.4 2.5 %collective-permute-start.11 = (bf16[272,128]{1,0:T(8,128)(2,1)S(1)}, bf16[272,128]{1,0:T(8,128)(2,1)S(1)}, u32[]{:S(2)}, u32[]{:S(2)}) collective-permute-start(bf16[272,128]{1,0:T(8,128)(2,1)S(1)} %slice.16), channel_id=1, source_target_pairs={{0,4},{1,5},{2,0},{3,1},{4,8},{5,9},{6,2},{7,3},{8,12},{9,13},{10,... | collective-permute-start | bytes 208904 | tf_op jit(solution)/shard_map/ppermute | solution.py:35
  39.4 1.2 collective-permute-start.12
  41.9 0.9 collective-permute-done.11
  44.4 1.3 collective-permute-start.17
  45.7 1.8 %collective-permute-start.15 = (bf16[128,2048]{1,0:T(8,128)(2,1)S(1)}, bf16[128,2048]{1,0:T(8,128)(2,1)}, u32[]{:S(2)}, u32[]{:S(2)}) collective-permute-start(bf16[128,2048]{1,0:T(8,128)(2,1)S(1)} %bitcast.59), channel_id=1, source_target_pairs={{0,2},{1,3},{2,0},{3,1},{4,6},{5,7},{6,4},{7,5},{8,10},{9,11},{10,... | collective-permute-start | bytes 1572872 | tf_op jit(solution)/shard_map/ppermute | solution.py:35
  47.4 1.3 collective-permute-start.18
  48.7 1.1 copy_bitcast_fusion.cols_ref
  51.0 0.7 slice.19
  51.8 9.2 %collective-permute-done.17.next_ref = bf16[128,2048]{1,0:T(8,128)(2,1)S(1)} collective-permute-done((bf16[128,2048]{1,0:T(8,128)(2,1)S(1)}, bf16[128,2048]{1,0:T(8,128)(2,1)S(1)}, u32[]{:S(2)}, u32[]{:S(2)}) %collective-permute-start.17) | collective-permute-done | bytes 524320 | tf_op jit(solution)/shard_map/ppermute | solution.py:196
  61.0 0.8 copy-done.5
  61.8 10.1 %collective-permute-done.18.next_other_ref = bf16[128,2048]{1,0:T(8,128)(2,1)} collective-permute-done((bf16[128,2048]{1,0:T(8,128)(2,1)S(1)}, bf16[128,2048]{1,0:T(8,128)(2,1)}, u32[]{:S(2)}, u32[]{:S(2)}) %collective-permute-start.18) | collective-permute-done | bytes 524320 | tf_op jit(solution)/shard_map/ppermute | solution.py:197
  71.9 1.0 copy-done.4
  73.0 1.0 copy-done.6
  74.0 9.8 %shard_map.68 = (bf16[512,2048]{1,0:T(8,128)(2,1)}, bf16[128,4096]{1,0:T(8,128)(2,1)S(1)}) custom-call(s32[128]{0:T(128)S(1)} %reshape.68.pos_ref, s32[1]{0:T(128)} %bitcast.6.side_ref, bf16[4352,128]{1,0:T(8,128)(2,1)} %constant_dynamic-update-slice_fusion.near_ref, bf16[4352,128]{1,0:T(8,128)(2,1)} %collective-permute-done.13.far_ref, ...), custom_call_target="tpu_custom_call" | custom-call | flops 1342177280 | bytes 8912896 | tf_op jit(solution)/shard_map/pallas_call | solution.py:148
  83.8 4.0 %collective-permute-start = (bf16[128,2048]{1,0:T(8,128)(2,1)S(1)}, bf16[128,2048]{1,0:T(8,128)(2,1)S(1)}, u32[]{:S(2)}, u32[]{:S(2)}) collective-permute-start(bf16[128,2048]{1,0:T(8,128)(2,1)S(1)} %bitcast.62), channel_id=1, source_target_pairs={{0,4},{1,5},{2,6},{3,7},{4,8},{5,9},{6,10},{7,11},{8,12},{9,13},{1... | collective-permute-start | bytes 1572872 | tf_op jit(solution)/shard_map/ppermute | solution.py:35
  87.8 1.3 collective-permute-start.2
  89.1 10.5 %collective-permute-done = bf16[128,2048]{1,0:T(8,128)(2,1)S(1)} collective-permute-done((bf16[128,2048]{1,0:T(8,128)(2,1)S(1)}, bf16[128,2048]{1,0:T(8,128)(2,1)S(1)}, u32[]{:S(2)}, u32[]{:S(2)}) %collective-permute-start) | collective-permute-done | bytes 524320 | tf_op jit(solution)/shard_map/ppermute | solution.py:35
  100.3 3.6 %collective-permute-done.2 = bf16[128,2048]{1,0:T(8,128)(2,1)} collective-permute-done((bf16[128,2048]{1,0:T(8,128)(2,1)S(1)}, bf16[128,2048]{1,0:T(8,128)(2,1)}, u32[]{:S(2)}, u32[]{:S(2)}) %collective-permute-start.2) | collective-permute-done | bytes 524320 | tf_op jit(solution)/shard_map/ppermute | solution.py:35
  103.9 1.3 collective-permute-start.3
  105.2 14.0 %collective-permute-done.3 = bf16[128,2048]{1,0:T(8,128)(2,1)S(1)} collective-permute-done((bf16[128,2048]{1,0:T(8,128)(2,1)}, bf16[128,2048]{1,0:T(8,128)(2,1)S(1)}, u32[]{:S(2)}, u32[]{:S(2)}) %collective-permute-start.3) | collective-permute-done | bytes 524320 | tf_op jit(solution)/shard_map/ppermute | solution.py:35
  119.2 1.3 collective-permute-start.4
  120.5 2.5 %broadcast_select_fusion.1 = (bf16[512,2048]{1,0:T(8,128)(2,1)S(1)}, bf16[512,2048]{1,0:T(8,128)(2,1)S(1)}) fusion(bf16[512,2048]{1,0:T(8,128)(2,1)} %get-tuple-element.4, bf16[512,2048]{1,0:T(8,128)(2,1)} %collective-permute-done.19, pred[]{:T(512)S(6)} %eq.14), kind=kLoop, calls=%fused_computation.2 | loop fusion | flops 2097152 | bytes 8388609 | tf_op jit(solution)/shard_map/jit(_where)/select_n | solution.py:213
  123.4 1.5 fusion.1
  125.0 8.5 %collective-permute-done.4 = bf16[128,2048]{1,0:T(8,128)(2,1)S(1)} collective-permute-done((bf16[128,2048]{1,0:T(8,128)(2,1)S(1)}, bf16[128,2048]{1,0:T(8,128)(2,1)S(1)}, u32[]{:S(2)}, u32[]{:S(2)}) %collective-permute-start.4) | collective-permute-done | bytes 524320 | tf_op jit(solution)/shard_map/ppermute | solution.py:35
  133.4 1.5 fusion
  135.0 1.9 %collective-permute-start.20 = (bf16[128,1024]{1,0:T(8,128)(2,1)S(1)}, bf16[128,1024]{1,0:T(8,128)(2,1)S(1)}, u32[]{:S(2)}, u32[]{:S(2)}) collective-permute-start(bf16[128,1024]{1,0:T(8,128)(2,1)S(1)} %fusion), channel_id=1, source_target_pairs={{0,12},{1,13},{2,14},{3,15},{12,0},{13,1},{14,2},{15,3},{16,28},{1... | collective-permute-start | bytes 786440 | tf_op jit(solution)/shard_map/ppermute | solution.py:35
  136.9 2.6 %fusion.7 = bf16[128,1024]{1,0:T(8,128)(2,1)S(1)} fusion(bf16[1024,2048]{1,0:T(8,128)(2,1)S(1)} %bitcast.69, bf16[128,2048]{1,0:T(8,128)(2,1)} %collective-permute-done.2), kind=kOutput, calls=%fused_computation.15 | convolution fusion | flops 537133056 | bytes 4980736 | tf_op jit(solution)/shard_map/dot_general | solution.py:18
  139.5 1.3 collective-permute-start.22
  140.8 1.5 fusion.5
  142.3 1.5 collective-permute-start.23
  143.8 5.7 %collective-permute-start.21 = (bf16[128,1024]{1,0:T(8,128)(2,1)S(1)}, bf16[128,1024]{1,0:T(8,128)(2,1)S(1)}, u32[]{:S(2)}, u32[]{:S(2)}) collective-permute-start(bf16[128,1024]{1,0:T(8,128)(2,1)S(1)} %fusion.1), channel_id=1, source_target_pairs={{0,8},{1,9},{2,10},{3,11},{4,12},{5,13},{6,14},{7,15},{8,0},{9,1},... | collective-permute-start | bytes 786440 | tf_op jit(solution)/shard_map/ppermute | solution.py:35
  149.5 1.5 fusion.6
  151.0 0.7 collective-permute-done.23
  151.7 12.2 %collective-permute-done.21 = bf16[128,1024]{1,0:T(8,128)(2,1)S(1)} collective-permute-done((bf16[128,1024]{1,0:T(8,128)(2,1)S(1)}, bf16[128,1024]{1,0:T(8,128)(2,1)S(1)}, u32[]{:S(2)}, u32[]{:S(2)}) %collective-permute-start.21) | collective-permute-done | bytes 262176 | tf_op jit(solution)/shard_map/ppermute | solution.py:35
  164.6 0.8 copy.51
  165.4 1.1 pad_maximum_fusion.1
  166.5 1.6 copy.43
  168.1 1.1 fusion.8
  (56 shorter events, 10.7 us)
Async XLA Ops:
  4.6 12.2 %collective-permute-start.5 = (bf16[544,128]{1,0:T(8,128)(2,1)S(1)}, bf16[544,128]{1,0:T(8,128)(2,1)S(1)}, u32[]{:S(2)}, u32[]{:S(2)}) collective-permute-start(bf16[544,128]{1,0:T(8,128)(2,1)S(1)} %pad_maximum_fusion.2), channel_id=1, source_target_pairs={{0,4},{1,5},{2,0},{3,1},{4,8},{5,9},{6,2},{7,3},{8,12},{9,13},{10,... | collective-permute-start | bytes 417800 | tf_op jit(solution)/shard_map/ppermute | solution.py:35
  7.7 11.0 %collective-permute-start.6 = (bf16[544,128]{1,0:T(8,128)(2,1)S(1)}, bf16[544,128]{1,0:T(8,128)(2,1)S(1)}, u32[]{:S(2)}, u32[]{:S(2)}) collective-permute-start(bf16[544,128]{1,0:T(8,128)(2,1)S(1)} %pad_maximum_fusion.2), channel_id=1, source_target_pairs={{0,2},{1,3},{2,6},{3,7},{4,0},{5,1},{6,10},{7,11},{8,4},{9,5},{10,... | collective-permute-start | bytes 417800 | tf_op jit(solution)/shard_map/ppermute | solution.py:35
  7.7 39.7 %collective-permute-start.14 = (bf16[128,2048]{1,0:T(8,128)(2,1)}, bf16[128,2048]{1,0:T(8,128)(2,1)S(1)}, u32[]{:S(2)}, u32[]{:S(2)}) collective-permute-start(bf16[128,2048]{1,0:T(8,128)(2,1)} %bitcast.64), channel_id=1, source_target_pairs={{0,2},{1,3},{2,0},{3,1},{4,6},{5,7},{6,4},{7,5},{8,10},{9,11},{10,... | collective-permute-start | bytes 1572872 | tf_op jit(solution)/shard_map/ppermute | solution.py:35
  11.7 37.0 %all-to-all-start = ((bf16[16,128,128]{2,1,0:T(8,128)(2,1)}), bf16[16,128,128]{2,1,0:T(8,128)(2,1)}, u32[]{:S(2)}, u32[]{:S(2)}) async-start(bf16[16,128,128]{2,1,0:T(8,128)(2,1)} %bitcast.10), calls=%async_computation | async-start | bytes 1048576 | tf_op jit(solution)/shard_map/all_to_all | solution.py:189
  16.8 13.5 %collective-permute-start.7 = (bf16[544,128]{1,0:T(8,128)(2,1)S(1)}, bf16[544,128]{1,0:T(8,128)(2,1)S(1)}, u32[]{:S(2)}, u32[]{:S(2)}) collective-permute-start(bf16[544,128]{1,0:T(8,128)(2,1)S(1)} %collective-permute-done.5), channel_id=1, source_target_pairs={{0,4},{1,5},{2,0},{3,1},{4,8},{5,9},{6,2},{7,3},{8,12},{9,13},{10,... | collective-permute-start | bytes 417800 | tf_op jit(solution)/shard_map/ppermute | solution.py:35
  18.7 15.0 %collective-permute-start.8 = (bf16[544,128]{1,0:T(8,128)(2,1)S(1)}, bf16[544,128]{1,0:T(8,128)(2,1)S(1)}, u32[]{:S(2)}, u32[]{:S(2)}) collective-permute-start(bf16[544,128]{1,0:T(8,128)(2,1)S(1)} %collective-permute-done.6), channel_id=1, source_target_pairs={{0,2},{1,3},{2,6},{3,7},{4,0},{5,1},{6,10},{7,11},{8,4},{9,5},{10,... | collective-permute-start | bytes 417800 | tf_op jit(solution)/shard_map/ppermute | solution.py:35
  18.8 25.5 %copy-start.2 = (bf16[1,128,2048]{2,1,0:T(8,128)(2,1)S(1)}, bf16[1,128,2048]{2,1,0:T(8,128)(2,1)}, u32[]{:S(2)}) copy-start(bf16[1,128,2048]{2,1,0:T(8,128)(2,1)} %param.8) | copy-start | bytes 1572868
  18.8 26.8 %copy-start = (bf16[1,128,2048]{2,1,0:T(8,128)(2,1)S(1)}, bf16[1,128,2048]{2,1,0:T(8,128)(2,1)}, u32[]{:S(2)}) copy-start(bf16[1,128,2048]{2,1,0:T(8,128)(2,1)} %param.9) | copy-start | bytes 1572868
  30.3 6.1 %collective-permute-start.9 = (bf16[544,128]{1,0:T(8,128)(2,1)S(1)}, bf16[544,128]{1,0:T(8,128)(2,1)S(1)}, u32[]{:S(2)}, u32[]{:S(2)}) collective-permute-start(bf16[544,128]{1,0:T(8,128)(2,1)S(1)} %collective-permute-done.7), channel_id=1, source_target_pairs={{0,4},{1,5},{2,0},{3,1},{4,8},{5,9},{6,2},{7,3},{8,12},{9,13},{10,... | collective-permute-start | bytes 417800 | tf_op jit(solution)/shard_map/ppermute | solution.py:35
  33.7 5.7 %collective-permute-start.10 = (bf16[544,128]{1,0:T(8,128)(2,1)S(1)}, bf16[544,128]{1,0:T(8,128)(2,1)S(1)}, u32[]{:S(2)}, u32[]{:S(2)}) collective-permute-start(bf16[544,128]{1,0:T(8,128)(2,1)S(1)} %collective-permute-done.8), channel_id=1, source_target_pairs={{0,2},{1,3},{2,6},{3,7},{4,0},{5,1},{6,10},{7,11},{8,4},{9,5},{10,... | collective-permute-start | bytes 417800 | tf_op jit(solution)/shard_map/ppermute | solution.py:35
  35.0 36.9 %copy-start.1 = (bf16[1,128,2048]{2,1,0:T(8,128)(2,1)S(1)}, bf16[1,128,2048]{2,1,0:T(8,128)(2,1)}, u32[]{:S(2)}) copy-start(bf16[1,128,2048]{2,1,0:T(8,128)(2,1)} %param.5) | copy-start | bytes 1572868
  36.4 6.4 %collective-permute-start.11 = (bf16[272,128]{1,0:T(8,128)(2,1)S(1)}, bf16[272,128]{1,0:T(8,128)(2,1)S(1)}, u32[]{:S(2)}, u32[]{:S(2)}) collective-permute-start(bf16[272,128]{1,0:T(8,128)(2,1)S(1)} %slice.16), channel_id=1, source_target_pairs={{0,4},{1,5},{2,0},{3,1},{4,8},{5,9},{6,2},{7,3},{8,12},{9,13},{10,... | collective-permute-start | bytes 208904 | tf_op jit(solution)/shard_map/ppermute | solution.py:35
  39.4 4.4 %collective-permute-start.12 = (bf16[272,128]{1,0:T(8,128)(2,1)S(1)}, bf16[272,128]{1,0:T(8,128)(2,1)S(1)}, u32[]{:S(2)}, u32[]{:S(2)}) collective-permute-start(bf16[272,128]{1,0:T(8,128)(2,1)S(1)} %slice.17), channel_id=1, source_target_pairs={{0,2},{1,3},{2,6},{3,7},{4,0},{5,1},{6,10},{7,11},{8,4},{9,5},{10,... | collective-permute-start | bytes 208904 | tf_op jit(solution)/shard_map/ppermute | solution.py:35
  44.4 6.6 %collective-permute-start.13 = (bf16[4352,128]{1,0:T(8,128)(2,1)}, bf16[4352,128]{1,0:T(8,128)(2,1)}, u32[]{:S(2)}, u32[]{:S(2)}) collective-permute-start(bf16[4352,128]{1,0:T(8,128)(2,1)} %constant_dynamic-update-slice_fusion.near_ref), channel_id=1, source_target_pairs={{0,1},{1,0},{2,3},{3,2},{4,5},{5,4},{6,7},{7,6},{8,9},{9,8},{10,11... | collective-permute-start | bytes 3342344 | tf_op jit(solution)/shard_map/ppermute | solution.py:35
  44.4 16.6 %collective-permute-start.17 = (bf16[128,2048]{1,0:T(8,128)(2,1)S(1)}, bf16[128,2048]{1,0:T(8,128)(2,1)S(1)}, u32[]{:S(2)}, u32[]{:S(2)}) collective-permute-start(bf16[128,2048]{1,0:T(8,128)(2,1)S(1)} %bitcast.65), channel_id=1, source_target_pairs={{16,0},{17,1},{18,2},{19,3},{20,4},{21,5},{22,6},{23,7},{24,8},{25... | collective-permute-start | bytes 1572872 | tf_op jit(solution)/shard_map/ppermute | solution.py:196
  45.7 16.1 %collective-permute-start.15 = (bf16[128,2048]{1,0:T(8,128)(2,1)S(1)}, bf16[128,2048]{1,0:T(8,128)(2,1)}, u32[]{:S(2)}, u32[]{:S(2)}) collective-permute-start(bf16[128,2048]{1,0:T(8,128)(2,1)S(1)} %bitcast.59), channel_id=1, source_target_pairs={{0,2},{1,3},{2,0},{3,1},{4,6},{5,7},{6,4},{7,5},{8,10},{9,11},{10,... | collective-permute-start | bytes 1572872 | tf_op jit(solution)/shard_map/ppermute | solution.py:35
  47.4 24.5 %copy-start.3 = (bf16[128,2048]{1,0:T(8,128)(2,1)}, bf16[128,2048]{1,0:T(8,128)(2,1)S(1)}, u32[]{:S(2)}) copy-start(bf16[128,2048]{1,0:T(8,128)(2,1)S(1)} %collective-permute-done.14.diag_other_ref) | copy-start | bytes 1572868
  47.4 24.5 %collective-permute-start.18 = (bf16[128,2048]{1,0:T(8,128)(2,1)S(1)}, bf16[128,2048]{1,0:T(8,128)(2,1)}, u32[]{:S(2)}, u32[]{:S(2)}) collective-permute-start(bf16[128,2048]{1,0:T(8,128)(2,1)S(1)} %collective-permute-done.14.diag_other_ref), channel_id=1, source_target_pairs={{16,0},{17,1},{18,2},{19,3},{20,4},{21,5},{22,6},{23,7},{24,8},{25... | collective-permute-start | bytes 1572872 | tf_op jit(solution)/shard_map/ppermute | solution.py:197
  49.8 22.1 %collective-permute-start.16 = (bf16[128,2048]{1,0:T(8,128)(2,1)S(1)}, bf16[128,2048]{1,0:T(8,128)(2,1)}, u32[]{:S(2)}, u32[]{:S(2)}) collective-permute-start(bf16[128,2048]{1,0:T(8,128)(2,1)S(1)} %copy_bitcast_fusion.cols_ref), channel_id=1, source_target_pairs={{0,2},{1,3},{2,0},{3,1},{4,6},{5,7},{6,4},{7,5},{8,10},{9,11},{10,... | collective-permute-start | bytes 1572872 | tf_op jit(solution)/shard_map/ppermute | solution.py:35
  61.0 0.8 copy-start.5
  71.9 1.0 copy-start.4
  73.0 1.0 copy-start.6
  83.8 36.7 %collective-permute-start.19 = (bf16[512,2048]{1,0:T(8,128)(2,1)}, bf16[512,2048]{1,0:T(8,128)(2,1)}, u32[]{:S(2)}, u32[]{:S(2)}) collective-permute-start(bf16[512,2048]{1,0:T(8,128)(2,1)} %get-tuple-element.4), channel_id=1, source_target_pairs={{0,1},{1,0},{2,3},{3,2},{4,5},{5,4},{6,7},{7,6},{8,9},{9,8},{10,11... | collective-permute-start | bytes 6291464 | tf_op jit(solution)/shard_map/ppermute | solution.py:35
  83.8 15.8 %collective-permute-start = (bf16[128,2048]{1,0:T(8,128)(2,1)S(1)}, bf16[128,2048]{1,0:T(8,128)(2,1)S(1)}, u32[]{:S(2)}, u32[]{:S(2)}) collective-permute-start(bf16[128,2048]{1,0:T(8,128)(2,1)S(1)} %bitcast.62), channel_id=1, source_target_pairs={{0,4},{1,5},{2,6},{3,7},{4,8},{5,9},{6,10},{7,11},{8,12},{9,13},{1... | collective-permute-start | bytes 1572872 | tf_op jit(solution)/shard_map/ppermute | solution.py:35
  87.8 16.1 %collective-permute-start.2 = (bf16[128,2048]{1,0:T(8,128)(2,1)S(1)}, bf16[128,2048]{1,0:T(8,128)(2,1)}, u32[]{:S(2)}, u32[]{:S(2)}) collective-permute-start(bf16[128,2048]{1,0:T(8,128)(2,1)S(1)} %bitcast.63), channel_id=1, source_target_pairs={{4,0},{5,1},{6,2},{7,3},{8,4},{9,5},{10,6},{11,7},{12,8},{13,9},{1... | collective-permute-start | bytes 1572872 | tf_op jit(solution)/shard_map/ppermute | solution.py:35
  99.6 5.6 %collective-permute-start.1 = (bf16[128,2048]{1,0:T(8,128)(2,1)S(1)}, bf16[128,2048]{1,0:T(8,128)(2,1)S(1)}, u32[]{:S(2)}, u32[]{:S(2)}) collective-permute-start(bf16[128,2048]{1,0:T(8,128)(2,1)S(1)} %collective-permute-done), channel_id=1, source_target_pairs={{4,8},{5,9},{6,10},{7,11},{8,12},{9,13},{10,14},{11,15},{20,24},{2... | collective-permute-start | bytes 1572872 | tf_op jit(solution)/shard_map/ppermute | solution.py:35
  103.9 15.3 %collective-permute-start.3 = (bf16[128,2048]{1,0:T(8,128)(2,1)}, bf16[128,2048]{1,0:T(8,128)(2,1)S(1)}, u32[]{:S(2)}, u32[]{:S(2)}) collective-permute-start(bf16[128,2048]{1,0:T(8,128)(2,1)} %collective-permute-done.2), channel_id=1, source_target_pairs={{4,0},{5,1},{6,2},{7,3},{8,4},{9,5},{10,6},{11,7},{20,16},{21,17},... | collective-permute-start | bytes 1572872 | tf_op jit(solution)/shard_map/ppermute | solution.py:35
  119.2 14.2 %collective-permute-start.4 = (bf16[128,2048]{1,0:T(8,128)(2,1)S(1)}, bf16[128,2048]{1,0:T(8,128)(2,1)S(1)}, u32[]{:S(2)}, u32[]{:S(2)}) collective-permute-start(bf16[128,2048]{1,0:T(8,128)(2,1)S(1)} %broadcast_select_fusion.2), channel_id=1, source_target_pairs={{4,0},{5,1},{6,2},{7,3},{8,12},{9,13},{10,14},{11,15},{20,16},{21,... | collective-permute-start | bytes 1572872 | tf_op jit(solution)/shard_map/ppermute | solution.py:35
  135.0 16.0 %collective-permute-start.20 = (bf16[128,1024]{1,0:T(8,128)(2,1)S(1)}, bf16[128,1024]{1,0:T(8,128)(2,1)S(1)}, u32[]{:S(2)}, u32[]{:S(2)}) collective-permute-start(bf16[128,1024]{1,0:T(8,128)(2,1)S(1)} %fusion), channel_id=1, source_target_pairs={{0,12},{1,13},{2,14},{3,15},{12,0},{13,1},{14,2},{15,3},{16,28},{1... | collective-permute-start | bytes 786440 | tf_op jit(solution)/shard_map/ppermute | solution.py:35
  139.5 11.5 %collective-permute-start.22 = (bf16[128,1024]{1,0:T(8,128)(2,1)S(1)}, bf16[128,1024]{1,0:T(8,128)(2,1)S(1)}, u32[]{:S(2)}, u32[]{:S(2)}) collective-permute-start(bf16[128,1024]{1,0:T(8,128)(2,1)S(1)} %fusion.7), channel_id=1, source_target_pairs={{0,4},{1,5},{2,6},{3,7},{4,8},{5,9},{6,10},{7,11},{8,12},{9,13},{1... | collective-permute-start | bytes 786440 | tf_op jit(solution)/shard_map/ppermute | solution.py:35
  142.3 9.4 %collective-permute-start.23 = (bf16[128,1024]{1,0:T(8,128)(2,1)S(1)}, bf16[128,1024]{1,0:T(8,128)(2,1)S(1)}, u32[]{:S(2)}, u32[]{:S(2)}) collective-permute-start(bf16[128,1024]{1,0:T(8,128)(2,1)S(1)} %fusion.5), channel_id=1, source_target_pairs={{4,0},{5,1},{6,2},{7,3},{8,4},{9,5},{10,6},{11,7},{12,8},{13,9},{1... | collective-permute-start | bytes 786440 | tf_op jit(solution)/shard_map/ppermute | solution.py:35
  143.8 20.1 %collective-permute-start.21 = (bf16[128,1024]{1,0:T(8,128)(2,1)S(1)}, bf16[128,1024]{1,0:T(8,128)(2,1)S(1)}, u32[]{:S(2)}, u32[]{:S(2)}) collective-permute-start(bf16[128,1024]{1,0:T(8,128)(2,1)S(1)} %fusion.1), channel_id=1, source_target_pairs={{0,8},{1,9},{2,10},{3,11},{4,12},{5,13},{6,14},{7,15},{8,0},{9,1},... | collective-permute-start | bytes 786440 | tf_op jit(solution)/shard_map/ppermute | solution.py:35

commit v2 on v0

v2 whole, which is shorter than its diff:
```python
import functools

import jax
import jax.numpy as jnp
from jax import lax
from jax.experimental import pallas as pl
from jax.experimental.pallas import tpu as pltpu
from jax.sharding import PartitionSpec as P

TILE = 128
PAD = 32
SIDES = 2
CORES = 2

WHOLE = pl.BlockSpec(memory_space=pltpu.VMEM)
SCALAR = pl.BlockSpec(memory_space=pltpu.SMEM)


def contract_last(left, right):
    return lax.dot_general(
        left, right, (((1,), (1,)), ((), ())), preferred_element_type=jnp.float32
    )


class Ring:
    def __init__(self, devices):
        self.line = devices // (SIDES * CORES)
        self.count = self.line * SIDES
        ups = [(z, 0) for z in range(self.line)]
        downs = [(z, 1) for z in reversed(range(self.line))]
        self.chips = [z * SIDES + y for z, y in ups + downs]
        self.spots = [self.chips.index(chip) for chip in range(self.count)]

    def turn(self, part, by):
        pairs = []
        for at, chip in enumerate(self.chips):
            target = self.chips[(at + by) % self.count]
            pairs += [(chip * CORES + c, target * CORES + c) for c in range(CORES)]
        return lax.ppermute(part, "rows", pairs)

    def to_core(self, part):
        devices = self.count * CORES
        return lax.ppermute(part, "rows", [(i, i ^ 1) for i in range(devices)])

    def opposite(self, ahead, behind):
        half = ahead.shape[0] // 2
        first = self.turn(ahead[:half], 1)
        return jnp.concatenate([first, self.turn(behind[half:], -1)], axis=0)


def pack_kernel(pos_ref, tiles_ref, cross_ref, packed_ref, flipped_ref):
    count = tiles_ref.shape[0]
    packed_ref[: count * TILE, :] = tiles_ref[...].reshape(count * TILE, TILE)
    lane = lax.broadcasted_iota(jnp.int32, (PAD, TILE), 1)
    marks = jnp.zeros((PAD, TILE), jnp.int32)
    for k in range(2 * count):
        marks = jnp.where(lane == k, pos_ref[k // 2, k % 2], marks)
    packed_ref[count * TILE :, :] = marks.astype(jnp.float32).astype(jnp.bfloat16)
    flipped_ref[...] = cross_ref[...].T


def pack(tiles, positions, cross):
    rows, width = cross.shape
    return pl.pallas_call(
        pack_kernel,
        out_shape=(
            jax.ShapeDtypeStruct((tiles.shape[0] * TILE + PAD, TILE), jnp.bfloat16),
            jax.ShapeDtypeStruct((width, rows), jnp.bfloat16),
        ),
        in_specs=[SCALAR, WHOLE, WHOLE],
        out_specs=(WHOLE, WHOLE),
        compiler_params=pltpu.CompilerParams(vmem_limit_bytes=16 * 1024 * 1024),
        cost_estimate=pl.CostEstimate(flops=0, bytes_accessed=rows, transcendentals=0),
    )(positions, tiles, cross)


def factors_kernel(
    per_shard,
    shards_each,
    near_ref,
    far_ref,
    wrows_ref,
    diag_ref,
    cross_ref,
    cols_ref,
    next_ref,
    updated_ref,
    factor_ref,
    sep_ref,
    wtile_ref,
    sum_ref,
    fac_ref,
    marks_ref,
    pos_ref,
    pos_sem,
):
    rows = wrows_ref.shape[0]
    count = wrows_ref.shape[1] // TILE
    stride = per_shard * TILE + PAD
    for half, ref in enumerate((near_ref, far_ref)):
        for s in range(shards_each):
            row = ref[s * stride + per_shard * TILE : (s + 1) * stride, :]
            marks_ref[half * shards_each + s] = row.astype(jnp.float32).astype(jnp.int32)[:8]
    fetch = pltpu.make_async_copy(marks_ref, pos_ref, pos_sem)
    fetch.start()
    for j in range(count):
        lanes = slice(j * TILE, (j + 1) * TILE)
        sep_ref[j, :rows, :] = diag_ref[:, lanes]
        sep_ref[j, rows:, :] = cols_ref[:, lanes]
        sep_ref[count + j, :rows, :] = cross_ref[:, lanes]
        sep_ref[count + j, rows:, :] = next_ref[:, lanes]
        wtile_ref[j] = wrows_ref[:, lanes]
    sum_ref[...] = jnp.zeros_like(sum_ref)
    fac_ref[...] = jnp.zeros_like(fac_ref)
    fetch.wait()

    def add(tile, shard, t):
        i = pos_ref[shard, 0, 2 * t]
        j = pos_ref[shard, 0, 2 * t + 1]
        sum_ref[i] += contract_last(sep_ref[j], tile)
        fac_ref[j] += jnp.dot(wtile_ref[i], tile, preferred_element_type=jnp.float32)

    @pl.loop(0, shards_each)
    def _(s):
        for half, ref in enumerate((near_ref, far_ref)):
            for t in range(per_shard):
                start = pl.multiple_of(s * stride + t * TILE, 16)
                add(ref[pl.ds(start, TILE), :], half * shards_each + s, t)

    for i in range(count):
        updated_ref[:, i * TILE : (i + 1) * TILE] = sum_ref[i].astype(jnp.bfloat16)
    for j in range(2 * count):
        factor_ref[:, j * TILE : (j + 1) * TILE] = fac_ref[j].astype(jnp.bfloat16)


def factors(near, far, wrows, seps, per_shard):
    rows, width = wrows.shape
    count = width // TILE
    shards_each = near.shape[0] // (per_shard * TILE + PAD)
    return pl.pallas_call(
        functools.partial(factors_kernel, per_shard, shards_each),
        out_shape=(
            jax.ShapeDtypeStruct((2 * rows, width), jnp.bfloat16),
            jax.ShapeDtypeStruct((rows, 2 * width), jnp.bfloat16),
        ),
        in_specs=[WHOLE] * (3 + len(seps)),
        out_specs=(WHOLE, WHOLE),
        scratch_shapes=[
            pltpu.VMEM((2 * count, 2 * rows, TILE), jnp.bfloat16),
            pltpu.VMEM((count, rows, TILE), jnp.bfloat16),
            pltpu.VMEM((count, 2 * rows, TILE), jnp.float32),
            pltpu.VMEM((2 * count, rows, TILE), jnp.float32),
            pltpu.VMEM((2 * shards_each, 8, TILE), jnp.int32),
            pltpu.SMEM((2 * shards_each, 8, TILE), jnp.int32),
            pltpu.SemaphoreType.DMA,
        ],
        compiler_params=pltpu.CompilerParams(vmem_limit_bytes=40 * 1024 * 1024),
        cost_estimate=pl.CostEstimate(flops=0, bytes_accessed=rows, transcendentals=0),
    )(near, far, wrows, *seps)


def products_kernel(many, *refs):
    lefts, (near_ref, far_ref), outs = refs[:many], refs[many : many + 2], refs[many + 2 :]
    size = near_ref.shape[0]
    for left_ref, out_ref in zip(lefts, outs):
        for at, ref in ((0, near_ref), (size, far_ref)):
            value = contract_last(left_ref[...], ref[...])
            out_ref[:, at : at + size] = (-value).astype(jnp.bfloat16)


def products(lefts, near, far):
    size = 2 * near.shape[0]
    return pl.pallas_call(
        functools.partial(products_kernel, len(lefts)),
        out_shape=tuple(jax.ShapeDtypeStruct((p.shape[0], size), jnp.bfloat16) for p in lefts),
        in_specs=[WHOLE] * (len(lefts) + 2),
        out_specs=(WHOLE,) * len(lefts),
        compiler_params=pltpu.CompilerParams(vmem_limit_bytes=32 * 1024 * 1024),
        cost_estimate=pl.CostEstimate(flops=0, bytes_accessed=size, transcendentals=0),
    )(*lefts, near, far)


def finish_kernel(line, place_ref, *refs):
    blocks = refs[: line * SIDES]
    factor_ref, wtile_ref, sigma_ref, tiles_ref = refs[line * SIDES :]
    rows = factor_ref.shape[0]
    width = sigma_ref.shape[1] // 2
    spot, core = place_ref[0], place_ref[1]
    total = wtile_ref[...].astype(jnp.float32)
    for d, ref in enumerate(blocks):
        at = lax.rem(spot + d, line * SIDES)
        chip = jnp.where(at < line, at * SIDES, (2 * line - 1 - at) * SIDES + 1)
        for turn in range(CORES):
            owner = core if turn == 0 else 1 - core
            for half in range(2):
                lane = (chip * CORES + owner) * rows + half * width
                lanes = pl.ds(pl.multiple_of(lane, TILE), rows)
                group = turn * 2 + half
                part = ref[:, group * rows : (group + 1) * rows]
                sigma_ref[:, lanes] = part.astype(jnp.float32)
                total -= contract_last(part, factor_ref[:, lanes])
    tiles_ref[...] = total


def finish(place, blocks, factor, wtile):
    rows = factor.shape[0]
    return pl.pallas_call(
        functools.partial(finish_kernel, len(blocks) // SIDES),
        out_shape=(
            jax.ShapeDtypeStruct(factor.shape, jnp.float32),
            jax.ShapeDtypeStruct((rows, TILE), jnp.float32),
        ),
        in_specs=[SCALAR] + [WHOLE] * (len(blocks) + 2),
        out_specs=(WHOLE, WHOLE),
        compiler_params=pltpu.CompilerParams(vmem_limit_bytes=24 * 1024 * 1024),
        cost_estimate=pl.CostEstimate(flops=0, bytes_accessed=rows, transcendentals=0),
    )(place, *blocks, factor, wtile)


def shards(ring, inverse_block, coupling_tiles, tile_pos, sep_diag, sep_cross):
    wrows = inverse_block[0]
    rows, width = wrows.shape
    tiles = coupling_tiles[0]
    per_shard = tiles.shape[0]
    diag = sep_diag[0]
    cross = sep_cross[0]
    index = lax.axis_index("rows")
    core = index % CORES
    spot = jnp.asarray(ring.spots, jnp.int32)[index // CORES]

    size = lax.axis_size("tm")
    following = lax.ppermute(diag, "tm", [(i + 1, i) for i in range(size - 1)])
    steps = ring.count // 2
    wahead = [wrows, ring.turn(wrows, 1)]
    wbehind = [wrows, ring.turn(wrows, -1)]
    packed, flipped = pack(tiles, tile_pos[0], cross)
    ahead, behind = ring.turn(packed, 1), ring.turn(packed, -1)
    ahead, behind, flipped = lax.optimization_barrier((ahead, behind, flipped))
    cols = lax.all_to_all(flipped, "rows", 0, 1, tiled=True)
    pieces = [packed, ahead, behind]
    for step in range(2, steps):
        ahead, behind = ring.turn(ahead, 1), ring.turn(behind, -1)
        if step == 2:
            ahead, behind, wahead[1], wbehind[1], following = lax.optimization_barrier(
                (ahead, behind, wahead[1], wbehind[1], following)
            )
        pieces += [ahead, behind]
    pieces.append(ring.opposite(ahead, behind))
    near = jnp.concatenate(pieces, axis=0)
    far = ring.to_core(near)

    updated, factor = factors(near, far, wrows, (diag, cross, cols, following), per_shard)
    for step in range(2, steps):
        wahead.append(ring.turn(wahead[-1], 1))
        wbehind.append(ring.turn(wbehind[-1], -1))
        if step == 2:
            updated, wahead[2], wbehind[2] = lax.optimization_barrier(
                (updated, wahead[2], wbehind[2])
            )
    other = ring.to_core(updated)

    early = min(3, steps)
    lefts = [wrows]
    for step in range(1, early):
        lefts += [wahead[step], wbehind[step]]
    done = products(lefts, updated, other)
    *done, wahead[-1], wbehind[-1] = lax.optimization_barrier((*done, wahead[-1], wbehind[-1]))
    last = ring.opposite(wahead[-1], wbehind[-1])
    blocks = [done[0]] + [None] * (ring.count - 1)
    for step in range(1, steps):
        if step < early:
            pair = done[2 * step - 1 : 2 * step + 1]
        else:
            pair = products([wahead[step], wbehind[step]], updated, other)
        blocks[step] = ring.turn(pair[0], -step)
        blocks[-step] = ring.turn(pair[1], step)
        if step == 1:
            last, blocks[1], blocks[-1] = lax.optimization_barrier((last, blocks[1], blocks[-1]))
    blocks[steps] = ring.turn(products([last], updated, other)[0], steps)

    if rows == TILE:
        wtile = lax.dynamic_slice_in_dim(wrows, index * rows, rows, 1)
        place = jnp.stack([spot, core]).astype(jnp.int32)
        sigma, result = finish(place, blocks, factor, wtile)
        return (sigma[None], result[None])
    order = (jnp.asarray(ring.spots, jnp.int32) - spot) % ring.count
    parts = jnp.take(jnp.stack(blocks), order, axis=0)
    parts = parts.reshape(ring.count, rows, CORES, 2, rows)
    parts = jnp.where(core == 0, parts, parts[:, :, ::-1])
    rounded = parts.transpose(1, 3, 0, 2, 4).reshape(rows, 2 * width)
    sigma = rounded.astype(jnp.float32)
    if rows < TILE:
        whole = factor
        for bit in range((TILE // rows).bit_length() - 1):
            pairs = [(i, i ^ 1 << bit) for i in range(lax.axis_size("rows"))]
            partner = lax.ppermute(whole, "rows", pairs)
            whole = jnp.where(
                index >> bit & 1 == 0,
                jnp.concatenate([whole, partner], axis=0),
                jnp.concatenate([partner, whole], axis=0),
            )
        overlap = contract_last(rounded, whole)
        start = index * rows // TILE * TILE
        wtile = lax.dynamic_slice_in_dim(wrows, start, TILE, 1).astype(jnp.float32)
        result_tiles = wtile - overlap
    else:
        many = rows // TILE
        overlap = jnp.einsum(
            "mrk,mck->mrc",
            rounded.reshape(many, TILE, 2 * width),
            factor.reshape(many, TILE, 2 * width),
            preferred_element_type=jnp.float32,
        )
        square = lax.dynamic_slice_in_dim(wrows, index * rows, rows, 1).reshape(
            many, TILE, many, TILE
        )
        wtile = jnp.stack([square[i, :, i, :] for i in range(many)]).astype(jnp.float32)
        result_tiles = (wtile - overlap).reshape(rows, TILE)
    return (sigma[None], result_tiles[None])


def solution(mesh):
    placed = (
        P("tm", "rows", None),
        P("tm", "rows", None, None),
        P("tm", "rows", None),
        P("tm", "rows", None),
        P("tm", "rows", None),
    )
    return jax.shard_map(
        functools.partial(shards, Ring(mesh.shape["rows"])),
        mesh=mesh,
        in_specs=placed,
        out_specs=(P("tm", "rows", None), P("tm", "rows", None)),
        check_vma=False,
    )
```

time: 303 us -> 117 us (0.39)
  waiting for transfers between devices: 229 us -> 40.3 us
  starting transfers between devices: 1.44 us -> 38.1 us
  matrix products: 29.9 us -> 0 us
  blocking collectives: 22.9 us -> 0 us
  Pallas kernels: 0 us -> 20.5 us
  between operations: 13.9 us -> 0.82 us
  local copies, waits for them, and re-layouts: 3.6 us -> 14.8 us
    all_gather x4 -> x0, waiting for transfers between devices: 212 us -> none  [the longest x1 70.6 us: shards(): piece_right = lax.all_gather(diag_right, 'rows', axis=0, tiled=True)]
    ppermute x1 -> x26, starting transfers between devices: 1.29 us -> 33.1 us  [the longest x23 31.9 us: turn(): return lax.ppermute(part, 'rows', pairs)]
    dot_general x7 -> x0, matrix products: 29.9 us -> none  [the longest x1 6.27 us: contract_last(): lax.dot_general(left, right, (((1,), (1,)), ((), ())), preferred_element_...]
    ppermute x1 -> x26, waiting for transfers between devices: 15.1 us -> 40.3 us  [the longest x23 38.7 us: turn(): return lax.ppermute(part, 'rows', pairs)]
    all_gather x1 -> x0, blocking collectives: 22.9 us -> none  [shards(): piece_pos = lax.all_gather(positions, 'rows', axis=0, tiled=True)]
    pallas_call x0 -> x6, Pallas kernels: none -> 20.5 us  [the longest x3 9.24 us: products(): pl.pallas_call(functools.partial(products_kernel, len(lefts)), out_shape=...]
    unnamed x7 -> x38, local copies, waits for them, and re-layouts: 2.29 us -> 11.2 us
    all_to_all x0 -> x1, starting transfers between devices: none -> 4.93 us  [shards(): cols = lax.all_to_all(flipped, 'rows', 0, 1, tiled=True)]
  transfers between devices with their start and end apart: 5 -> 27, of which waited for: 5 -> 13; matrix products, arithmetic and copies ran while one was open for 6% -> 8% of each run, Pallas kernels for 0% -> 15%
where the time goes in v2:
time: 117 us; the launch traced here: 116 us
  waiting for transfers between devices  40.3 us (34%)
  starting transfers between devices  38.1 us (33%)
  Pallas kernels  20.5 us (18%)
  local copies, waits for them, and re-layouts  14.8 us (13%)
  other arithmetic  1.7 us (1%)
    ppermute x23, waiting for transfers between devices, turn(): return lax.ppermute(part, 'rows', pairs)  38.7 us
    ppermute x23, starting transfers between devices, turn(): return lax.ppermute(part, 'rows', pairs)  31.9 us
    unnamed x38, local copies, waits for them, and re-layouts  11.2 us
    pallas_call x3, Pallas kernels, products(): pl.pallas_call(functools.partial(products_kernel, len(lefts)), out_shape=...  9.24 us
    pallas_call x1, Pallas kernels, factors(): pl.pallas_call(functools.partial(factors_kernel, per_shard, shards_each),...  7.08 us
    all_to_all x1, starting transfers between devices, shards(): cols = lax.all_to_all(flipped, 'rows', 0, 1, tiled=True)  4.93 us
    pallas_call x1, Pallas kernels, finish(): pl.pallas_call(functools.partial(finish_kernel, len(blocks) // SIDES), ou...  2.58 us
  transfers between devices with their start and end apart: 27, of which 13 were waited for; matrix products, arithmetic and copies ran while one was open for 8% of the time, Pallas kernels for 15%

profile of v2, /device:TPU:0, one launch (start us, length us, event | category | flops | bytes accessed | tf_op | source)
XLA Modules:
  0.0 116.2 jit_solution(6679268056942607383)
XLA Ops:
  0.6 3.1 %collective-permute-start.4 = (bf16[128,2048]{1,0:T(8,128)(2,1)}, bf16[128,2048]{1,0:T(8,128)(2,1)S(1)}, u32[]{:S(2)}, u32[]{:S(2)}) collective-permute-start(bf16[128,2048]{1,0:T(8,128)(2,1)} %bitcast.17), channel_id=1, source_target_pairs={{0,4},{1,5},{4,8},{5,9},{8,12},{9,13},{12,14},{13,15},{14,10},{15,... | collective-permute-start | bytes 1572872 | tf_op jit(solution)/shard_map/ppermute | solution.py:39
  3.7 1.3 %collective-permute-start.6 = (bf16[128,2048]{1,0:T(8,128)(2,1)}, bf16[128,2048]{1,0:T(8,128)(2,1)S(1)}, u32[]{:S(2)}, u32[]{:S(2)}) collective-permute-start(bf16[128,2048]{1,0:T(8,128)(2,1)} %bitcast.23), channel_id=1, source_target_pairs={{16,0},{17,1},{18,2},{19,3},{20,4},{21,5},{22,6},{23,7},{24,8},{25... | collective-permute-start | bytes 1572872 | tf_op jit(solution)/shard_map/ppermute | solution.py:232
  5.0 0.8 copy.10.pos_ref
  5.8 1.0 copy-done.1
  6.8 0.9 copy-done.12
  7.7 1.6 %shard_map.77 = (bf16[544,128]{1,0:T(8,128)(2,1)S(1)}, bf16[2048,128]{1,0:T(8,128)(2,1)}) custom-call(s32[4,2]{1,0:T(4,128)S(1)} %copy.10.pos_ref, bf16[4,128,128]{2,1,0:T(8,128)(2,1)S(1)} %bitcast.25, bf16[128,2048]{1,0:T(8,128)(2,1)S(1)} %bitcast.21), custom_call_target="tpu_custom_call" | custom-call | bytes 128 | tf_op jit(solution)/shard_map/pallas_call | solution.py:64
  9.3 2.0 %collective-permute-start = (bf16[544,128]{1,0:T(8,128)(2,1)S(1)}, bf16[544,128]{1,0:T(8,128)(2,1)S(1)}, u32[]{:S(2)}, u32[]{:S(2)}) collective-permute-start(bf16[544,128]{1,0:T(8,128)(2,1)S(1)} %get-tuple-element.36), channel_id=1, source_target_pairs={{0,4},{1,5},{4,8},{5,9},{8,12},{9,13},{12,14},{13,15},{14,10},{15,... | collective-permute-start | bytes 417800 | tf_op jit(solution)/shard_map/ppermute | solution.py:39
  11.3 0.7 constant_dynamic-update-slice_fusion.8
  12.0 6.8 %collective-permute-done = bf16[544,128]{1,0:T(8,128)(2,1)S(1)} collective-permute-done((bf16[544,128]{1,0:T(8,128)(2,1)S(1)}, bf16[544,128]{1,0:T(8,128)(2,1)S(1)}, u32[]{:S(2)}, u32[]{:S(2)}) %collective-permute-start) | collective-permute-done | bytes 139296 | tf_op jit(solution)/shard_map/ppermute | solution.py:39
  18.8 1.5 %collective-permute-done.1 = bf16[544,128]{1,0:T(8,128)(2,1)S(1)} collective-permute-done((bf16[544,128]{1,0:T(8,128)(2,1)S(1)}, bf16[544,128]{1,0:T(8,128)(2,1)S(1)}, u32[]{:S(2)}, u32[]{:S(2)}) %collective-permute-start.1) | collective-permute-done | bytes 139296 | tf_op jit(solution)/shard_map/ppermute | solution.py:39
  20.3 1.6 %collective-permute-start.2 = (bf16[544,128]{1,0:T(8,128)(2,1)S(1)}, bf16[544,128]{1,0:T(8,128)(2,1)S(1)}, u32[]{:S(2)}, u32[]{:S(2)}) collective-permute-start(bf16[544,128]{1,0:T(8,128)(2,1)S(1)} %collective-permute-done), channel_id=1, source_target_pairs={{0,4},{1,5},{4,8},{5,9},{8,12},{9,13},{12,14},{13,15},{14,10},{15,... | collective-permute-start | bytes 417800 | tf_op jit(solution)/shard_map/ppermute | solution.py:39
  22.3 0.7 constant_dynamic-update-slice_fusion.7
  23.0 4.9 %all-to-all-start = ((bf16[16,128,128]{2,1,0:T(8,128)(2,1)}), bf16[16,128,128]{2,1,0:T(8,128)(2,1)S(1)}, u32[]{:S(2)}, u32[]{:S(2)}) async-start(bf16[16,128,128]{2,1,0:T(8,128)(2,1)} %bitcast.6), calls=%async_computation | async-start | bytes 1048576 | tf_op jit(solution)/shard_map/all_to_all | solution.py:239
  27.9 0.7 constant_dynamic-update-slice_fusion.6
  28.6 2.0 %collective-permute-start.7 = (bf16[544,128]{1,0:T(8,128)(2,1)S(1)}, bf16[544,128]{1,0:T(8,128)(2,1)S(1)}, u32[]{:S(2)}, u32[]{:S(2)}) collective-permute-start(bf16[544,128]{1,0:T(8,128)(2,1)S(1)} %collective-permute-done.2), channel_id=1, source_target_pairs={{0,4},{1,5},{4,8},{5,9},{8,12},{9,13},{12,14},{13,15},{14,10},{15,... | collective-permute-start | bytes 417800 | tf_op jit(solution)/shard_map/ppermute | solution.py:39
  30.7 0.7 constant_dynamic-update-slice_fusion.5
  31.4 0.7 constant_dynamic-update-slice_fusion.4
  32.1 8.4 %collective-permute-done.7 = bf16[544,128]{1,0:T(8,128)(2,1)S(1)} collective-permute-done((bf16[544,128]{1,0:T(8,128)(2,1)S(1)}, bf16[544,128]{1,0:T(8,128)(2,1)S(1)}, u32[]{:S(2)}, u32[]{:S(2)}) %collective-permute-start.7) | collective-permute-done | bytes 139296 | tf_op jit(solution)/shard_map/ppermute | solution.py:39
  40.4 4.5 %collective-permute-start.9 = (bf16[272,128]{1,0:T(8,128)(2,1)S(1)}, bf16[272,128]{1,0:T(8,128)(2,1)S(1)}, u32[]{:S(2)}, u32[]{:S(2)}) collective-permute-start(bf16[272,128]{1,0:T(8,128)(2,1)S(1)} %slice.16), channel_id=1, source_target_pairs={{0,4},{1,5},{4,8},{5,9},{8,12},{9,13},{12,14},{13,15},{14,10},{15,... | collective-permute-start | bytes 208904 | tf_op jit(solution)/shard_map/ppermute | solution.py:39
  45.0 0.7 constant_dynamic-update-slice_fusion.3
  47.5 2.3 %collective-permute-done.10 = bf16[272,128]{1,0:T(8,128)(2,1)S(1)} collective-permute-done((bf16[272,128]{1,0:T(8,128)(2,1)S(1)}, bf16[272,128]{1,0:T(8,128)(2,1)S(1)}, u32[]{:S(2)}, u32[]{:S(2)}) %collective-permute-start.10) | collective-permute-done | bytes 69664 | tf_op jit(solution)/shard_map/ppermute | solution.py:39
  50.4 2.0 %collective-permute-start.12 = (bf16[128,2048]{1,0:T(8,128)(2,1)S(1)}, bf16[128,2048]{1,0:T(8,128)(2,1)}, u32[]{:S(2)}, u32[]{:S(2)}) collective-permute-start(bf16[128,2048]{1,0:T(8,128)(2,1)S(1)} %collective-permute-done.4.refs_1_), channel_id=1, source_target_pairs={{0,4},{1,5},{4,8},{5,9},{8,12},{9,13},{12,14},{13,15},{14,10},{15,... | collective-permute-start | bytes 1572872 | tf_op jit(solution)/shard_map/ppermute | solution.py:39
  52.5 1.0 collective-permute-done.11.far_ref
  53.5 1.0 copy-done.11
  54.5 7.1 %shard_map.78 = (bf16[256,2048]{1,0:T(8,128)(2,1)S(1)}, bf16[128,4096]{1,0:T(8,128)(2,1)S(1)}) custom-call(bf16[4352,128]{1,0:T(8,128)(2,1)} %constant_dynamic-update-slice_fusion.near_ref, bf16[4352,128]{1,0:T(8,128)(2,1)} %collective-permute-done.11.far_ref, bf16[128,2048]{1,0:T(8,128)(2,1)S(1)} %bitcast.19, bf16[128,2048]{1,0:T(8,128)(2,1)S(1)} %bitcast.24, ...), custom_call_target="tpu_custom_call" | custom-call | bytes 128 | tf_op jit(solution)/shard_map/pallas_call | solution.py:140
  61.6 3.2 %collective-permute-done.12.refs_3_ = bf16[128,2048]{1,0:T(8,128)(2,1)} collective-permute-done((bf16[128,2048]{1,0:T(8,128)(2,1)S(1)}, bf16[128,2048]{1,0:T(8,128)(2,1)}, u32[]{:S(2)}, u32[]{:S(2)}) %collective-permute-start.12) | collective-permute-done | bytes 524320 | tf_op jit(solution)/shard_map/ppermute | solution.py:39
  64.8 2.0 %collective-permute-done.13.refs_4_ = bf16[128,2048]{1,0:T(8,128)(2,1)} collective-permute-done((bf16[128,2048]{1,0:T(8,128)(2,1)}, bf16[128,2048]{1,0:T(8,128)(2,1)}, u32[]{:S(2)}, u32[]{:S(2)}) %collective-permute-start.13) | collective-permute-done | bytes 524320 | tf_op jit(solution)/shard_map/ppermute | solution.py:39
  67.3 1.4 %collective-permute-start.16 = (bf16[128,2048]{1,0:T(8,128)(2,1)}, bf16[128,2048]{1,0:T(8,128)(2,1)S(1)}, u32[]{:S(2)}, u32[]{:S(2)}) collective-permute-start(bf16[128,2048]{1,0:T(8,128)(2,1)} %collective-permute-done.13.refs_4_), channel_id=1, source_target_pairs={{0,2},{1,3},{4,0},{5,1},{8,4},{9,5},{12,8},{13,9},{14,12},{15,13},... | collective-permute-start | bytes 1572872 | tf_op jit(solution)/shard_map/ppermute | solution.py:39
  69.4 5.6 %shard_map.79 = (bf16[128,512]{1,0:T(8,128)(2,1)S(1)}, bf16[128,512]{1,0:T(8,128)(2,1)}, bf16[128,512]{1,0:T(8,128)(2,1)S(1)}, bf16[128,512]{1,0:T(8,128)(2,1)}, bf16[128,512]{1,0:T(8,128)(2,1)}) custom-call(bf16[128,2048]{1,0:T(8,128)(2,1)S(1)} %bitcast.20, bf16[128,2048]{1,0:T(8,128)(2,1)S(1)} %copy-done.9, ...), custom_call_target="tpu_custom_call" | custom-call | bytes 512 | tf_op jit(solution)/shard_map/pallas_call | solution.py:173
  75.7 5.6 %collective-permute-done.15.refs_0_ = bf16[128,2048]{1,0:T(8,128)(2,1)S(1)} collective-permute-done((bf16[128,2048]{1,0:T(8,128)(2,1)}, bf16[128,2048]{1,0:T(8,128)(2,1)S(1)}, u32[]{:S(2)}, u32[]{:S(2)}) %collective-permute-start.15) | collective-permute-done | bytes 524320 | tf_op jit(solution)/shard_map/ppermute | solution.py:39
  81.6 0.8 slice.14
  82.4 0.8 collective-permute-start.17
  83.2 0.7 slice.15
  84.0 1.2 %collective-permute-start.18 = (bf16[64,2048]{1,0:T(8,128)(2,1)}, bf16[64,2048]{1,0:T(8,128)(2,1)}, u32[]{:S(2)}, u32[]{:S(2)}) collective-permute-start(bf16[64,2048]{1,0:T(8,128)(2,1)} %slice.15), channel_id=1, source_target_pairs={{0,2},{1,3},{4,0},{5,1},{8,4},{9,5},{12,8},{13,9},{14,12},{15,13},... | collective-permute-start | bytes 786440 | tf_op jit(solution)/shard_map/ppermute | solution.py:39
  85.7 1.4 %collective-permute-start.19 = (bf16[128,512]{1,0:T(8,128)(2,1)}, bf16[128,512]{1,0:T(8,128)(2,1)S(1)}, u32[]{:S(2)}, u32[]{:S(2)}) collective-permute-start(bf16[128,512]{1,0:T(8,128)(2,1)} %get-tuple-element.58), channel_id=1, source_target_pairs={{0,2},{1,3},{4,0},{5,1},{8,4},{9,5},{12,8},{13,9},{14,12},{15,13},... | collective-permute-start | bytes 393224 | tf_op jit(solution)/shard_map/ppermute | solution.py:39
  87.8 1.0 copy-done.4
  88.8 2.2 %shard_map.80 = (bf16[128,512]{1,0:T(8,128)(2,1)}, bf16[128,512]{1,0:T(8,128)(2,1)}) custom-call(bf16[128,2048]{1,0:T(8,128)(2,1)S(1)} %collective-permute-done.15.refs_0_, bf16[128,2048]{1,0:T(8,128)(2,1)S(1)} %copy-done.4, bf16[256,2048]{1,0:T(8,128)(2,1)S(1)} %get-tuple-element.49.refs_5_.refs_2_.refs_1_, ...), custom_call_target="tpu_custom_call" | custom-call | bytes 512 | tf_op jit(solution)/shard_map/pallas_call | solution.py:173
  91.0 2.0 %collective-permute-start.22 = (bf16[128,512]{1,0:T(8,128)(2,1)}, bf16[128,512]{1,0:T(8,128)(2,1)S(1)}, u32[]{:S(2)}, u32[]{:S(2)}) collective-permute-start(bf16[128,512]{1,0:T(8,128)(2,1)} %get-tuple-element.62), channel_id=1, source_target_pairs={{0,10},{1,11},{4,6},{5,7},{8,2},{9,3},{12,0},{13,1},{14,4},{15,5},... | collective-permute-start | bytes 393224 | tf_op jit(solution)/shard_map/ppermute | solution.py:39
  93.0 1.9 %collective-permute-start.24 = (bf16[128,512]{1,0:T(8,128)(2,1)}, bf16[128,512]{1,0:T(8,128)(2,1)S(1)}, u32[]{:S(2)}, u32[]{:S(2)}) collective-permute-start(bf16[128,512]{1,0:T(8,128)(2,1)} %get-tuple-element.64), channel_id=1, source_target_pairs={{0,12},{1,13},{4,14},{5,15},{8,10},{9,11},{12,6},{13,7},{14,2},{15... | collective-permute-start | bytes 393224 | tf_op jit(solution)/shard_map/ppermute | solution.py:39
  94.9 0.8 collective-permute-start.21
  95.7 1.1 pad_maximum_fusion.refs_0_
  96.8 2.4 %collective-permute-start.25 = (bf16[128,512]{1,0:T(8,128)(2,1)}, bf16[128,512]{1,0:T(8,128)(2,1)S(1)}, u32[]{:S(2)}, u32[]{:S(2)}) collective-permute-start(bf16[128,512]{1,0:T(8,128)(2,1)} %get-tuple-element.65), channel_id=1, source_target_pairs={{0,8},{1,9},{4,12},{5,13},{8,14},{9,15},{12,10},{13,11},{14,6},{15... | collective-permute-start | bytes 393224 | tf_op jit(solution)/shard_map/ppermute | solution.py:39
  99.2 1.5 %shard_map.81 = bf16[128,512]{1,0:T(8,128)(2,1)} custom-call(bf16[128,2048]{1,0:T(8,128)(2,1)S(1)} %pad_maximum_fusion.refs_0_, bf16[256,2048]{1,0:T(8,128)(2,1)S(1)} %get-tuple-element.49.refs_5_.refs_2_.refs_1_, bf16[256,2048]{1,0:T(8,128)(2,1)S(1)} %collective-permute-done.14.refs_6_.refs_3_.refs_2_), custom_call_target="tpu_custom_call" | custom-call | bytes 512 | tf_op jit(solution)/shard_map/pallas_call | solution.py:173
  100.6 2.9 %collective-permute-start.23 = (bf16[128,512]{1,0:T(8,128)(2,1)}, bf16[128,512]{1,0:T(8,128)(2,1)S(1)}, u32[]{:S(2)}, u32[]{:S(2)}) collective-permute-start(bf16[128,512]{1,0:T(8,128)(2,1)} %shard_map.81), channel_id=1, source_target_pairs={{0,14},{1,15},{4,10},{5,11},{8,6},{9,7},{12,2},{13,3},{14,0},{15,1... | collective-permute-start | bytes 393224 | tf_op jit(solution)/shard_map/ppermute | solution.py:39
  104.2 5.4 %collective-permute-done.24.refs_5_ = bf16[128,512]{1,0:T(8,128)(2,1)S(1)} collective-permute-done((bf16[128,512]{1,0:T(8,128)(2,1)}, bf16[128,512]{1,0:T(8,128)(2,1)S(1)}, u32[]{:S(2)}, u32[]{:S(2)}) %collective-permute-start.24) | collective-permute-done | bytes 131104 | tf_op jit(solution)/shard_map/ppermute | solution.py:39
  109.7 2.7 %collective-permute-done.21.refs_2_ = bf16[128,512]{1,0:T(8,128)(2,1)S(1)} collective-permute-done((bf16[128,512]{1,0:T(8,128)(2,1)}, bf16[128,512]{1,0:T(8,128)(2,1)S(1)}, u32[]{:S(2)}, u32[]{:S(2)}) %collective-permute-start.21) | collective-permute-done | bytes 131104 | tf_op jit(solution)/shard_map/ppermute | solution.py:39
  112.4 1.2 %copy-done.6 = bf16[128,4096]{1,0:T(8,128)(2,1)S(1)} copy-done((bf16[128,4096]{1,0:T(8,128)(2,1)S(1)}, bf16[128,4096]{1,0:T(8,128)(2,1)}, u32[]{:S(2)}) %copy-start.6) | copy-done | bytes 1048600
  113.6 2.6 %shard_map.82 = (f32[128,4096]{1,0:T(8,128)}, f32[128,128]{1,0:T(8,128)}) custom-call(s32[2]{0:T(128)S(1)} %pad_add_fusion.place_ref, bf16[128,512]{1,0:T(8,128)(2,1)S(1)} %get-tuple-element.55.refs_0_, bf16[128,512]{1,0:T(8,128)(2,1)S(1)} %collective-permute-done.19.refs_1_, bf16[128,512]{1,0:T(8,128)(2,1)S(1)} %collective-permute-done.21.refs_2_, ...), custom_call_target="tpu_custom_call" | custom-call | bytes 128 | tf_op jit(solution)/shard_map/pallas_call | solution.py:207
  (61 shorter events, 7.2 us)
Async XLA Ops:
  0.6 28.0 %collective-permute-start.4 = (bf16[128,2048]{1,0:T(8,128)(2,1)}, bf16[128,2048]{1,0:T(8,128)(2,1)S(1)}, u32[]{:S(2)}, u32[]{:S(2)}) collective-permute-start(bf16[128,2048]{1,0:T(8,128)(2,1)} %bitcast.17), channel_id=1, source_target_pairs={{0,4},{1,5},{4,8},{5,9},{8,12},{9,13},{12,14},{13,15},{14,10},{15,... | collective-permute-start | bytes 1572872 | tf_op jit(solution)/shard_map/ppermute | solution.py:39
  3.7 24.9 %collective-permute-start.5 = (bf16[128,2048]{1,0:T(8,128)(2,1)}, bf16[128,2048]{1,0:T(8,128)(2,1)}, u32[]{:S(2)}, u32[]{:S(2)}) collective-permute-start(bf16[128,2048]{1,0:T(8,128)(2,1)} %bitcast.18), channel_id=1, source_target_pairs={{0,2},{1,3},{4,0},{5,1},{8,4},{9,5},{12,8},{13,9},{14,12},{15,13},... | collective-permute-start | bytes 1572872 | tf_op jit(solution)/shard_map/ppermute | solution.py:39
  3.7 24.9 %collective-permute-start.6 = (bf16[128,2048]{1,0:T(8,128)(2,1)}, bf16[128,2048]{1,0:T(8,128)(2,1)S(1)}, u32[]{:S(2)}, u32[]{:S(2)}) collective-permute-start(bf16[128,2048]{1,0:T(8,128)(2,1)} %bitcast.23), channel_id=1, source_target_pairs={{16,0},{17,1},{18,2},{19,3},{20,4},{21,5},{22,6},{23,7},{24,8},{25... | collective-permute-start | bytes 1572872 | tf_op jit(solution)/shard_map/ppermute | solution.py:232
  5.8 1.0 copy-start.1
  6.8 0.9 copy-start.12
  9.3 9.5 %collective-permute-start = (bf16[544,128]{1,0:T(8,128)(2,1)S(1)}, bf16[544,128]{1,0:T(8,128)(2,1)S(1)}, u32[]{:S(2)}, u32[]{:S(2)}) collective-permute-start(bf16[544,128]{1,0:T(8,128)(2,1)S(1)} %get-tuple-element.36), channel_id=1, source_target_pairs={{0,4},{1,5},{4,8},{5,9},{8,12},{9,13},{12,14},{13,15},{14,10},{15,... | collective-permute-start | bytes 417800 | tf_op jit(solution)/shard_map/ppermute | solution.py:39
  11.3 9.0 %collective-permute-start.1 = (bf16[544,128]{1,0:T(8,128)(2,1)S(1)}, bf16[544,128]{1,0:T(8,128)(2,1)S(1)}, u32[]{:S(2)}, u32[]{:S(2)}) collective-permute-start(bf16[544,128]{1,0:T(8,128)(2,1)S(1)} %get-tuple-element.36), channel_id=1, source_target_pairs={{0,2},{1,3},{4,0},{5,1},{8,4},{9,5},{12,8},{13,9},{14,12},{15,13},... | collective-permute-start | bytes 417800 | tf_op jit(solution)/shard_map/ppermute | solution.py:39
  20.3 8.3 %collective-permute-start.2 = (bf16[544,128]{1,0:T(8,128)(2,1)S(1)}, bf16[544,128]{1,0:T(8,128)(2,1)S(1)}, u32[]{:S(2)}, u32[]{:S(2)}) collective-permute-start(bf16[544,128]{1,0:T(8,128)(2,1)S(1)} %collective-permute-done), channel_id=1, source_target_pairs={{0,4},{1,5},{4,8},{5,9},{8,12},{9,13},{12,14},{13,15},{14,10},{15,... | collective-permute-start | bytes 417800 | tf_op jit(solution)/shard_map/ppermute | solution.py:39
  21.9 6.7 %collective-permute-start.3 = (bf16[544,128]{1,0:T(8,128)(2,1)S(1)}, bf16[544,128]{1,0:T(8,128)(2,1)S(1)}, u32[]{:S(2)}, u32[]{:S(2)}) collective-permute-start(bf16[544,128]{1,0:T(8,128)(2,1)S(1)} %collective-permute-done.1), channel_id=1, source_target_pairs={{0,2},{1,3},{4,0},{5,1},{8,4},{9,5},{12,8},{13,9},{14,12},{15,13},... | collective-permute-start | bytes 417800 | tf_op jit(solution)/shard_map/ppermute | solution.py:39
  23.0 29.4 %all-to-all-start = ((bf16[16,128,128]{2,1,0:T(8,128)(2,1)}), bf16[16,128,128]{2,1,0:T(8,128)(2,1)S(1)}, u32[]{:S(2)}, u32[]{:S(2)}) async-start(bf16[16,128,128]{2,1,0:T(8,128)(2,1)} %bitcast.6), calls=%async_computation | async-start | bytes 1048576 | tf_op jit(solution)/shard_map/all_to_all | solution.py:239
  28.6 23.9 %copy-start.8 = (bf16[128,2048]{1,0:T(8,128)(2,1)}, bf16[128,2048]{1,0:T(8,128)(2,1)S(1)}, u32[]{:S(2)}) copy-start(bf16[128,2048]{1,0:T(8,128)(2,1)S(1)} %collective-permute-done.4.refs_1_) | copy-start | bytes 1572868
  28.6 23.9 %copy-start.10 = (bf16[128,2048]{1,0:T(8,128)(2,1)}, bf16[128,2048]{1,0:T(8,128)(2,1)S(1)}, u32[]{:S(2)}) copy-start(bf16[128,2048]{1,0:T(8,128)(2,1)S(1)} %collective-permute-done.6.next_ref) | copy-start | bytes 1572868
  28.6 11.8 %collective-permute-start.7 = (bf16[544,128]{1,0:T(8,128)(2,1)S(1)}, bf16[544,128]{1,0:T(8,128)(2,1)S(1)}, u32[]{:S(2)}, u32[]{:S(2)}) collective-permute-start(bf16[544,128]{1,0:T(8,128)(2,1)S(1)} %collective-permute-done.2), channel_id=1, source_target_pairs={{0,4},{1,5},{4,8},{5,9},{8,12},{9,13},{12,14},{13,15},{14,10},{15,... | collective-permute-start | bytes 417800 | tf_op jit(solution)/shard_map/ppermute | solution.py:39
  30.6 14.3 %collective-permute-start.8 = (bf16[544,128]{1,0:T(8,128)(2,1)S(1)}, bf16[544,128]{1,0:T(8,128)(2,1)S(1)}, u32[]{:S(2)}, u32[]{:S(2)}) collective-permute-start(bf16[544,128]{1,0:T(8,128)(2,1)S(1)} %collective-permute-done.3), channel_id=1, source_target_pairs={{0,2},{1,3},{4,0},{5,1},{8,4},{9,5},{12,8},{13,9},{14,12},{15,13},... | collective-permute-start | bytes 417800 | tf_op jit(solution)/shard_map/ppermute | solution.py:39
  32.1 21.4 %copy-start = (bf16[1,128,2048]{2,1,0:T(8,128)(2,1)S(1)}, bf16[1,128,2048]{2,1,0:T(8,128)(2,1)}, u32[]{:S(2)}) copy-start(bf16[1,128,2048]{2,1,0:T(8,128)(2,1)} %param.6) | copy-start | bytes 1572868
  32.1 21.4 %copy-start.2 = (bf16[1,128,2048]{2,1,0:T(8,128)(2,1)S(1)}, bf16[1,128,2048]{2,1,0:T(8,128)(2,1)}, u32[]{:S(2)}) copy-start(bf16[1,128,2048]{2,1,0:T(8,128)(2,1)} %param.10) | copy-start | bytes 1572868
  32.1 21.4 %copy-start.7 = (bf16[1,128,2048]{2,1,0:T(8,128)(2,1)S(1)}, bf16[1,128,2048]{2,1,0:T(8,128)(2,1)}, u32[]{:S(2)}) copy-start(bf16[1,128,2048]{2,1,0:T(8,128)(2,1)} %param.9) | copy-start | bytes 1572868
  40.4 6.4 %collective-permute-start.9 = (bf16[272,128]{1,0:T(8,128)(2,1)S(1)}, bf16[272,128]{1,0:T(8,128)(2,1)S(1)}, u32[]{:S(2)}, u32[]{:S(2)}) collective-permute-start(bf16[272,128]{1,0:T(8,128)(2,1)S(1)} %slice.16), channel_id=1, source_target_pairs={{0,4},{1,5},{4,8},{5,9},{8,12},{9,13},{12,14},{13,15},{14,10},{15,... | collective-permute-start | bytes 208904 | tf_op jit(solution)/shard_map/ppermute | solution.py:39
  44.9 4.8 %collective-permute-start.10 = (bf16[272,128]{1,0:T(8,128)(2,1)S(1)}, bf16[272,128]{1,0:T(8,128)(2,1)S(1)}, u32[]{:S(2)}, u32[]{:S(2)}) collective-permute-start(bf16[272,128]{1,0:T(8,128)(2,1)S(1)} %slice.17), channel_id=1, source_target_pairs={{0,2},{1,3},{4,0},{5,1},{8,4},{9,5},{12,8},{13,9},{14,12},{15,13},... | collective-permute-start | bytes 208904 | tf_op jit(solution)/shard_map/ppermute | solution.py:39
  50.4 3.1 %collective-permute-start.11 = (bf16[4352,128]{1,0:T(8,128)(2,1)}, bf16[4352,128]{1,0:T(8,128)(2,1)}, u32[]{:S(2)}, u32[]{:S(2)}) collective-permute-start(bf16[4352,128]{1,0:T(8,128)(2,1)} %constant_dynamic-update-slice_fusion.near_ref), channel_id=1, source_target_pairs={{0,1},{1,0},{2,3},{3,2},{4,5},{5,4},{6,7},{7,6},{8,9},{9,8},{10,11... | collective-permute-start | bytes 3342344 | tf_op jit(solution)/shard_map/ppermute | solution.py:43
  50.4 14.4 %collective-permute-start.12 = (bf16[128,2048]{1,0:T(8,128)(2,1)S(1)}, bf16[128,2048]{1,0:T(8,128)(2,1)}, u32[]{:S(2)}, u32[]{:S(2)}) collective-permute-start(bf16[128,2048]{1,0:T(8,128)(2,1)S(1)} %collective-permute-done.4.refs_1_), channel_id=1, source_target_pairs={{0,4},{1,5},{4,8},{5,9},{8,12},{9,13},{12,14},{13,15},{14,10},{15,... | collective-permute-start | bytes 1572872 | tf_op jit(solution)/shard_map/ppermute | solution.py:39
  52.4 14.4 %collective-permute-start.13 = (bf16[128,2048]{1,0:T(8,128)(2,1)}, bf16[128,2048]{1,0:T(8,128)(2,1)}, u32[]{:S(2)}, u32[]{:S(2)}) collective-permute-start(bf16[128,2048]{1,0:T(8,128)(2,1)} %collective-permute-done.5.refs_2_), channel_id=1, source_target_pairs={{0,2},{1,3},{4,0},{5,1},{8,4},{9,5},{12,8},{13,9},{14,12},{15,13},... | collective-permute-start | bytes 1572872 | tf_op jit(solution)/shard_map/ppermute | solution.py:39
  53.5 1.0 copy-start.11
  54.5 14.9 %copy-start.9 = (bf16[128,2048]{1,0:T(8,128)(2,1)S(1)}, bf16[128,2048]{1,0:T(8,128)(2,1)}, u32[]{:S(2)}) copy-start(bf16[128,2048]{1,0:T(8,128)(2,1)} %copy-done.8) | copy-start | bytes 1572868
  61.6 13.4 %copy-start.5 = (bf16[128,4096]{1,0:T(8,128)(2,1)}, bf16[128,4096]{1,0:T(8,128)(2,1)S(1)}, u32[]{:S(2)}) copy-start(bf16[128,4096]{1,0:T(8,128)(2,1)S(1)} %get-tuple-element.67.refs_8_) | copy-start | bytes 3145732
  66.8 18.4 %copy-start.14 = (s32[8]{0:T(128)S(1)}, s32[8]{0:T(128)}, u32[]{:S(2)}) copy-start(s32[8]{0:T(128)} %constant.38.clone) | copy-start | bytes 100
  66.8 2.7 %collective-permute-start.14 = (bf16[256,2048]{1,0:T(8,128)(2,1)S(1)}, bf16[256,2048]{1,0:T(8,128)(2,1)S(1)}, u32[]{:S(2)}, u32[]{:S(2)}) collective-permute-start(bf16[256,2048]{1,0:T(8,128)(2,1)S(1)} %get-tuple-element.49.refs_5_.refs_2_.refs_1_), channel_id=1, source_target_pairs={{0,1},{1,0},{2,3},{3,2},{4,5},{5,4},{6,7},{7,6},{8,9},{9,8},{10,11... | collective-permute-start | bytes 3145736 | tf_op jit(solution)/shard_map/ppermute | solution.py:43
  66.8 14.5 %collective-permute-start.15 = (bf16[128,2048]{1,0:T(8,128)(2,1)}, bf16[128,2048]{1,0:T(8,128)(2,1)S(1)}, u32[]{:S(2)}, u32[]{:S(2)}) collective-permute-start(bf16[128,2048]{1,0:T(8,128)(2,1)} %collective-permute-done.12.refs_3_), channel_id=1, source_target_pairs={{0,4},{1,5},{4,8},{5,9},{8,12},{9,13},{12,14},{13,15},{14,10},{15,... | collective-permute-start | bytes 1572872 | tf_op jit(solution)/shard_map/ppermute | solution.py:39
  67.3 14.3 %collective-permute-start.16 = (bf16[128,2048]{1,0:T(8,128)(2,1)}, bf16[128,2048]{1,0:T(8,128)(2,1)S(1)}, u32[]{:S(2)}, u32[]{:S(2)}) collective-permute-start(bf16[128,2048]{1,0:T(8,128)(2,1)} %collective-permute-done.13.refs_4_), channel_id=1, source_target_pairs={{0,2},{1,3},{4,0},{5,1},{8,4},{9,5},{12,8},{13,9},{14,12},{15,13},... | collective-permute-start | bytes 1572872 | tf_op jit(solution)/shard_map/ppermute | solution.py:39
  75.0 0.7 copy-start.13
  81.6 1.6 %copy-start.3 = (bf16[128,2048]{1,0:T(8,128)(2,1)}, bf16[128,2048]{1,0:T(8,128)(2,1)S(1)}, u32[]{:S(2)}) copy-start(bf16[128,2048]{1,0:T(8,128)(2,1)S(1)} %collective-permute-done.16.refs_1_) | copy-start | bytes 1572868
  82.4 10.6 %collective-permute-start.17 = (bf16[64,2048]{1,0:T(8,128)(2,1)}, bf16[64,2048]{1,0:T(8,128)(2,1)}, u32[]{:S(2)}, u32[]{:S(2)}) collective-permute-start(bf16[64,2048]{1,0:T(8,128)(2,1)} %slice.14), channel_id=1, source_target_pairs={{0,4},{1,5},{4,8},{5,9},{8,12},{9,13},{12,14},{13,15},{14,10},{15,... | collective-permute-start | bytes 786440 | tf_op jit(solution)/shard_map/ppermute | solution.py:39
  84.0 11.0 %collective-permute-start.18 = (bf16[64,2048]{1,0:T(8,128)(2,1)}, bf16[64,2048]{1,0:T(8,128)(2,1)}, u32[]{:S(2)}, u32[]{:S(2)}) collective-permute-start(bf16[64,2048]{1,0:T(8,128)(2,1)} %slice.15), channel_id=1, source_target_pairs={{0,2},{1,3},{4,0},{5,1},{8,4},{9,5},{12,8},{13,9},{14,12},{15,13},... | collective-permute-start | bytes 786440 | tf_op jit(solution)/shard_map/ppermute | solution.py:39
  85.7 11.1 %collective-permute-start.19 = (bf16[128,512]{1,0:T(8,128)(2,1)}, bf16[128,512]{1,0:T(8,128)(2,1)S(1)}, u32[]{:S(2)}, u32[]{:S(2)}) collective-permute-start(bf16[128,512]{1,0:T(8,128)(2,1)} %get-tuple-element.58), channel_id=1, source_target_pairs={{0,2},{1,3},{4,0},{5,1},{8,4},{9,5},{12,8},{13,9},{14,12},{15,13},... | collective-permute-start | bytes 393224 | tf_op jit(solution)/shard_map/ppermute | solution.py:39
  87.2 12.0 %collective-permute-start.20 = (bf16[128,512]{1,0:T(8,128)(2,1)}, bf16[128,512]{1,0:T(8,128)(2,1)S(1)}, u32[]{:S(2)}, u32[]{:S(2)}) collective-permute-start(bf16[128,512]{1,0:T(8,128)(2,1)} %copy-done.13), channel_id=1, source_target_pairs={{0,4},{1,5},{4,8},{5,9},{8,12},{9,13},{12,14},{13,15},{14,10},{15,... | collective-permute-start | bytes 393224 | tf_op jit(solution)/shard_map/ppermute | solution.py:39
  87.8 1.0 copy-start.4
  91.0 13.2 %collective-permute-start.22 = (bf16[128,512]{1,0:T(8,128)(2,1)}, bf16[128,512]{1,0:T(8,128)(2,1)S(1)}, u32[]{:S(2)}, u32[]{:S(2)}) collective-permute-start(bf16[128,512]{1,0:T(8,128)(2,1)} %get-tuple-element.62), channel_id=1, source_target_pairs={{0,10},{1,11},{4,6},{5,7},{8,2},{9,3},{12,0},{13,1},{14,4},{15,5},... | collective-permute-start | bytes 393224 | tf_op jit(solution)/shard_map/ppermute | solution.py:39
  93.0 16.7 %collective-permute-start.24 = (bf16[128,512]{1,0:T(8,128)(2,1)}, bf16[128,512]{1,0:T(8,128)(2,1)S(1)}, u32[]{:S(2)}, u32[]{:S(2)}) collective-permute-start(bf16[128,512]{1,0:T(8,128)(2,1)} %get-tuple-element.64), channel_id=1, source_target_pairs={{0,12},{1,13},{4,14},{5,15},{8,10},{9,11},{12,6},{13,7},{14,2},{15... | collective-permute-start | bytes 393224 | tf_op jit(solution)/shard_map/ppermute | solution.py:39
  94.9 17.4 %collective-permute-start.21 = (bf16[128,512]{1,0:T(8,128)(2,1)}, bf16[128,512]{1,0:T(8,128)(2,1)S(1)}, u32[]{:S(2)}, u32[]{:S(2)}) collective-permute-start(bf16[128,512]{1,0:T(8,128)(2,1)} %get-tuple-element.61), channel_id=1, source_target_pairs={{0,6},{1,7},{4,2},{5,3},{8,0},{9,1},{12,4},{13,5},{14,8},{15,9},{1... | collective-permute-start | bytes 393224 | tf_op jit(solution)/shard_map/ppermute | solution.py:39
  96.8 15.6 %collective-permute-start.25 = (bf16[128,512]{1,0:T(8,128)(2,1)}, bf16[128,512]{1,0:T(8,128)(2,1)S(1)}, u32[]{:S(2)}, u32[]{:S(2)}) collective-permute-start(bf16[128,512]{1,0:T(8,128)(2,1)} %get-tuple-element.65), channel_id=1, source_target_pairs={{0,8},{1,9},{4,12},{5,13},{8,14},{9,15},{12,10},{13,11},{14,6},{15... | collective-permute-start | bytes 393224 | tf_op jit(solution)/shard_map/ppermute | solution.py:39
  100.6 11.7 %collective-permute-start.23 = (bf16[128,512]{1,0:T(8,128)(2,1)}, bf16[128,512]{1,0:T(8,128)(2,1)S(1)}, u32[]{:S(2)}, u32[]{:S(2)}) collective-permute-start(bf16[128,512]{1,0:T(8,128)(2,1)} %shard_map.81), channel_id=1, source_target_pairs={{0,14},{1,15},{4,10},{5,11},{8,6},{9,7},{12,2},{13,3},{14,0},{15,1... | collective-permute-start | bytes 393224 | tf_op jit(solution)/shard_map/ppermute | solution.py:39
  112.4 1.2 %copy-start.6 = (bf16[128,4096]{1,0:T(8,128)(2,1)S(1)}, bf16[128,4096]{1,0:T(8,128)(2,1)}, u32[]{:S(2)}) copy-start(bf16[128,4096]{1,0:T(8,128)(2,1)} %copy-done.5) | copy-start | bytes 3145732

commit v3 on v2

v3 whole, which is shorter than its diff:
```python
import functools

import jax
import jax.numpy as jnp
from jax import lax
from jax.experimental import pallas as pl
from jax.experimental.pallas import tpu as pltpu
from jax.sharding import PartitionSpec as P

TILE = 128
PAD = 16
SIDES = 2
CORES = 2

WHOLE = pl.BlockSpec(memory_space=pltpu.VMEM)
SCALAR = pl.BlockSpec(memory_space=pltpu.SMEM)


def contract_last(left, right):
    return lax.dot_general(
        left, right, (((1,), (1,)), ((), ())), preferred_element_type=jnp.float32
    )


class Ring:
    def __init__(self, devices):
        self.line = devices // (SIDES * CORES)
        self.count = self.line * SIDES
        ups = [(z, 0) for z in range(self.line)]
        downs = [(z, 1) for z in reversed(range(self.line))]
        self.chips = [z * SIDES + y for z, y in ups + downs]
        self.spots = [self.chips.index(chip) for chip in range(self.count)]

    def turn(self, part, by):
        pairs = []
        for at, chip in enumerate(self.chips):
            target = self.chips[(at + by) % self.count]
            pairs += [(chip * CORES + c, target * CORES + c) for c in range(CORES)]
        return lax.ppermute(part, "rows", pairs)

    def to_core(self, part):
        devices = self.count * CORES
        return lax.ppermute(part, "rows", [(i, i ^ 1) for i in range(devices)])

    def opposite(self, ahead, behind):
        half = ahead.shape[0] // 2
        first = self.turn(ahead[:half], 1)
        return jnp.concatenate([first, self.turn(behind[half:], -1)], axis=0)


def flip_kernel(pos_ref, cross_ref, out_ref):
    devices, _, rows = out_ref.shape
    lane = lax.broadcasted_iota(jnp.int32, (PAD, rows), 1)
    marks = jnp.zeros((PAD, rows), jnp.int32)
    for k in range(pos_ref.shape[0]):
        marks = jnp.where(lane == 2 * k, pos_ref[k, 0], marks)
        marks = jnp.where(lane == 2 * k + 1, pos_ref[k, 1], marks)
    marks = marks.astype(jnp.float32).astype(jnp.bfloat16)
    for i in range(devices):
        out_ref[i, :rows, :] = cross_ref[:, i * rows : (i + 1) * rows].T
        out_ref[i, rows:, :] = marks


def flip(positions, cross):
    rows, width = cross.shape
    return pl.pallas_call(
        flip_kernel,
        out_shape=jax.ShapeDtypeStruct((width // rows, rows + PAD, rows), jnp.bfloat16),
        in_specs=[SCALAR, WHOLE],
        out_specs=WHOLE,
        compiler_params=pltpu.CompilerParams(vmem_limit_bytes=6 * 1024 * 1024),
        cost_estimate=pl.CostEstimate(flops=0, bytes_accessed=rows, transcendentals=0),
    )(positions, cross)


def read_marks(marks_in, first, marks_ref, pos_ref, pos_sem):
    devices, _, lanes = marks_in.shape
    for i in range(devices):
        row = marks_in[i, first : first + PAD, :].astype(jnp.float32).astype(jnp.int32)
        marks_ref[i, :, :lanes] = row[:8]
    fetch = pltpu.make_async_copy(marks_ref, pos_ref, pos_sem)
    fetch.start()
    return fetch


def each_tile(line, place_ref, near_ref, far_ref, pos_ref, add):
    spot, core = place_ref[0], place_ref[1]
    count = line * SIDES
    per_shard = near_ref.shape[0] // (count * TILE)

    @pl.loop(0, count)
    def _(s):
        step = (s + 1) // 2
        at = lax.rem(spot + jnp.where(s == 2 * step, step, count - step), count)
        chip = jnp.where(at < line, at * SIDES, (2 * line - 1 - at) * SIDES + 1)
        for turn, ref in enumerate((near_ref, far_ref)):
            source = chip * CORES + (core if turn == 0 else 1 - core)
            for t in range(per_shard):
                start = pl.multiple_of((s * per_shard + t) * TILE, TILE)
                tile = ref[pl.ds(start, TILE), :]
                add(tile, pos_ref[source, 0, 2 * t], pos_ref[source, 0, 2 * t + 1])


def mark_scratch(devices):
    return [
        pltpu.VMEM((devices, 8, TILE), jnp.int32),
        pltpu.SMEM((devices, 8, TILE), jnp.int32),
        pltpu.SemaphoreType.DMA,
    ]


def update_kernel(
    line,
    first,
    place_ref,
    near_ref,
    far_ref,
    marks_in,
    diag_ref,
    cross_ref,
    cols_ref,
    next_ref,
    out_ref,
    sep_ref,
    sum_ref,
    marks_ref,
    pos_ref,
    pos_sem,
):
    fetch = read_marks(marks_in, first, marks_ref, pos_ref, pos_sem)
    rows, width = diag_ref.shape
    count = width // TILE
    for j in range(count):
        lanes = slice(j * TILE, (j + 1) * TILE)
        sep_ref[j, :rows, :] = diag_ref[:, lanes]
        sep_ref[j, rows:, :] = cols_ref[j, :rows, :]
        sep_ref[count + j, :rows, :] = cross_ref[:, lanes]
        sep_ref[count + j, rows:, :] = next_ref[:, lanes]
    sum_ref[...] = jnp.zeros_like(sum_ref)
    fetch.wait()

    def add(tile, i, j):
        sum_ref[i] += contract_last(sep_ref[j], tile)

    each_tile(line, place_ref, near_ref, far_ref, pos_ref, add)
    for i in range(count):
        out_ref[:, i * TILE : (i + 1) * TILE] = sum_ref[i].astype(jnp.bfloat16)


def update(line, first, place, near, far, marks, diag, cross, cols, following):
    rows, width = diag.shape
    count = width // TILE
    return pl.pallas_call(
        functools.partial(update_kernel, line, first),
        out_shape=jax.ShapeDtypeStruct((2 * rows, width), jnp.bfloat16),
        in_specs=[SCALAR] + [WHOLE] * 7,
        out_specs=WHOLE,
        scratch_shapes=[
            pltpu.VMEM((2 * count, 2 * rows, TILE), jnp.bfloat16),
            pltpu.VMEM((count, 2 * rows, TILE), jnp.float32),
        ]
        + mark_scratch(marks.shape[0]),
        compiler_params=pltpu.CompilerParams(vmem_limit_bytes=12 * 1024 * 1024),
        cost_estimate=pl.CostEstimate(flops=0, bytes_accessed=rows, transcendentals=0),
    )(place, near, far, marks, diag, cross, cols, following)


def factor_kernel(
    line,
    first,
    place_ref,
    near_ref,
    far_ref,
    marks_in,
    wrows_ref,
    out_ref,
    wtile_ref,
    sum_ref,
    marks_ref,
    pos_ref,
    pos_sem,
):
    fetch = read_marks(marks_in, first, marks_ref, pos_ref, pos_sem)
    count = wrows_ref.shape[1] // TILE
    for j in range(count):
        wtile_ref[j] = wrows_ref[:, j * TILE : (j + 1) * TILE]
    sum_ref[...] = jnp.zeros_like(sum_ref)
    fetch.wait()

    def add(tile, i, j):
        sum_ref[j] += jnp.dot(wtile_ref[i], tile, preferred_element_type=jnp.float32)

    each_tile(line, place_ref, near_ref, far_ref, pos_ref, add)
    for j in range(2 * count):
        out_ref[:, j * TILE : (j + 1) * TILE] = sum_ref[j].astype(jnp.bfloat16)


def factor_rows(line, first, place, near, far, marks, wrows):
    rows, width = wrows.shape
    count = width // TILE
    return pl.pallas_call(
        functools.partial(factor_kernel, line, first),
        out_shape=jax.ShapeDtypeStruct((rows, 2 * width), jnp.bfloat16),
        in_specs=[SCALAR] + [WHOLE] * 4,
        out_specs=WHOLE,
        scratch_shapes=[
            pltpu.VMEM((count, rows, TILE), jnp.bfloat16),
            pltpu.VMEM((2 * count, rows, TILE), jnp.float32),
        ]
        + mark_scratch(marks.shape[0]),
        compiler_params=pltpu.CompilerParams(vmem_limit_bytes=8 * 1024 * 1024),
        cost_estimate=pl.CostEstimate(flops=0, bytes_accessed=rows, transcendentals=0),
    )(place, near, far, marks, wrows)


def products_kernel(many, *refs):
    lefts, (near_ref, far_ref), outs = refs[:many], refs[many : many + 2], refs[many + 2 : -1]
    all_ref = refs[-1]
    size = near_ref.shape[0]
    rows = lefts[0].shape[0]
    for k, left_ref in enumerate(lefts):
        all_ref[k * rows : (k + 1) * rows, :] = left_ref[...]
    for at, ref in ((0, near_ref), (size, far_ref)):
        value = (-contract_last(all_ref[...], ref[...])).astype(jnp.bfloat16)
        for k, out_ref in enumerate(outs):
            out_ref[:, at : at + size] = value[k * rows : (k + 1) * rows, :]


def products(lefts, near, far):
    size = 2 * near.shape[0]
    rows, width = lefts[0].shape
    return pl.pallas_call(
        functools.partial(products_kernel, len(lefts)),
        out_shape=(jax.ShapeDtypeStruct((rows, size), jnp.bfloat16),) * len(lefts),
        in_specs=[WHOLE] * (len(lefts) + 2),
        out_specs=(WHOLE,) * len(lefts),
        scratch_shapes=[pltpu.VMEM((len(lefts) * rows, width), jnp.bfloat16)],
        compiler_params=pltpu.CompilerParams(vmem_limit_bytes=12 * 1024 * 1024),
        cost_estimate=pl.CostEstimate(flops=0, bytes_accessed=size, transcendentals=0),
    )(*lefts, near, far)


def finish_kernel(line, place_ref, *refs):
    blocks = refs[: line * SIDES]
    factor_ref, wtile_ref, sigma_ref, tiles_ref = refs[line * SIDES :]
    rows = factor_ref.shape[0]
    width = sigma_ref.shape[1] // 2
    spot, core = place_ref[0], place_ref[1]
    total = wtile_ref[...].astype(jnp.float32)
    for d, ref in enumerate(blocks):
        at = lax.rem(spot + d, line * SIDES)
        chip = jnp.where(at < line, at * SIDES, (2 * line - 1 - at) * SIDES + 1)
        for turn in range(CORES):
            owner = core if turn == 0 else 1 - core
            for half in range(2):
                lane = (chip * CORES + owner) * rows + half * width
                lanes = pl.ds(pl.multiple_of(lane, TILE), rows)
                group = turn * 2 + half
                part = ref[:, group * rows : (group + 1) * rows]
                sigma_ref[:, lanes] = part.astype(jnp.float32)
                total -= contract_last(part, factor_ref[:, lanes])
    tiles_ref[...] = total


def finish(place, blocks, factor, wtile):
    rows = factor.shape[0]
    return pl.pallas_call(
        functools.partial(finish_kernel, len(blocks) // SIDES),
        out_shape=(
            jax.ShapeDtypeStruct(factor.shape, jnp.float32),
            jax.ShapeDtypeStruct((rows, TILE), jnp.float32),
        ),
        in_specs=[SCALAR] + [WHOLE] * (len(blocks) + 2),
        out_specs=(WHOLE, WHOLE),
        compiler_params=pltpu.CompilerParams(vmem_limit_bytes=10 * 1024 * 1024),
        cost_estimate=pl.CostEstimate(flops=0, bytes_accessed=rows, transcendentals=0),
    )(place, *blocks, factor, wtile)


def shards(ring, inverse_block, coupling_tiles, tile_pos, sep_diag, sep_cross):
    wrows = inverse_block[0]
    rows, width = wrows.shape
    tiles = coupling_tiles[0]
    per_shard = tiles.shape[0]
    diag = sep_diag[0]
    cross = sep_cross[0]
    index = lax.axis_index("rows")
    core = index % CORES
    chip = index // CORES
    far_side = chip % SIDES == 1
    spot = jnp.where(far_side, ring.count - 1 - chip // SIDES, chip // SIDES)

    place = jnp.stack([spot, core]).astype(jnp.int32)

    size = lax.axis_size("tm")
    steps = ring.count // 2
    plain = tiles.reshape(-1, TILE)
    wahead, wbehind = [wrows, ring.turn(wrows, 1)], [wrows, ring.turn(wrows, -1)]
    following = lax.ppermute(diag, "tm", [(i + 1, i) for i in range(size - 1)])
    flipped = flip(tile_pos[0], cross)
    pieces = [plain]
    ahead = behind = plain
    across = [ring.turn(plain, steps)]
    for step in range(1, steps - 0):
        ahead, behind = ring.turn(ahead, 1), ring.turn(behind, -1)
        beside = []
        if step == 1:
            across, ahead, behind = lax.optimization_barrier((across, ahead, behind))
        if step == 3:
            beside = [wahead[1], wbehind[1], following]
        if step == 1:
            ahead, behind, flipped, place, *beside = lax.optimization_barrier(
                (ahead, behind, flipped, place, *beside)
            )
            cols = lax.all_to_all(flipped, "rows", 0, 0, tiled=True)
        else:
            ahead, behind, *beside = lax.optimization_barrier((ahead, behind, *beside))
        if beside:
            wahead[1], wbehind[1], following = beside
        pieces += [ahead, behind]
    pieces += across[1:] + across[:1]
    for step in range(2, steps):
        wahead.append(ring.turn(wahead[-1], 1))
        wbehind.append(ring.turn(wbehind[-1], -1))
    near = jnp.concatenate(pieces, axis=0)
    if False:
        near, wahead[2], wbehind[2] = lax.optimization_barrier((near, wahead[2], wbehind[2]))
    far = ring.to_core(near)

    first, marks = rows, cols
    if rows < TILE:
        first, marks = 0, cols[:, rows:, :]
        cols = cols[:, :rows, :].reshape(width // TILE, TILE // rows, rows, rows)
        cols = cols.transpose(0, 2, 1, 3).reshape(width // TILE, rows, TILE)
    updated = update(ring.line, first, place, near, far, marks, diag, cross, cols, following)
    if not False:
        updated, wahead[2], wbehind[2] = lax.optimization_barrier(
            (updated, wahead[2], wbehind[2])
        )
    other = ring.to_core(updated)
    factor = factor_rows(ring.line, first, place, near, far, marks, wrows)

    early = min(3, steps)
    lefts = [wrows]
    for step in range(1, early):
        lefts += [wahead[step], wbehind[step]]
    done = products(lefts, updated, other)
    blocks = [done[0]] + [None] * (ring.count - 1)
    for step in range(1, early):
        blocks[step] = ring.turn(done[2 * step - 1], -step)
        blocks[-step] = ring.turn(done[2 * step], step)
        if step == 1:
            blocks[1], blocks[-1], wahead[-1], wbehind[-1] = lax.optimization_barrier(
                (blocks[1], blocks[-1], wahead[-1], wbehind[-1])
            )
    last = ring.opposite(wahead[-1], wbehind[-1])
    for step in range(early, steps):
        pair = products([wahead[step], wbehind[step]], updated, other)
        blocks[step] = ring.turn(pair[0], -step)
        blocks[-step] = ring.turn(pair[1], step)
    blocks[steps] = ring.turn(products([last], updated, other)[0], steps)

    if rows == TILE:
        wtile = lax.dynamic_slice_in_dim(wrows, index * rows, rows, 1)
        sigma, result = finish(place, blocks, factor, wtile)
        return (sigma[None], result[None])
    order = (jnp.asarray(ring.spots, jnp.int32) - spot) % ring.count
    parts = jnp.take(jnp.stack(blocks), order, axis=0)
    parts = parts.reshape(ring.count, rows, CORES, 2, rows)
    parts = jnp.where(core == 0, parts, parts[:, :, ::-1])
    rounded = parts.transpose(1, 3, 0, 2, 4).reshape(rows, 2 * width)
    sigma = rounded.astype(jnp.float32)
    if rows < TILE:
        whole = factor
        for bit in range((TILE // rows).bit_length() - 1):
            pairs = [(i, i ^ 1 << bit) for i in range(lax.axis_size("rows"))]
            partner = lax.ppermute(whole, "rows", pairs)
            whole = jnp.where(
                index >> bit & 1 == 0,
                jnp.concatenate([whole, partner], axis=0),
                jnp.concatenate([partner, whole], axis=0),
            )
        overlap = contract_last(rounded, whole)
        start = index * rows // TILE * TILE
        wtile = lax.dynamic_slice_in_dim(wrows, start, TILE, 1).astype(jnp.float32)
        result_tiles = wtile - overlap
    else:
        many = rows // TILE
        overlap = jnp.einsum(
            "mrk,mck->mrc",
            rounded.reshape(many, TILE, 2 * width),
            factor.reshape(many, TILE, 2 * width),
            preferred_element_type=jnp.float32,
        )
        square = lax.dynamic_slice_in_dim(wrows, index * rows, rows, 1).reshape(
            many, TILE, many, TILE
        )
        wtile = jnp.stack([square[i, :, i, :] for i in range(many)]).astype(jnp.float32)
        result_tiles = (wtile - overlap).reshape(rows, TILE)
    return (sigma[None], result_tiles[None])


def solution(mesh):
    placed = (
        P("tm", "rows", None),
        P("tm", "rows", None, None),
        P("tm", "rows", None),
        P("tm", "rows", None),
        P("tm", "rows", None),
    )
    return jax.shard_map(
        functools.partial(shards, Ring(mesh.shape["rows"])),
        mesh=mesh,
        in_specs=placed,
        out_specs=(P("tm", "rows", None), P("tm", "rows", None)),
        check_vma=False,
    )
```

time: 117 us -> 109 us (0.932)
  waiting for transfers between devices: 40.3 us -> 31.9 us
  starting transfers between devices: 38.1 us -> 44.5 us
  local copies, waits for them, and re-layouts: 14.8 us -> 10.5 us
  other arithmetic: 1.7 us -> 0.12 us
    ppermute x23 -> x22, starting transfers between devices: 31.9 us -> 39.6 us  [turn(): return lax.ppermute(part, 'rows', pairs)]
    ppermute x23 -> x22, waiting for transfers between devices: 38.7 us -> 31.2 us  [turn(): return lax.ppermute(part, 'rows', pairs)]
    pallas_call x3, Pallas kernels: 9.24 us -> 6.29 us  [products(): pl.pallas_call(functools.partial(products_kernel, len(lefts)), out_shape=...]
    pallas_call x2 -> x3, Pallas kernels: 8.63 us -> 10.7 us  [the longest x1 4.93 us: update(): pl.pallas_call(functools.partial(update_kernel, line, first), out_shape=j...]
    unnamed x38 -> x31, local copies, waits for them, and re-layouts: 11.2 us -> 9.66 us
    all_to_all x1, starting transfers between devices: 4.93 us -> 3.6 us  [shards(): cols = lax.all_to_all(flipped, 'rows', 0, 0, tiled=True)]
  transfers between devices with their start and end apart: 27 -> 26, of which waited for: 13 -> 13; matrix products, arithmetic and copies ran while one was open for 8% -> 4% of each run, Pallas kernels for 15% -> 16%
where the time goes in v3:
time: 109 us; the launch traced here: 108 us
  starting transfers between devices  44.5 us (41%)
  waiting for transfers between devices  31.9 us (29%)
  Pallas kernels  20.2 us (19%)
  local copies, waits for them, and re-layouts  10.5 us (10%)
    ppermute x22, starting transfers between devices, turn(): return lax.ppermute(part, 'rows', pairs)  39.6 us
    ppermute x22, waiting for transfers between devices, turn(): return lax.ppermute(part, 'rows', pairs)  31.2 us
    unnamed x31, local copies, waits for them, and re-layouts  9.66 us
    pallas_call x3, Pallas kernels, products(): pl.pallas_call(functools.partial(products_kernel, len(lefts)), out_shape=...  6.29 us
    pallas_call x1, Pallas kernels, update(): pl.pallas_call(functools.partial(update_kernel, line, first), out_shape=j...  4.93 us
    pallas_call x1, Pallas kernels, factor_rows(): pl.pallas_call(functools.partial(factor_kernel, line, first), out_shape=j...  4.21 us
    all_to_all x1, starting transfers between devices, shards(): cols = lax.all_to_all(flipped, 'rows', 0, 0, tiled=True)  3.6 us
    pallas_call x1, Pallas kernels, finish(): pl.pallas_call(functools.partial(finish_kernel, len(blocks) // SIDES), ou...  3.23 us
  transfers between devices with their start and end apart: 26, of which 13 were waited for; matrix products, arithmetic and copies ran while one was open for 4% of the time, Pallas kernels for 16%

profile of v3, /device:TPU:0, one launch (start us, length us, event | category | flops | bytes accessed | tf_op | source)
XLA Modules:
  0.0 108.1 jit_solution(6928547969823765399)
XLA Ops:
  0.6 6.1 %collective-permute-start = (bf16[512,128]{1,0:T(8,128)(2,1)}, bf16[512,128]{1,0:T(8,128)(2,1)S(1)}, u32[]{:S(2)}, u32[]{:S(2)}) collective-permute-start(bf16[512,128]{1,0:T(8,128)(2,1)} %bitcast.19), channel_id=1, source_target_pairs={{0,14},{1,15},{4,10},{5,11},{8,6},{9,7},{12,2},{13,3},{14,0},{15,1... | collective-permute-start | bytes 393224 | tf_op jit(solution)/shard_map/ppermute | solution.py:39
  6.7 2.0 %collective-permute-start.2 = (bf16[512,128]{1,0:T(8,128)(2,1)}, bf16[512,128]{1,0:T(8,128)(2,1)}, u32[]{:S(2)}, u32[]{:S(2)}) collective-permute-start(bf16[512,128]{1,0:T(8,128)(2,1)} %bitcast.21), channel_id=1, source_target_pairs={{0,2},{1,3},{4,0},{5,1},{8,4},{9,5},{12,8},{13,9},{14,12},{15,13},... | collective-permute-start | bytes 393224 | tf_op jit(solution)/shard_map/ppermute | solution.py:39
  8.7 2.0 %collective-permute-start.8 = (bf16[128,2048]{1,0:T(8,128)(2,1)}, bf16[128,2048]{1,0:T(8,128)(2,1)S(1)}, u32[]{:S(2)}, u32[]{:S(2)}) collective-permute-start(bf16[128,2048]{1,0:T(8,128)(2,1)} %bitcast.12), channel_id=1, source_target_pairs={{0,2},{1,3},{4,0},{5,1},{8,4},{9,5},{12,8},{13,9},{14,12},{15,13},... | collective-permute-start | bytes 1572872 | tf_op jit(solution)/shard_map/ppermute | solution.py:39
  10.8 0.9 constant_dynamic-update-slice_fusion.7
  11.7 0.8 copy.7.pos_ref
  12.5 1.0 copy-done.1
  13.5 1.6 %shard_map.68 = bf16[16,144,128]{2,1,0:T(8,128)(2,1)} custom-call(s32[4,2]{1,0:T(4,128)S(1)} %copy.7.pos_ref, bf16[128,2048]{1,0:T(8,128)(2,1)S(1)} %bitcast.15), custom_call_target="tpu_custom_call" | custom-call | bytes 128 | tf_op jit(solution)/shard_map/pallas_call | solution.py:66
  15.1 1.3 %collective-permute-start.9 = (bf16[128,2048]{1,0:T(8,128)(2,1)}, bf16[128,2048]{1,0:T(8,128)(2,1)S(1)}, u32[]{:S(2)}, u32[]{:S(2)}) collective-permute-start(bf16[128,2048]{1,0:T(8,128)(2,1)} %bitcast.17), channel_id=1, source_target_pairs={{16,0},{17,1},{18,2},{19,3},{20,4},{21,5},{22,6},{23,7},{24,8},{25... | collective-permute-start | bytes 1572872 | tf_op jit(solution)/shard_map/ppermute | solution.py:299
  16.7 1.8 %collective-permute-start.4 = (bf16[512,128]{1,0:T(8,128)(2,1)}, bf16[512,128]{1,0:T(8,128)(2,1)}, u32[]{:S(2)}, u32[]{:S(2)}) collective-permute-start(bf16[512,128]{1,0:T(8,128)(2,1)} %collective-permute-done.2), channel_id=1, source_target_pairs={{0,2},{1,3},{4,0},{5,1},{8,4},{9,5},{12,8},{13,9},{14,12},{15,13},... | collective-permute-start | bytes 393224 | tf_op jit(solution)/shard_map/ppermute | solution.py:39
  18.5 3.6 %all-to-all-start = ((bf16[16,144,128]{2,1,0:T(8,128)(2,1)}), bf16[16,144,128]{2,1,0:T(8,128)(2,1)S(1)}, u32[]{:S(2)}, u32[]{:S(2)}) async-start(bf16[16,144,128]{2,1,0:T(8,128)(2,1)} %shard_map.68), calls=%async_computation | async-start | bytes 1179648 | tf_op jit(solution)/shard_map/all_to_all | solution.py:315
  22.1 0.9 constant_dynamic-update-slice_fusion.5
  23.1 5.4 %collective-permute-done.3 = bf16[512,128]{1,0:T(8,128)(2,1)} collective-permute-done((bf16[512,128]{1,0:T(8,128)(2,1)S(1)}, bf16[512,128]{1,0:T(8,128)(2,1)}, u32[]{:S(2)}, u32[]{:S(2)}) %collective-permute-start.3) | collective-permute-done | bytes 131104 | tf_op jit(solution)/shard_map/ppermute | solution.py:39
  28.4 1.1 %collective-permute-done.4 = bf16[512,128]{1,0:T(8,128)(2,1)} collective-permute-done((bf16[512,128]{1,0:T(8,128)(2,1)}, bf16[512,128]{1,0:T(8,128)(2,1)}, u32[]{:S(2)}, u32[]{:S(2)}) %collective-permute-start.4) | collective-permute-done | bytes 131104 | tf_op jit(solution)/shard_map/ppermute | solution.py:39
  29.6 7.5 %collective-permute-start.5 = (bf16[512,128]{1,0:T(8,128)(2,1)}, bf16[512,128]{1,0:T(8,128)(2,1)S(1)}, u32[]{:S(2)}, u32[]{:S(2)}) collective-permute-start(bf16[512,128]{1,0:T(8,128)(2,1)} %collective-permute-done.3), channel_id=1, source_target_pairs={{0,4},{1,5},{4,8},{5,9},{8,12},{9,13},{12,14},{13,15},{14,10},{15,... | collective-permute-start | bytes 393224 | tf_op jit(solution)/shard_map/ppermute | solution.py:39
  37.1 1.0 constant_dynamic-update-slice_fusion.4
  38.1 0.9 constant_dynamic-update-slice_fusion.3
  39.0 1.0 collective-permute-done.5
  39.9 2.5 %collective-permute-done.6 = bf16[512,128]{1,0:T(8,128)(2,1)S(1)} collective-permute-done((bf16[512,128]{1,0:T(8,128)(2,1)}, bf16[512,128]{1,0:T(8,128)(2,1)S(1)}, u32[]{:S(2)}, u32[]{:S(2)}) %collective-permute-start.6) | collective-permute-done | bytes 131104 | tf_op jit(solution)/shard_map/ppermute | solution.py:39
  42.5 0.8 copy-done.8
  43.7 2.8 %collective-permute-start.11 = (bf16[128,2048]{1,0:T(8,128)(2,1)}, bf16[128,2048]{1,0:T(8,128)(2,1)}, u32[]{:S(2)}, u32[]{:S(2)}) collective-permute-start(bf16[128,2048]{1,0:T(8,128)(2,1)} %copy-done.4), channel_id=1, source_target_pairs={{0,4},{1,5},{4,8},{5,9},{8,12},{9,13},{12,14},{13,15},{14,10},{15,... | collective-permute-start | bytes 1572872 | tf_op jit(solution)/shard_map/ppermute | solution.py:39
  46.6 1.0 copy-done.2
  47.6 1.0 copy-done.3
  48.6 1.0 copy-done.9
  49.7 4.9 %shard_map.69.refs_5_.refs_2_.refs_1_ = bf16[256,2048]{1,0:T(8,128)(2,1)S(1)} custom-call(s32[2]{0:T(128)S(1)} %pad_add_fusion.place_ref, bf16[4096,128]{1,0:T(8,128)(2,1)S(1)} %constant_dynamic-update-slice_fusion.near_ref, bf16[4096,128]{1,0:T(8,128)(2,1)S(1)} %collective-permute-done.10.far_ref, bf16[16,144,128]{2,1,0:T(8,128)(2,1)S(1)} %all-to-all-done.marks_in.cols_ref, ...), custom_call_target="tpu_custom_call" | custom-call | bytes 128 | tf_op jit(solution)/shard_map/pallas_call | solution.py:153
  54.6 4.0 %collective-permute-done.11.refs_3_ = bf16[128,2048]{1,0:T(8,128)(2,1)} collective-permute-done((bf16[128,2048]{1,0:T(8,128)(2,1)}, bf16[128,2048]{1,0:T(8,128)(2,1)}, u32[]{:S(2)}, u32[]{:S(2)}) %collective-permute-start.11) | collective-permute-done | bytes 524320 | tf_op jit(solution)/shard_map/ppermute | solution.py:39
  58.7 2.2 %collective-permute-done.12.refs_4_ = bf16[128,2048]{1,0:T(8,128)(2,1)} collective-permute-done((bf16[128,2048]{1,0:T(8,128)(2,1)}, bf16[128,2048]{1,0:T(8,128)(2,1)}, u32[]{:S(2)}, u32[]{:S(2)}) %collective-permute-start.12) | collective-permute-done | bytes 524320 | tf_op jit(solution)/shard_map/ppermute | solution.py:39
  60.9 1.6 %collective-permute-start.16 = (bf16[128,2048]{1,0:T(8,128)(2,1)}, bf16[128,2048]{1,0:T(8,128)(2,1)S(1)}, u32[]{:S(2)}, u32[]{:S(2)}) collective-permute-start(bf16[128,2048]{1,0:T(8,128)(2,1)} %collective-permute-done.11.refs_3_), channel_id=1, source_target_pairs={{0,4},{1,5},{4,8},{5,9},{8,12},{9,13},{12,14},{13,15},{14,10},{15,... | collective-permute-start | bytes 1572872 | tf_op jit(solution)/shard_map/ppermute | solution.py:39
  62.4 0.4 collective-permute-start.17
  62.9 0.6 collective-permute-done.13.refs_6_.refs_3_.refs_2_
  63.5 3.4 %shard_map.70 = (bf16[128,512]{1,0:T(8,128)(2,1)S(1)}, bf16[128,512]{1,0:T(8,128)(2,1)S(1)}, bf16[128,512]{1,0:T(8,128)(2,1)S(1)}, bf16[128,512]{1,0:T(8,128)(2,1)}, bf16[128,512]{1,0:T(8,128)(2,1)}) custom-call(bf16[128,2048]{1,0:T(8,128)(2,1)S(1)} %bitcast.13, bf16[128,2048]{1,0:T(8,128)(2,1)S(1)} %copy-done.5, bf16[128,2048]{1,0:T(8,128)(2,1)S(1)} %copy-done.7, ...), custom_call_target="tpu_custom_call" | custom-call | bytes 512 | tf_op jit(solution)/shard_map/pallas_call | solution.py:232
  66.9 0.3 collective-permute-start.14
  67.2 1.7 %collective-permute-start.15 = (bf16[128,512]{1,0:T(8,128)(2,1)S(1)}, bf16[128,512]{1,0:T(8,128)(2,1)S(1)}, u32[]{:S(2)}, u32[]{:S(2)}) collective-permute-start(bf16[128,512]{1,0:T(8,128)(2,1)S(1)} %get-tuple-element.51), channel_id=1, source_target_pairs={{0,4},{1,5},{4,8},{5,9},{8,12},{9,13},{12,14},{13,15},{14,10},{15,... | collective-permute-start | bytes 393224 | tf_op jit(solution)/shard_map/ppermute | solution.py:39
  69.0 6.8 %collective-permute-done.16.refs_0_ = bf16[128,2048]{1,0:T(8,128)(2,1)S(1)} collective-permute-done((bf16[128,2048]{1,0:T(8,128)(2,1)}, bf16[128,2048]{1,0:T(8,128)(2,1)S(1)}, u32[]{:S(2)}, u32[]{:S(2)}) %collective-permute-start.16) | collective-permute-done | bytes 524320 | tf_op jit(solution)/shard_map/ppermute | solution.py:39
  75.8 1.6 %collective-permute-done.17.refs_1_ = bf16[128,2048]{1,0:T(8,128)(2,1)S(1)} collective-permute-done((bf16[128,2048]{1,0:T(8,128)(2,1)}, bf16[128,2048]{1,0:T(8,128)(2,1)S(1)}, u32[]{:S(2)}, u32[]{:S(2)}) %collective-permute-start.17) | collective-permute-done | bytes 524320 | tf_op jit(solution)/shard_map/ppermute | solution.py:39
  77.4 2.1 %collective-permute-done.14.refs_1_ = bf16[128,512]{1,0:T(8,128)(2,1)S(1)} collective-permute-done((bf16[128,512]{1,0:T(8,128)(2,1)S(1)}, bf16[128,512]{1,0:T(8,128)(2,1)S(1)}, u32[]{:S(2)}, u32[]{:S(2)}) %collective-permute-start.14) | collective-permute-done | bytes 131104 | tf_op jit(solution)/shard_map/ppermute | solution.py:39
  79.5 0.7 copy-done.10
  80.2 0.3 collective-permute-start.20
  80.6 1.8 %collective-permute-start.21 = (bf16[64,2048]{1,0:T(8,128)(2,1)S(1)}, bf16[64,2048]{1,0:T(8,128)(2,1)S(1)}, u32[]{:S(2)}, u32[]{:S(2)}) collective-permute-start(bf16[64,2048]{1,0:T(8,128)(2,1)S(1)} %slice.7), channel_id=1, source_target_pairs={{0,2},{1,3},{4,0},{5,1},{8,4},{9,5},{12,8},{13,9},{14,12},{15,13},... | collective-permute-start | bytes 786440 | tf_op jit(solution)/shard_map/ppermute | solution.py:39
  82.5 2.8 %collective-permute-start.24 = (bf16[128,512]{1,0:T(8,128)(2,1)}, bf16[128,512]{1,0:T(8,128)(2,1)}, u32[]{:S(2)}, u32[]{:S(2)}) collective-permute-start(bf16[128,512]{1,0:T(8,128)(2,1)} %get-tuple-element.58), channel_id=1, source_target_pairs={{0,8},{1,9},{4,12},{5,13},{8,14},{9,15},{12,10},{13,11},{14,6},{15... | collective-permute-start | bytes 393224 | tf_op jit(solution)/shard_map/ppermute | solution.py:39
  85.3 1.4 %shard_map.71 = (bf16[128,512]{1,0:T(8,128)(2,1)}, bf16[128,512]{1,0:T(8,128)(2,1)}) custom-call(bf16[128,2048]{1,0:T(8,128)(2,1)S(1)} %collective-permute-done.16.refs_0_, bf16[128,2048]{1,0:T(8,128)(2,1)S(1)} %collective-permute-done.17.refs_1_, bf16[256,2048]{1,0:T(8,128)(2,1)S(1)} %shard_map.69.refs_5_.refs_2_.refs_1_, ...), custom_call_target="tpu_custom_call" | custom-call | bytes 512 | tf_op jit(solution)/shard_map/pallas_call | solution.py:232
  86.8 1.6 %collective-permute-done.20 = bf16[64,2048]{1,0:T(8,128)(2,1)S(1)} collective-permute-done((bf16[64,2048]{1,0:T(8,128)(2,1)S(1)}, bf16[64,2048]{1,0:T(8,128)(2,1)S(1)}, u32[]{:S(2)}, u32[]{:S(2)}) %collective-permute-start.20) | collective-permute-done | bytes 262176 | tf_op jit(solution)/shard_map/ppermute | solution.py:39
  88.4 6.3 %collective-permute-start.23 = (bf16[128,512]{1,0:T(8,128)(2,1)}, bf16[128,512]{1,0:T(8,128)(2,1)}, u32[]{:S(2)}, u32[]{:S(2)}) collective-permute-start(bf16[128,512]{1,0:T(8,128)(2,1)} %get-tuple-element.57), channel_id=1, source_target_pairs={{0,12},{1,13},{4,14},{5,15},{8,10},{9,11},{12,6},{13,7},{14,2},{15... | collective-permute-start | bytes 393224 | tf_op jit(solution)/shard_map/ppermute | solution.py:39
  94.7 1.5 %shard_map.72 = bf16[128,512]{1,0:T(8,128)(2,1)} custom-call(bf16[128,2048]{1,0:T(8,128)(2,1)S(1)} %pad_maximum_fusion.refs_0_, bf16[256,2048]{1,0:T(8,128)(2,1)S(1)} %shard_map.69.refs_5_.refs_2_.refs_1_, bf16[256,2048]{1,0:T(8,128)(2,1)S(1)} %collective-permute-done.13.refs_6_.refs_3_.refs_2_), custom_call_target="tpu_custom_call" | custom-call | bytes 512 | tf_op jit(solution)/shard_map/pallas_call | solution.py:232
  96.2 1.5 %collective-permute-start.22 = (bf16[128,512]{1,0:T(8,128)(2,1)}, bf16[128,512]{1,0:T(8,128)(2,1)}, u32[]{:S(2)}, u32[]{:S(2)}) collective-permute-start(bf16[128,512]{1,0:T(8,128)(2,1)} %shard_map.72), channel_id=1, source_target_pairs={{0,14},{1,15},{4,10},{5,11},{8,6},{9,7},{12,2},{13,3},{14,0},{15,1... | collective-permute-start | bytes 393224 | tf_op jit(solution)/shard_map/ppermute | solution.py:39
  97.7 4.2 %shard_map.73.refs_8_ = bf16[128,4096]{1,0:T(8,128)(2,1)S(1)} custom-call(s32[2]{0:T(128)S(1)} %pad_add_fusion.place_ref, bf16[4096,128]{1,0:T(8,128)(2,1)S(1)} %constant_dynamic-update-slice_fusion.near_ref, bf16[4096,128]{1,0:T(8,128)(2,1)S(1)} %collective-permute-done.10.far_ref, bf16[16,144,128]{2,1,0:T(8,128)(2,1)S(1)} %all-to-all-done.marks_in.cols_ref, ...), custom_call_target="tpu_custom_call" | custom-call | bytes 128 | tf_op jit(solution)/shard_map/pallas_call | solution.py:201
  101.9 2.0 %collective-permute-done.18.refs_2_ = bf16[128,512]{1,0:T(8,128)(2,1)} collective-permute-done((bf16[128,512]{1,0:T(8,128)(2,1)}, bf16[128,512]{1,0:T(8,128)(2,1)}, u32[]{:S(2)}, u32[]{:S(2)}) %collective-permute-start.18) | collective-permute-done | bytes 131104 | tf_op jit(solution)/shard_map/ppermute | solution.py:39
  103.9 0.9 collective-permute-done.23.refs_5_
  104.9 3.2 %shard_map.74 = (f32[128,4096]{1,0:T(8,128)}, f32[128,128]{1,0:T(8,128)}) custom-call(s32[2]{0:T(128)S(1)} %pad_add_fusion.place_ref, bf16[128,512]{1,0:T(8,128)(2,1)S(1)} %get-tuple-element.49.refs_0_, bf16[128,512]{1,0:T(8,128)(2,1)S(1)} %collective-permute-done.14.refs_1_, bf16[128,512]{1,0:T(8,128)(2,1)} %collective-permute-done.18.refs_2_, ...), custom_call_target="tpu_custom_call" | custom-call | bytes 128 | tf_op jit(solution)/shard_map/pallas_call | solution.py:267
  (49 shorter events, 1.2 us)
Async XLA Ops:
  0.6 14.5 %collective-permute-start = (bf16[512,128]{1,0:T(8,128)(2,1)}, bf16[512,128]{1,0:T(8,128)(2,1)S(1)}, u32[]{:S(2)}, u32[]{:S(2)}) collective-permute-start(bf16[512,128]{1,0:T(8,128)(2,1)} %bitcast.19), channel_id=1, source_target_pairs={{0,14},{1,15},{4,10},{5,11},{8,6},{9,7},{12,2},{13,3},{14,0},{15,1... | collective-permute-start | bytes 393224 | tf_op jit(solution)/shard_map/ppermute | solution.py:39
  6.7 9.8 %collective-permute-start.1 = (bf16[512,128]{1,0:T(8,128)(2,1)}, bf16[512,128]{1,0:T(8,128)(2,1)S(1)}, u32[]{:S(2)}, u32[]{:S(2)}) collective-permute-start(bf16[512,128]{1,0:T(8,128)(2,1)} %bitcast.20), channel_id=1, source_target_pairs={{0,4},{1,5},{4,8},{5,9},{8,12},{9,13},{12,14},{13,15},{14,10},{15,... | collective-permute-start | bytes 393224 | tf_op jit(solution)/shard_map/ppermute | solution.py:39
  6.7 9.8 %collective-permute-start.2 = (bf16[512,128]{1,0:T(8,128)(2,1)}, bf16[512,128]{1,0:T(8,128)(2,1)}, u32[]{:S(2)}, u32[]{:S(2)}) collective-permute-start(bf16[512,128]{1,0:T(8,128)(2,1)} %bitcast.21), channel_id=1, source_target_pairs={{0,2},{1,3},{4,0},{5,1},{8,4},{9,5},{12,8},{13,9},{14,12},{15,13},... | collective-permute-start | bytes 393224 | tf_op jit(solution)/shard_map/ppermute | solution.py:39
  8.7 33.7 %collective-permute-start.7 = (bf16[128,2048]{1,0:T(8,128)(2,1)}, bf16[128,2048]{1,0:T(8,128)(2,1)S(1)}, u32[]{:S(2)}, u32[]{:S(2)}) collective-permute-start(bf16[128,2048]{1,0:T(8,128)(2,1)} %bitcast.11), channel_id=1, source_target_pairs={{0,4},{1,5},{4,8},{5,9},{8,12},{9,13},{12,14},{13,15},{14,10},{15,... | collective-permute-start | bytes 1572872 | tf_op jit(solution)/shard_map/ppermute | solution.py:39
  8.7 33.7 %collective-permute-start.8 = (bf16[128,2048]{1,0:T(8,128)(2,1)}, bf16[128,2048]{1,0:T(8,128)(2,1)S(1)}, u32[]{:S(2)}, u32[]{:S(2)}) collective-permute-start(bf16[128,2048]{1,0:T(8,128)(2,1)} %bitcast.12), channel_id=1, source_target_pairs={{0,2},{1,3},{4,0},{5,1},{8,4},{9,5},{12,8},{13,9},{14,12},{15,13},... | collective-permute-start | bytes 1572872 | tf_op jit(solution)/shard_map/ppermute | solution.py:39
  12.5 1.0 copy-start.1
  15.1 27.4 %collective-permute-start.9 = (bf16[128,2048]{1,0:T(8,128)(2,1)}, bf16[128,2048]{1,0:T(8,128)(2,1)S(1)}, u32[]{:S(2)}, u32[]{:S(2)}) collective-permute-start(bf16[128,2048]{1,0:T(8,128)(2,1)} %bitcast.17), channel_id=1, source_target_pairs={{16,0},{17,1},{18,2},{19,3},{20,4},{21,5},{22,6},{23,7},{24,8},{25... | collective-permute-start | bytes 1572872 | tf_op jit(solution)/shard_map/ppermute | solution.py:299
  16.5 12.0 %collective-permute-start.3 = (bf16[512,128]{1,0:T(8,128)(2,1)S(1)}, bf16[512,128]{1,0:T(8,128)(2,1)}, u32[]{:S(2)}, u32[]{:S(2)}) collective-permute-start(bf16[512,128]{1,0:T(8,128)(2,1)S(1)} %collective-permute-done.1), channel_id=1, source_target_pairs={{0,4},{1,5},{4,8},{5,9},{8,12},{9,13},{12,14},{13,15},{14,10},{15,... | collective-permute-start | bytes 393224 | tf_op jit(solution)/shard_map/ppermute | solution.py:39
  16.7 12.8 %collective-permute-start.4 = (bf16[512,128]{1,0:T(8,128)(2,1)}, bf16[512,128]{1,0:T(8,128)(2,1)}, u32[]{:S(2)}, u32[]{:S(2)}) collective-permute-start(bf16[512,128]{1,0:T(8,128)(2,1)} %collective-permute-done.2), channel_id=1, source_target_pairs={{0,2},{1,3},{4,0},{5,1},{8,4},{9,5},{12,8},{13,9},{14,12},{15,13},... | collective-permute-start | bytes 393224 | tf_op jit(solution)/shard_map/ppermute | solution.py:39
  18.5 28.0 %all-to-all-start = ((bf16[16,144,128]{2,1,0:T(8,128)(2,1)}), bf16[16,144,128]{2,1,0:T(8,128)(2,1)S(1)}, u32[]{:S(2)}, u32[]{:S(2)}) async-start(bf16[16,144,128]{2,1,0:T(8,128)(2,1)} %shard_map.68), calls=%async_computation | async-start | bytes 1179648 | tf_op jit(solution)/shard_map/all_to_all | solution.py:315
  29.6 10.4 %collective-permute-start.5 = (bf16[512,128]{1,0:T(8,128)(2,1)}, bf16[512,128]{1,0:T(8,128)(2,1)S(1)}, u32[]{:S(2)}, u32[]{:S(2)}) collective-permute-start(bf16[512,128]{1,0:T(8,128)(2,1)} %collective-permute-done.3), channel_id=1, source_target_pairs={{0,4},{1,5},{4,8},{5,9},{8,12},{9,13},{12,14},{13,15},{14,10},{15,... | collective-permute-start | bytes 393224 | tf_op jit(solution)/shard_map/ppermute | solution.py:39
  37.1 5.3 %collective-permute-start.6 = (bf16[512,128]{1,0:T(8,128)(2,1)}, bf16[512,128]{1,0:T(8,128)(2,1)S(1)}, u32[]{:S(2)}, u32[]{:S(2)}) collective-permute-start(bf16[512,128]{1,0:T(8,128)(2,1)} %collective-permute-done.4), channel_id=1, source_target_pairs={{0,2},{1,3},{4,0},{5,1},{8,4},{9,5},{12,8},{13,9},{14,12},{15,13},... | collective-permute-start | bytes 393224 | tf_op jit(solution)/shard_map/ppermute | solution.py:39
  42.4 1.0 copy-start.4
  42.4 1.1 %copy-start.6 = (bf16[128,2048]{1,0:T(8,128)(2,1)}, bf16[128,2048]{1,0:T(8,128)(2,1)S(1)}, u32[]{:S(2)}) copy-start(bf16[128,2048]{1,0:T(8,128)(2,1)S(1)} %collective-permute-done.8.refs_2_) | copy-start | bytes 1572868
  42.5 0.9 copy-start.8
  43.6 19.9 %copy-start = (bf16[1,128,2048]{2,1,0:T(8,128)(2,1)S(1)}, bf16[1,128,2048]{2,1,0:T(8,128)(2,1)}, u32[]{:S(2)}) copy-start(bf16[1,128,2048]{2,1,0:T(8,128)(2,1)} %param.5) | copy-start | bytes 1572868
  43.6 2.9 %collective-permute-start.10 = (bf16[4096,128]{1,0:T(8,128)(2,1)S(1)}, bf16[4096,128]{1,0:T(8,128)(2,1)S(1)}, u32[]{:S(2)}, u32[]{:S(2)}) collective-permute-start(bf16[4096,128]{1,0:T(8,128)(2,1)S(1)} %constant_dynamic-update-slice_fusion.near_ref), channel_id=1, source_target_pairs={{0,1},{1,0},{2,3},{3,2},{4,5},{5,4},{6,7},{7,6},{8,9},{9,8},{10,11... | collective-permute-start | bytes 3145736 | tf_op jit(solution)/shard_map/ppermute | solution.py:43
  43.7 15.0 %collective-permute-start.11 = (bf16[128,2048]{1,0:T(8,128)(2,1)}, bf16[128,2048]{1,0:T(8,128)(2,1)}, u32[]{:S(2)}, u32[]{:S(2)}) collective-permute-start(bf16[128,2048]{1,0:T(8,128)(2,1)} %copy-done.4), channel_id=1, source_target_pairs={{0,4},{1,5},{4,8},{5,9},{8,12},{9,13},{12,14},{13,15},{14,10},{15,... | collective-permute-start | bytes 1572872 | tf_op jit(solution)/shard_map/ppermute | solution.py:39
  46.5 14.3 %collective-permute-start.12 = (bf16[128,2048]{1,0:T(8,128)(2,1)}, bf16[128,2048]{1,0:T(8,128)(2,1)}, u32[]{:S(2)}, u32[]{:S(2)}) collective-permute-start(bf16[128,2048]{1,0:T(8,128)(2,1)} %copy-done.6), channel_id=1, source_target_pairs={{0,2},{1,3},{4,0},{5,1},{8,4},{9,5},{12,8},{13,9},{14,12},{15,13},... | collective-permute-start | bytes 1572872 | tf_op jit(solution)/shard_map/ppermute | solution.py:39
  46.6 1.0 copy-start.2
  47.6 1.0 copy-start.3
  48.6 1.0 copy-start.9
  49.7 13.8 %copy-start.5 = (bf16[128,2048]{1,0:T(8,128)(2,1)S(1)}, bf16[128,2048]{1,0:T(8,128)(2,1)}, u32[]{:S(2)}) copy-start(bf16[128,2048]{1,0:T(8,128)(2,1)} %copy-done.4) | copy-start | bytes 1572868
  49.7 13.8 %copy-start.7 = (bf16[128,2048]{1,0:T(8,128)(2,1)S(1)}, bf16[128,2048]{1,0:T(8,128)(2,1)}, u32[]{:S(2)}) copy-start(bf16[128,2048]{1,0:T(8,128)(2,1)} %copy-done.6) | copy-start | bytes 1572868
  60.9 2.7 %collective-permute-start.13 = (bf16[256,2048]{1,0:T(8,128)(2,1)S(1)}, bf16[256,2048]{1,0:T(8,128)(2,1)S(1)}, u32[]{:S(2)}, u32[]{:S(2)}) collective-permute-start(bf16[256,2048]{1,0:T(8,128)(2,1)S(1)} %shard_map.69.refs_5_.refs_2_.refs_1_), channel_id=1, source_target_pairs={{0,1},{1,0},{2,3},{3,2},{4,5},{5,4},{6,7},{7,6},{8,9},{9,8},{10,11... | collective-permute-start | bytes 3145736 | tf_op jit(solution)/shard_map/ppermute | solution.py:43
  60.9 14.9 %collective-permute-start.16 = (bf16[128,2048]{1,0:T(8,128)(2,1)}, bf16[128,2048]{1,0:T(8,128)(2,1)S(1)}, u32[]{:S(2)}, u32[]{:S(2)}) collective-permute-start(bf16[128,2048]{1,0:T(8,128)(2,1)} %collective-permute-done.11.refs_3_), channel_id=1, source_target_pairs={{0,4},{1,5},{4,8},{5,9},{8,12},{9,13},{12,14},{13,15},{14,10},{15,... | collective-permute-start | bytes 1572872 | tf_op jit(solution)/shard_map/ppermute | solution.py:39
  62.4 15.0 %collective-permute-start.17 = (bf16[128,2048]{1,0:T(8,128)(2,1)}, bf16[128,2048]{1,0:T(8,128)(2,1)S(1)}, u32[]{:S(2)}, u32[]{:S(2)}) collective-permute-start(bf16[128,2048]{1,0:T(8,128)(2,1)} %collective-permute-done.12.refs_4_), channel_id=1, source_target_pairs={{0,2},{1,3},{4,0},{5,1},{8,4},{9,5},{12,8},{13,9},{14,12},{15,13},... | collective-permute-start | bytes 1572872 | tf_op jit(solution)/shard_map/ppermute | solution.py:39
  66.9 12.6 %collective-permute-start.14 = (bf16[128,512]{1,0:T(8,128)(2,1)S(1)}, bf16[128,512]{1,0:T(8,128)(2,1)S(1)}, u32[]{:S(2)}, u32[]{:S(2)}) collective-permute-start(bf16[128,512]{1,0:T(8,128)(2,1)S(1)} %get-tuple-element.50), channel_id=1, source_target_pairs={{0,2},{1,3},{4,0},{5,1},{8,4},{9,5},{12,8},{13,9},{14,12},{15,13},... | collective-permute-start | bytes 393224 | tf_op jit(solution)/shard_map/ppermute | solution.py:39
  67.2 12.3 %collective-permute-start.15 = (bf16[128,512]{1,0:T(8,128)(2,1)S(1)}, bf16[128,512]{1,0:T(8,128)(2,1)S(1)}, u32[]{:S(2)}, u32[]{:S(2)}) collective-permute-start(bf16[128,512]{1,0:T(8,128)(2,1)S(1)} %get-tuple-element.51), channel_id=1, source_target_pairs={{0,4},{1,5},{4,8},{5,9},{8,12},{9,13},{12,14},{13,15},{14,10},{15,... | collective-permute-start | bytes 393224 | tf_op jit(solution)/shard_map/ppermute | solution.py:39
  79.5 0.7 copy-start.10
  80.2 8.2 %collective-permute-start.20 = (bf16[64,2048]{1,0:T(8,128)(2,1)S(1)}, bf16[64,2048]{1,0:T(8,128)(2,1)S(1)}, u32[]{:S(2)}, u32[]{:S(2)}) collective-permute-start(bf16[64,2048]{1,0:T(8,128)(2,1)S(1)} %slice.6), channel_id=1, source_target_pairs={{0,4},{1,5},{4,8},{5,9},{8,12},{9,13},{12,14},{13,15},{14,10},{15,... | collective-permute-start | bytes 786440 | tf_op jit(solution)/shard_map/ppermute | solution.py:39
  80.6 14.1 %collective-permute-start.21 = (bf16[64,2048]{1,0:T(8,128)(2,1)S(1)}, bf16[64,2048]{1,0:T(8,128)(2,1)S(1)}, u32[]{:S(2)}, u32[]{:S(2)}) collective-permute-start(bf16[64,2048]{1,0:T(8,128)(2,1)S(1)} %slice.7), channel_id=1, source_target_pairs={{0,2},{1,3},{4,0},{5,1},{8,4},{9,5},{12,8},{13,9},{14,12},{15,13},... | collective-permute-start | bytes 786440 | tf_op jit(solution)/shard_map/ppermute | solution.py:39
  82.3 21.6 %collective-permute-start.18 = (bf16[128,512]{1,0:T(8,128)(2,1)}, bf16[128,512]{1,0:T(8,128)(2,1)}, u32[]{:S(2)}, u32[]{:S(2)}) collective-permute-start(bf16[128,512]{1,0:T(8,128)(2,1)} %get-tuple-element.53), channel_id=1, source_target_pairs={{0,6},{1,7},{4,2},{5,3},{8,0},{9,1},{12,4},{13,5},{14,8},{15,9},{1... | collective-permute-start | bytes 393224 | tf_op jit(solution)/shard_map/ppermute | solution.py:39
  82.5 21.4 %collective-permute-start.24 = (bf16[128,512]{1,0:T(8,128)(2,1)}, bf16[128,512]{1,0:T(8,128)(2,1)}, u32[]{:S(2)}, u32[]{:S(2)}) collective-permute-start(bf16[128,512]{1,0:T(8,128)(2,1)} %get-tuple-element.58), channel_id=1, source_target_pairs={{0,8},{1,9},{4,12},{5,13},{8,14},{9,15},{12,10},{13,11},{14,6},{15... | collective-permute-start | bytes 393224 | tf_op jit(solution)/shard_map/ppermute | solution.py:39
  86.7 17.3 %collective-permute-start.19 = (bf16[128,512]{1,0:T(8,128)(2,1)}, bf16[128,512]{1,0:T(8,128)(2,1)}, u32[]{:S(2)}, u32[]{:S(2)}) collective-permute-start(bf16[128,512]{1,0:T(8,128)(2,1)} %get-tuple-element.56), channel_id=1, source_target_pairs={{0,10},{1,11},{4,6},{5,7},{8,2},{9,3},{12,0},{13,1},{14,4},{15,5},... | collective-permute-start | bytes 393224 | tf_op jit(solution)/shard_map/ppermute | solution.py:39
  88.4 16.5 %collective-permute-start.23 = (bf16[128,512]{1,0:T(8,128)(2,1)}, bf16[128,512]{1,0:T(8,128)(2,1)}, u32[]{:S(2)}, u32[]{:S(2)}) collective-permute-start(bf16[128,512]{1,0:T(8,128)(2,1)} %get-tuple-element.57), channel_id=1, source_target_pairs={{0,12},{1,13},{4,14},{5,15},{8,10},{9,11},{12,6},{13,7},{14,2},{15... | collective-permute-start | bytes 393224 | tf_op jit(solution)/shard_map/ppermute | solution.py:39
  96.2 8.7 %collective-permute-start.22 = (bf16[128,512]{1,0:T(8,128)(2,1)}, bf16[128,512]{1,0:T(8,128)(2,1)}, u32[]{:S(2)}, u32[]{:S(2)}) collective-permute-start(bf16[128,512]{1,0:T(8,128)(2,1)} %shard_map.72), channel_id=1, source_target_pairs={{0,14},{1,15},{4,10},{5,11},{8,6},{9,7},{12,2},{13,3},{14,0},{15,1... | collective-permute-start | bytes 393224 | tf_op jit(solution)/shard_map/ppermute | solution.py:39
  97.7 7.2 %copy-start.11 = (bf16[128,512]{1,0:T(8,128)(2,1)S(1)}, bf16[128,512]{1,0:T(8,128)(2,1)}, u32[]{:S(2)}) copy-start(bf16[128,512]{1,0:T(8,128)(2,1)} %copy-done.10) | copy-start | bytes 393220

commit v4 on v3

--- a/solution.py
+++ b/solution.py
@@ -14,6 +14,7 @@
 
 WHOLE = pl.BlockSpec(memory_space=pltpu.VMEM)
 SCALAR = pl.BlockSpec(memory_space=pltpu.SMEM)
+ANY = pl.BlockSpec(memory_space=pl.ANY)
 
 
 def contract_last(left, right):
@@ -116,27 +117,35 @@
     near_ref,
     far_ref,
     marks_in,
-    diag_ref,
-    cross_ref,
+    diag_in,
+    cross_in,
     cols_ref,
-    next_ref,
+    next_in,
     out_ref,
     sep_ref,
     sum_ref,
+    loaded_ref,
+    sems,
     marks_ref,
     pos_ref,
     pos_sem,
 ):
+    loads = []
+    for k, source in enumerate((diag_in, cross_in, next_in)):
+        loads.append(pltpu.make_async_copy(source, loaded_ref.at[k], sems.at[k]))
+        loads[-1].start()
     fetch = read_marks(marks_in, first, marks_ref, pos_ref, pos_sem)
-    rows, width = diag_ref.shape
+    sum_ref[...] = jnp.zeros_like(sum_ref)
+    for load in loads:
+        load.wait()
+    _, rows, width = loaded_ref.shape
     count = width // TILE
     for j in range(count):
         lanes = slice(j * TILE, (j + 1) * TILE)
-        sep_ref[j, :rows, :] = diag_ref[:, lanes]
+        sep_ref[j, :rows, :] = loaded_ref[0, :, lanes]
         sep_ref[j, rows:, :] = cols_ref[j, :rows, :]
-        sep_ref[count + j, :rows, :] = cross_ref[:, lanes]
-        sep_ref[count + j, rows:, :] = next_ref[:, lanes]
-    sum_ref[...] = jnp.zeros_like(sum_ref)
+        sep_ref[count + j, :rows, :] = loaded_ref[1, :, lanes]
+        sep_ref[count + j, rows:, :] = loaded_ref[2, :, lanes]
     fetch.wait()
 
     def add(tile, i, j):
@@ -153,14 +162,16 @@
     return pl.pallas_call(
         functools.partial(update_kernel, line, first),
         out_shape=jax.ShapeDtypeStruct((2 * rows, width), jnp.bfloat16),
-        in_specs=[SCALAR] + [WHOLE] * 7,
+        in_specs=[SCALAR] + [WHOLE] * 3 + [ANY, ANY, WHOLE, ANY],
         out_specs=WHOLE,
         scratch_shapes=[
             pltpu.VMEM((2 * count, 2 * rows, TILE), jnp.bfloat16),
             pltpu.VMEM((count, 2 * rows, TILE), jnp.float32),
+            pltpu.VMEM((3, rows, width), jnp.bfloat16),
+            pltpu.SemaphoreType.DMA((3,)),
         ]
         + mark_scratch(marks.shape[0]),
-        compiler_params=pltpu.CompilerParams(vmem_limit_bytes=12 * 1024 * 1024),
+        compiler_params=pltpu.CompilerParams(vmem_limit_bytes=54 * 1024 * 1024),
         cost_estimate=pl.CostEstimate(flops=0, bytes_accessed=rows, transcendentals=0),
     )(place, near, far, marks, diag, cross, cols, following)
 
@@ -296,6 +307,7 @@
     steps = ring.count // 2
     plain = tiles.reshape(-1, TILE)
     wahead, wbehind = [wrows, ring.turn(wrows, 1)], [wrows, ring.turn(wrows, -1)]
+    second = [ring.turn(wahead[1], 1), ring.turn(wbehind[1], -1)]
     following = lax.ppermute(diag, "tm", [(i + 1, i) for i in range(size - 1)])
     flipped = flip(tile_pos[0], cross)
     pieces = [plain]
@@ -319,12 +331,9 @@
             wahead[1], wbehind[1], following = beside
         pieces += [ahead, behind]
     pieces += across[1:] + across[:1]
-    for step in range(2, steps):
-        wahead.append(ring.turn(wahead[-1], 1))
-        wbehind.append(ring.turn(wbehind[-1], -1))
+    wahead.append(second[0])
+    wbehind.append(second[1])
     near = jnp.concatenate(pieces, axis=0)
-    if False:
-        near, wahead[2], wbehind[2] = lax.optimization_barrier((near, wahead[2], wbehind[2]))
     far = ring.to_core(near)
 
     first, marks = rows, cols
@@ -333,10 +342,10 @@
         cols = cols[:, :rows, :].reshape(width // TILE, TILE // rows, rows, rows)
         cols = cols.transpose(0, 2, 1, 3).reshape(width // TILE, rows, TILE)
     updated = update(ring.line, first, place, near, far, marks, diag, cross, cols, following)
-    if not False:
-        updated, wahead[2], wbehind[2] = lax.optimization_barrier(
-            (updated, wahead[2], wbehind[2])
-        )
+    updated, wahead[2], wbehind[2] = lax.optimization_barrier((updated, wahead[2], wbehind[2]))
+    for step in range(3, steps):
+        wahead.append(ring.turn(wahead[-1], 1))
+        wbehind.append(ring.turn(wbehind[-1], -1))
     other = ring.to_core(updated)
     factor = factor_rows(ring.line, first, place, near, far, marks, wrows)
 

time: 109 us -> 108 us (level)
  local copies, waits for them, and re-layouts: 10.5 us -> 6.73 us
  Pallas kernels: 20.2 us -> 23 us
    unnamed x31 -> x35, local copies, waits for them, and re-layouts: 9.66 us -> 5.9 us
    pallas_call x1, Pallas kernels: 4.93 us -> 7.32 us  [update(): pl.pallas_call(functools.partial(update_kernel, line, first), out_shape=j...]
    ppermute x22, waiting for transfers between devices: 31.2 us -> 30.1 us  [turn(): return lax.ppermute(part, 'rows', pairs)]
  transfers between devices with their start and end apart: 26 -> 26, of which waited for: 13 -> 13; matrix products, arithmetic and copies ran while one was open for 4% -> 2% of each run, Pallas kernels for 16% -> 18%
where the time goes in v4:
time: 108 us; the launch traced here: 107 us
  starting transfers between devices  44.9 us (42%)
  waiting for transfers between devices  31 us (29%)
  Pallas kernels  23 us (21%)
  local copies, waits for them, and re-layouts  6.73 us (6%)
    ppermute x22, starting transfers between devices, turn(): return lax.ppermute(part, 'rows', pairs)  40 us
    ppermute x22, waiting for transfers between devices, turn(): return lax.ppermute(part, 'rows', pairs)  30.1 us
    pallas_call x1, Pallas kernels, update(): pl.pallas_call(functools.partial(update_kernel, line, first), out_shape=j...  7.32 us
    pallas_call x3, Pallas kernels, products(): pl.pallas_call(functools.partial(products_kernel, len(lefts)), out_shape=...  6.62 us
    unnamed x35, local copies, waits for them, and re-layouts  5.9 us
    pallas_call x1, Pallas kernels, factor_rows(): pl.pallas_call(functools.partial(factor_kernel, line, first), out_shape=j...  4.21 us
    all_to_all x1, starting transfers between devices, shards(): cols = lax.all_to_all(flipped, 'rows', 0, 0, tiled=True)  3.59 us
    pallas_call x1, Pallas kernels, finish(): pl.pallas_call(functools.partial(finish_kernel, len(blocks) // SIDES), ou...  3.23 us
  transfers between devices with their start and end apart: 26, of which 13 were waited for; matrix products, arithmetic and copies ran while one was open for 2% of the time, Pallas kernels for 18%

profile of v4, /device:TPU:0, one launch (start us, length us, event | category | flops | bytes accessed | tf_op | source)
XLA Modules:
  0.0 107.1 jit_solution(7689695141441050981)
XLA Ops:
  0.6 6.1 %collective-permute-start = (bf16[512,128]{1,0:T(8,128)(2,1)}, bf16[512,128]{1,0:T(8,128)(2,1)S(1)}, u32[]{:S(2)}, u32[]{:S(2)}) collective-permute-start(bf16[512,128]{1,0:T(8,128)(2,1)} %bitcast.19), channel_id=1, source_target_pairs={{0,14},{1,15},{4,10},{5,11},{8,6},{9,7},{12,2},{13,3},{14,0},{15,1... | collective-permute-start | bytes 393224 | tf_op jit(solution)/shard_map/ppermute | solution.py:40
  6.7 2.0 %collective-permute-start.2 = (bf16[512,128]{1,0:T(8,128)(2,1)}, bf16[512,128]{1,0:T(8,128)(2,1)S(1)}, u32[]{:S(2)}, u32[]{:S(2)}) collective-permute-start(bf16[512,128]{1,0:T(8,128)(2,1)} %bitcast.21), channel_id=1, source_target_pairs={{0,2},{1,3},{4,0},{5,1},{8,4},{9,5},{12,8},{13,9},{14,12},{15,13},... | collective-permute-start | bytes 393224 | tf_op jit(solution)/shard_map/ppermute | solution.py:40
  8.7 2.0 %collective-permute-start.8 = (bf16[128,2048]{1,0:T(8,128)(2,1)}, bf16[128,2048]{1,0:T(8,128)(2,1)}, u32[]{:S(2)}, u32[]{:S(2)}) collective-permute-start(bf16[128,2048]{1,0:T(8,128)(2,1)} %bitcast.12), channel_id=1, source_target_pairs={{0,2},{1,3},{4,0},{5,1},{8,4},{9,5},{12,8},{13,9},{14,12},{15,13},... | collective-permute-start | bytes 1572872 | tf_op jit(solution)/shard_map/ppermute | solution.py:40
  10.8 0.9 constant_dynamic-update-slice_fusion.7
  11.7 0.8 copy.7.pos_ref
  12.5 1.0 copy-done.9
  13.5 1.6 %shard_map.68 = bf16[16,144,128]{2,1,0:T(8,128)(2,1)} custom-call(s32[4,2]{1,0:T(4,128)S(1)} %copy.7.pos_ref, bf16[128,2048]{1,0:T(8,128)(2,1)S(1)} %bitcast.16), custom_call_target="tpu_custom_call" | custom-call | bytes 128 | tf_op jit(solution)/shard_map/pallas_call | solution.py:67
  15.1 1.3 %collective-permute-start.9 = (bf16[128,2048]{1,0:T(8,128)(2,1)}, bf16[128,2048]{1,0:T(8,128)(2,1)S(1)}, u32[]{:S(2)}, u32[]{:S(2)}) collective-permute-start(bf16[128,2048]{1,0:T(8,128)(2,1)} %bitcast.17), channel_id=1, source_target_pairs={{16,0},{17,1},{18,2},{19,3},{20,4},{21,5},{22,6},{23,7},{24,8},{25... | collective-permute-start | bytes 1572872 | tf_op jit(solution)/shard_map/ppermute | solution.py:311
  16.4 0.6 pad_add_fusion.place_ref
  17.0 2.0 %collective-permute-start.4 = (bf16[512,128]{1,0:T(8,128)(2,1)S(1)}, bf16[512,128]{1,0:T(8,128)(2,1)S(1)}, u32[]{:S(2)}, u32[]{:S(2)}) collective-permute-start(bf16[512,128]{1,0:T(8,128)(2,1)S(1)} %collective-permute-done.2), channel_id=1, source_target_pairs={{0,2},{1,3},{4,0},{5,1},{8,4},{9,5},{12,8},{13,9},{14,12},{15,13},... | collective-permute-start | bytes 393224 | tf_op jit(solution)/shard_map/ppermute | solution.py:40
  19.0 3.6 %all-to-all-start = ((bf16[16,144,128]{2,1,0:T(8,128)(2,1)}), bf16[16,144,128]{2,1,0:T(8,128)(2,1)S(1)}, u32[]{:S(2)}, u32[]{:S(2)}) async-start(bf16[16,144,128]{2,1,0:T(8,128)(2,1)} %shard_map.68), calls=%async_computation | async-start | bytes 1179648 | tf_op jit(solution)/shard_map/all_to_all | solution.py:327
  22.7 6.0 %collective-permute-done.3 = bf16[512,128]{1,0:T(8,128)(2,1)S(1)} collective-permute-done((bf16[512,128]{1,0:T(8,128)(2,1)S(1)}, bf16[512,128]{1,0:T(8,128)(2,1)S(1)}, u32[]{:S(2)}, u32[]{:S(2)}) %collective-permute-start.3) | collective-permute-done | bytes 131104 | tf_op jit(solution)/shard_map/ppermute | solution.py:40
  28.7 0.5 collective-permute-done.4
  29.3 7.7 %collective-permute-start.5 = (bf16[512,128]{1,0:T(8,128)(2,1)S(1)}, bf16[512,128]{1,0:T(8,128)(2,1)S(1)}, u32[]{:S(2)}, u32[]{:S(2)}) collective-permute-start(bf16[512,128]{1,0:T(8,128)(2,1)S(1)} %collective-permute-done.3), channel_id=1, source_target_pairs={{0,4},{1,5},{4,8},{5,9},{8,12},{9,13},{12,14},{13,15},{14,10},{15,... | collective-permute-start | bytes 393224 | tf_op jit(solution)/shard_map/ppermute | solution.py:40
  37.1 2.5 %collective-permute-done.5 = bf16[512,128]{1,0:T(8,128)(2,1)S(1)} collective-permute-done((bf16[512,128]{1,0:T(8,128)(2,1)S(1)}, bf16[512,128]{1,0:T(8,128)(2,1)S(1)}, u32[]{:S(2)}, u32[]{:S(2)}) %collective-permute-start.5) | collective-permute-done | bytes 131104 | tf_op jit(solution)/shard_map/ppermute | solution.py:40
  39.5 2.8 %collective-permute-done.6 = bf16[512,128]{1,0:T(8,128)(2,1)S(1)} collective-permute-done((bf16[512,128]{1,0:T(8,128)(2,1)S(1)}, bf16[512,128]{1,0:T(8,128)(2,1)S(1)}, u32[]{:S(2)}, u32[]{:S(2)}) %collective-permute-start.6) | collective-permute-done | bytes 131104 | tf_op jit(solution)/shard_map/ppermute | solution.py:40
  42.4 0.8 copy-done.13
  43.2 0.1 collective-permute-start.10
  43.2 3.0 %collective-permute-start.11 = (bf16[128,2048]{1,0:T(8,128)(2,1)}, bf16[128,2048]{1,0:T(8,128)(2,1)}, u32[]{:S(2)}, u32[]{:S(2)}) collective-permute-start(bf16[128,2048]{1,0:T(8,128)(2,1)} %collective-permute-done.7.refs_1_), channel_id=1, source_target_pairs={{0,4},{1,5},{4,8},{5,9},{8,12},{9,13},{12,14},{13,15},{14,10},{15,... | collective-permute-start | bytes 1572872 | tf_op jit(solution)/shard_map/ppermute | solution.py:40
  46.3 0.8 copy-done.2
  47.1 1.0 copy-done.6
  48.1 7.3 %shard_map.69.refs_5_.refs_2_.refs_1_ = bf16[256,2048]{1,0:T(8,128)(2,1)} custom-call(s32[2]{0:T(128)} %pad_add_fusion.place_ref, bf16[4096,128]{1,0:T(8,128)(2,1)} %copy-done.4, bf16[4096,128]{1,0:T(8,128)(2,1)} %copy-done.6, bf16[16,144,128]{2,1,0:T(8,128)(2,1)} %copy-done.2, bf16[128,2048]{1,0:T(8,128)(2,1)} %bitcast.18, bf16[128,2048]{1,0:T(8,128)(2,1)} %bitcast.15, ...), custom_call_target="tpu_custom_call" | custom-call | bytes 128 | tf_op jit(solution)/shard_map/pallas_call | solution.py:162
  55.4 2.9 %collective-permute-done.11.refs_3_ = bf16[128,2048]{1,0:T(8,128)(2,1)} collective-permute-done((bf16[128,2048]{1,0:T(8,128)(2,1)}, bf16[128,2048]{1,0:T(8,128)(2,1)}, u32[]{:S(2)}, u32[]{:S(2)}) %collective-permute-start.11) | collective-permute-done | bytes 524320 | tf_op jit(solution)/shard_map/ppermute | solution.py:40
  58.4 2.2 %collective-permute-done.12.refs_4_ = bf16[128,2048]{1,0:T(8,128)(2,1)} collective-permute-done((bf16[128,2048]{1,0:T(8,128)(2,1)}, bf16[128,2048]{1,0:T(8,128)(2,1)}, u32[]{:S(2)}, u32[]{:S(2)}) %collective-permute-start.12) | collective-permute-done | bytes 524320 | tf_op jit(solution)/shard_map/ppermute | solution.py:40
  60.6 1.6 %collective-permute-start.16 = (bf16[128,2048]{1,0:T(8,128)(2,1)}, bf16[128,2048]{1,0:T(8,128)(2,1)S(1)}, u32[]{:S(2)}, u32[]{:S(2)}) collective-permute-start(bf16[128,2048]{1,0:T(8,128)(2,1)} %collective-permute-done.11.refs_3_), channel_id=1, source_target_pairs={{0,4},{1,5},{4,8},{5,9},{8,12},{9,13},{12,14},{13,15},{14,10},{15,... | collective-permute-start | bytes 1572872 | tf_op jit(solution)/shard_map/ppermute | solution.py:40
  62.2 0.4 collective-permute-start.17
  62.6 0.8 collective-permute-done.13.refs_6_.refs_3_.refs_2_
  63.4 1.2 %copy-done = bf16[256,2048]{1,0:T(8,128)(2,1)S(1)} copy-done((bf16[256,2048]{1,0:T(8,128)(2,1)S(1)}, bf16[256,2048]{1,0:T(8,128)(2,1)}, u32[]{:S(2)}) %copy-start) | copy-done | bytes 1048600
  64.7 3.8 %shard_map.70 = (bf16[128,512]{1,0:T(8,128)(2,1)S(1)}, bf16[128,512]{1,0:T(8,128)(2,1)S(1)}, bf16[128,512]{1,0:T(8,128)(2,1)S(1)}, bf16[128,512]{1,0:T(8,128)(2,1)}, bf16[128,512]{1,0:T(8,128)(2,1)}) custom-call(bf16[128,2048]{1,0:T(8,128)(2,1)S(1)} %bitcast.13, bf16[128,2048]{1,0:T(8,128)(2,1)} %collective-permute-done.7.refs_1_, ...), custom_call_target="tpu_custom_call" | custom-call | bytes 512 | tf_op jit(solution)/shard_map/pallas_call | solution.py:243
  68.4 0.3 collective-permute-start.14
  68.7 1.7 %collective-permute-start.15 = (bf16[128,512]{1,0:T(8,128)(2,1)S(1)}, bf16[128,512]{1,0:T(8,128)(2,1)S(1)}, u32[]{:S(2)}, u32[]{:S(2)}) collective-permute-start(bf16[128,512]{1,0:T(8,128)(2,1)S(1)} %get-tuple-element.51), channel_id=1, source_target_pairs={{0,4},{1,5},{4,8},{5,9},{8,12},{9,13},{12,14},{13,15},{14,10},{15,... | collective-permute-start | bytes 393224 | tf_op jit(solution)/shard_map/ppermute | solution.py:40
  70.4 5.1 %collective-permute-done.16.refs_0_ = bf16[128,2048]{1,0:T(8,128)(2,1)S(1)} collective-permute-done((bf16[128,2048]{1,0:T(8,128)(2,1)}, bf16[128,2048]{1,0:T(8,128)(2,1)S(1)}, u32[]{:S(2)}, u32[]{:S(2)}) %collective-permute-start.16) | collective-permute-done | bytes 524320 | tf_op jit(solution)/shard_map/ppermute | solution.py:40
  75.5 1.6 %collective-permute-done.17.refs_1_ = bf16[128,2048]{1,0:T(8,128)(2,1)S(1)} collective-permute-done((bf16[128,2048]{1,0:T(8,128)(2,1)}, bf16[128,2048]{1,0:T(8,128)(2,1)S(1)}, u32[]{:S(2)}, u32[]{:S(2)}) %collective-permute-start.17) | collective-permute-done | bytes 524320 | tf_op jit(solution)/shard_map/ppermute | solution.py:40
  77.1 2.1 %collective-permute-done.14.refs_1_ = bf16[128,512]{1,0:T(8,128)(2,1)S(1)} collective-permute-done((bf16[128,512]{1,0:T(8,128)(2,1)S(1)}, bf16[128,512]{1,0:T(8,128)(2,1)S(1)}, u32[]{:S(2)}, u32[]{:S(2)}) %collective-permute-start.14) | collective-permute-done | bytes 131104 | tf_op jit(solution)/shard_map/ppermute | solution.py:40
  79.3 0.3 collective-permute-start.20
  79.6 1.8 %collective-permute-start.21 = (bf16[64,2048]{1,0:T(8,128)(2,1)S(1)}, bf16[64,2048]{1,0:T(8,128)(2,1)S(1)}, u32[]{:S(2)}, u32[]{:S(2)}) collective-permute-start(bf16[64,2048]{1,0:T(8,128)(2,1)S(1)} %slice.7), channel_id=1, source_target_pairs={{0,2},{1,3},{4,0},{5,1},{8,4},{9,5},{12,8},{13,9},{14,12},{15,13},... | collective-permute-start | bytes 786440 | tf_op jit(solution)/shard_map/ppermute | solution.py:40
  81.4 0.2 collective-permute-start.18
  81.6 2.8 %collective-permute-start.24 = (bf16[128,512]{1,0:T(8,128)(2,1)}, bf16[128,512]{1,0:T(8,128)(2,1)}, u32[]{:S(2)}, u32[]{:S(2)}) collective-permute-start(bf16[128,512]{1,0:T(8,128)(2,1)} %get-tuple-element.58), channel_id=1, source_target_pairs={{0,8},{1,9},{4,12},{5,13},{8,14},{9,15},{12,10},{13,11},{14,6},{15... | collective-permute-start | bytes 393224 | tf_op jit(solution)/shard_map/ppermute | solution.py:40
  84.3 1.4 %shard_map.71 = (bf16[128,512]{1,0:T(8,128)(2,1)}, bf16[128,512]{1,0:T(8,128)(2,1)}) custom-call(bf16[128,2048]{1,0:T(8,128)(2,1)S(1)} %collective-permute-done.16.refs_0_, bf16[128,2048]{1,0:T(8,128)(2,1)S(1)} %collective-permute-done.17.refs_1_, bf16[256,2048]{1,0:T(8,128)(2,1)S(1)} %copy-done, ...), custom_call_target="tpu_custom_call" | custom-call | bytes 512 | tf_op jit(solution)/shard_map/pallas_call | solution.py:243
  85.8 0.2 collective-permute-start.19
  85.9 1.5 %collective-permute-done.20 = bf16[64,2048]{1,0:T(8,128)(2,1)S(1)} collective-permute-done((bf16[64,2048]{1,0:T(8,128)(2,1)S(1)}, bf16[64,2048]{1,0:T(8,128)(2,1)S(1)}, u32[]{:S(2)}, u32[]{:S(2)}) %collective-permute-start.20) | collective-permute-done | bytes 262176 | tf_op jit(solution)/shard_map/ppermute | solution.py:40
  87.4 6.2 %collective-permute-start.23 = (bf16[128,512]{1,0:T(8,128)(2,1)}, bf16[128,512]{1,0:T(8,128)(2,1)}, u32[]{:S(2)}, u32[]{:S(2)}) collective-permute-start(bf16[128,512]{1,0:T(8,128)(2,1)} %get-tuple-element.57), channel_id=1, source_target_pairs={{0,12},{1,13},{4,14},{5,15},{8,10},{9,11},{12,6},{13,7},{14,2},{15... | collective-permute-start | bytes 393224 | tf_op jit(solution)/shard_map/ppermute | solution.py:40
  93.7 1.5 %shard_map.72 = bf16[128,512]{1,0:T(8,128)(2,1)} custom-call(bf16[128,2048]{1,0:T(8,128)(2,1)S(1)} %pad_maximum_fusion.refs_0_, bf16[256,2048]{1,0:T(8,128)(2,1)S(1)} %copy-done.1, bf16[256,2048]{1,0:T(8,128)(2,1)S(1)} %collective-permute-done.13.refs_6_.refs_3_.refs_2_), custom_call_target="tpu_custom_call" | custom-call | bytes 512 | tf_op jit(solution)/shard_map/pallas_call | solution.py:243
  95.2 1.5 %collective-permute-start.22 = (bf16[128,512]{1,0:T(8,128)(2,1)}, bf16[128,512]{1,0:T(8,128)(2,1)}, u32[]{:S(2)}, u32[]{:S(2)}) collective-permute-start(bf16[128,512]{1,0:T(8,128)(2,1)} %shard_map.72), channel_id=1, source_target_pairs={{0,14},{1,15},{4,10},{5,11},{8,6},{9,7},{12,2},{13,3},{14,0},{15,1... | collective-permute-start | bytes 393224 | tf_op jit(solution)/shard_map/ppermute | solution.py:40
  96.8 4.2 %shard_map.73.refs_8_ = bf16[128,4096]{1,0:T(8,128)(2,1)S(1)} custom-call(s32[2]{0:T(128)S(1)} %copy-done.12, bf16[4096,128]{1,0:T(8,128)(2,1)S(1)} %copy-done.5, bf16[4096,128]{1,0:T(8,128)(2,1)S(1)} %copy-done.7, bf16[16,144,128]{2,1,0:T(8,128)(2,1)S(1)} %copy-done.3, bf16[128,2048]{1,0:T(8,128)(2,1)S(1)} %bitcast.14), custom_call_target="tpu_custom_call" | custom-call | bytes 128 | tf_op jit(solution)/shard_map/pallas_call | solution.py:212
  101.0 2.0 %collective-permute-done.18.refs_2_ = bf16[128,512]{1,0:T(8,128)(2,1)} collective-permute-done((bf16[128,512]{1,0:T(8,128)(2,1)}, bf16[128,512]{1,0:T(8,128)(2,1)}, u32[]{:S(2)}, u32[]{:S(2)}) %collective-permute-start.18) | collective-permute-done | bytes 131104 | tf_op jit(solution)/shard_map/ppermute | solution.py:40
  103.0 0.9 collective-permute-done.23.refs_5_
  103.9 3.2 %shard_map.74 = (f32[128,4096]{1,0:T(8,128)}, f32[128,128]{1,0:T(8,128)}) custom-call(s32[2]{0:T(128)S(1)} %copy-done.12, bf16[128,512]{1,0:T(8,128)(2,1)S(1)} %get-tuple-element.49.refs_0_, bf16[128,512]{1,0:T(8,128)(2,1)S(1)} %collective-permute-done.14.refs_1_, bf16[128,512]{1,0:T(8,128)(2,1)} %collective-permute-done.18.refs_2_, ...), custom_call_target="tpu_custom_call" | custom-call | bytes 128 | tf_op jit(solution)/shard_map/pallas_call | solution.py:278
  (53 shorter events, 0.3 us)
Async XLA Ops:
  0.6 14.5 %collective-permute-start = (bf16[512,128]{1,0:T(8,128)(2,1)}, bf16[512,128]{1,0:T(8,128)(2,1)S(1)}, u32[]{:S(2)}, u32[]{:S(2)}) collective-permute-start(bf16[512,128]{1,0:T(8,128)(2,1)} %bitcast.19), channel_id=1, source_target_pairs={{0,14},{1,15},{4,10},{5,11},{8,6},{9,7},{12,2},{13,3},{14,0},{15,1... | collective-permute-start | bytes 393224 | tf_op jit(solution)/shard_map/ppermute | solution.py:40
  6.7 10.3 %collective-permute-start.1 = (bf16[512,128]{1,0:T(8,128)(2,1)}, bf16[512,128]{1,0:T(8,128)(2,1)S(1)}, u32[]{:S(2)}, u32[]{:S(2)}) collective-permute-start(bf16[512,128]{1,0:T(8,128)(2,1)} %bitcast.20), channel_id=1, source_target_pairs={{0,4},{1,5},{4,8},{5,9},{8,12},{9,13},{12,14},{13,15},{14,10},{15,... | collective-permute-start | bytes 393224 | tf_op jit(solution)/shard_map/ppermute | solution.py:40
  6.7 10.3 %collective-permute-start.2 = (bf16[512,128]{1,0:T(8,128)(2,1)}, bf16[512,128]{1,0:T(8,128)(2,1)S(1)}, u32[]{:S(2)}, u32[]{:S(2)}) collective-permute-start(bf16[512,128]{1,0:T(8,128)(2,1)} %bitcast.21), channel_id=1, source_target_pairs={{0,2},{1,3},{4,0},{5,1},{8,4},{9,5},{12,8},{13,9},{14,12},{15,13},... | collective-permute-start | bytes 393224 | tf_op jit(solution)/shard_map/ppermute | solution.py:40
  8.7 33.6 %collective-permute-start.7 = (bf16[128,2048]{1,0:T(8,128)(2,1)}, bf16[128,2048]{1,0:T(8,128)(2,1)}, u32[]{:S(2)}, u32[]{:S(2)}) collective-permute-start(bf16[128,2048]{1,0:T(8,128)(2,1)} %bitcast.11), channel_id=1, source_target_pairs={{0,4},{1,5},{4,8},{5,9},{8,12},{9,13},{12,14},{13,15},{14,10},{15,... | collective-permute-start | bytes 1572872 | tf_op jit(solution)/shard_map/ppermute | solution.py:40
  8.7 33.6 %collective-permute-start.8 = (bf16[128,2048]{1,0:T(8,128)(2,1)}, bf16[128,2048]{1,0:T(8,128)(2,1)}, u32[]{:S(2)}, u32[]{:S(2)}) collective-permute-start(bf16[128,2048]{1,0:T(8,128)(2,1)} %bitcast.12), channel_id=1, source_target_pairs={{0,2},{1,3},{4,0},{5,1},{8,4},{9,5},{12,8},{13,9},{14,12},{15,13},... | collective-permute-start | bytes 1572872 | tf_op jit(solution)/shard_map/ppermute | solution.py:40
  12.5 1.0 copy-start.9
  15.1 27.2 %collective-permute-start.9 = (bf16[128,2048]{1,0:T(8,128)(2,1)}, bf16[128,2048]{1,0:T(8,128)(2,1)S(1)}, u32[]{:S(2)}, u32[]{:S(2)}) collective-permute-start(bf16[128,2048]{1,0:T(8,128)(2,1)} %bitcast.17), channel_id=1, source_target_pairs={{16,0},{17,1},{18,2},{19,3},{20,4},{21,5},{22,6},{23,7},{24,8},{25... | collective-permute-start | bytes 1572872 | tf_op jit(solution)/shard_map/ppermute | solution.py:311
  17.0 11.7 %collective-permute-start.3 = (bf16[512,128]{1,0:T(8,128)(2,1)S(1)}, bf16[512,128]{1,0:T(8,128)(2,1)S(1)}, u32[]{:S(2)}, u32[]{:S(2)}) collective-permute-start(bf16[512,128]{1,0:T(8,128)(2,1)S(1)} %collective-permute-done.1), channel_id=1, source_target_pairs={{0,4},{1,5},{4,8},{5,9},{8,12},{9,13},{12,14},{13,15},{14,10},{15,... | collective-permute-start | bytes 393224 | tf_op jit(solution)/shard_map/ppermute | solution.py:40
  17.0 12.3 %collective-permute-start.4 = (bf16[512,128]{1,0:T(8,128)(2,1)S(1)}, bf16[512,128]{1,0:T(8,128)(2,1)S(1)}, u32[]{:S(2)}, u32[]{:S(2)}) collective-permute-start(bf16[512,128]{1,0:T(8,128)(2,1)S(1)} %collective-permute-done.2), channel_id=1, source_target_pairs={{0,2},{1,3},{4,0},{5,1},{8,4},{9,5},{12,8},{13,9},{14,12},{15,13},... | collective-permute-start | bytes 393224 | tf_op jit(solution)/shard_map/ppermute | solution.py:40
  19.0 27.2 %all-to-all-start = ((bf16[16,144,128]{2,1,0:T(8,128)(2,1)}), bf16[16,144,128]{2,1,0:T(8,128)(2,1)S(1)}, u32[]{:S(2)}, u32[]{:S(2)}) async-start(bf16[16,144,128]{2,1,0:T(8,128)(2,1)} %shard_map.68), calls=%async_computation | async-start | bytes 1179648 | tf_op jit(solution)/shard_map/all_to_all | solution.py:327
  29.3 10.3 %collective-permute-start.5 = (bf16[512,128]{1,0:T(8,128)(2,1)S(1)}, bf16[512,128]{1,0:T(8,128)(2,1)S(1)}, u32[]{:S(2)}, u32[]{:S(2)}) collective-permute-start(bf16[512,128]{1,0:T(8,128)(2,1)S(1)} %collective-permute-done.3), channel_id=1, source_target_pairs={{0,4},{1,5},{4,8},{5,9},{8,12},{9,13},{12,14},{13,15},{14,10},{15,... | collective-permute-start | bytes 393224 | tf_op jit(solution)/shard_map/ppermute | solution.py:40
  37.0 5.3 %collective-permute-start.6 = (bf16[512,128]{1,0:T(8,128)(2,1)S(1)}, bf16[512,128]{1,0:T(8,128)(2,1)S(1)}, u32[]{:S(2)}, u32[]{:S(2)}) collective-permute-start(bf16[512,128]{1,0:T(8,128)(2,1)S(1)} %collective-permute-done.4), channel_id=1, source_target_pairs={{0,2},{1,3},{4,0},{5,1},{8,4},{9,5},{12,8},{13,9},{14,12},{15,13},... | collective-permute-start | bytes 393224 | tf_op jit(solution)/shard_map/ppermute | solution.py:40
  42.3 0.8 copy-start.13
  43.1 3.1 %copy-start.4 = (bf16[4096,128]{1,0:T(8,128)(2,1)}, bf16[4096,128]{1,0:T(8,128)(2,1)S(1)}, u32[]{:S(2)}) copy-start(bf16[4096,128]{1,0:T(8,128)(2,1)S(1)} %constant_dynamic-update-slice_fusion.near_ref) | copy-start | bytes 3145732
  43.2 20.3 %copy-start.8 = (bf16[1,128,2048]{2,1,0:T(8,128)(2,1)S(1)}, bf16[1,128,2048]{2,1,0:T(8,128)(2,1)}, u32[]{:S(2)}) copy-start(bf16[1,128,2048]{2,1,0:T(8,128)(2,1)} %param.5) | copy-start | bytes 1572868
  43.2 3.1 %collective-permute-start.10 = (bf16[4096,128]{1,0:T(8,128)(2,1)S(1)}, bf16[4096,128]{1,0:T(8,128)(2,1)S(1)}, u32[]{:S(2)}, u32[]{:S(2)}) collective-permute-start(bf16[4096,128]{1,0:T(8,128)(2,1)S(1)} %constant_dynamic-update-slice_fusion.near_ref), channel_id=1, source_target_pairs={{0,1},{1,0},{2,3},{3,2},{4,5},{5,4},{6,7},{7,6},{8,9},{9,8},{10,11... | collective-permute-start | bytes 3145736 | tf_op jit(solution)/shard_map/ppermute | solution.py:44
  43.2 15.1 %collective-permute-start.11 = (bf16[128,2048]{1,0:T(8,128)(2,1)}, bf16[128,2048]{1,0:T(8,128)(2,1)}, u32[]{:S(2)}, u32[]{:S(2)}) collective-permute-start(bf16[128,2048]{1,0:T(8,128)(2,1)} %collective-permute-done.7.refs_1_), channel_id=1, source_target_pairs={{0,4},{1,5},{4,8},{5,9},{8,12},{9,13},{12,14},{13,15},{14,10},{15,... | collective-permute-start | bytes 1572872 | tf_op jit(solution)/shard_map/ppermute | solution.py:40
  46.3 14.3 %collective-permute-start.12 = (bf16[128,2048]{1,0:T(8,128)(2,1)}, bf16[128,2048]{1,0:T(8,128)(2,1)}, u32[]{:S(2)}, u32[]{:S(2)}) collective-permute-start(bf16[128,2048]{1,0:T(8,128)(2,1)} %collective-permute-done.8.refs_2_), channel_id=1, source_target_pairs={{0,2},{1,3},{4,0},{5,1},{8,4},{9,5},{12,8},{13,9},{14,12},{15,13},... | collective-permute-start | bytes 1572872 | tf_op jit(solution)/shard_map/ppermute | solution.py:40
  46.3 0.8 copy-start.2
  47.1 1.0 copy-start.6
  60.6 2.9 %collective-permute-start.13 = (bf16[256,2048]{1,0:T(8,128)(2,1)}, bf16[256,2048]{1,0:T(8,128)(2,1)S(1)}, u32[]{:S(2)}, u32[]{:S(2)}) collective-permute-start(bf16[256,2048]{1,0:T(8,128)(2,1)} %shard_map.69.refs_5_.refs_2_.refs_1_), channel_id=1, source_target_pairs={{0,1},{1,0},{2,3},{3,2},{4,5},{5,4},{6,7},{7,6},{8,9},{9,8},{10,11... | collective-permute-start | bytes 3145736 | tf_op jit(solution)/shard_map/ppermute | solution.py:44
  60.6 14.9 %collective-permute-start.16 = (bf16[128,2048]{1,0:T(8,128)(2,1)}, bf16[128,2048]{1,0:T(8,128)(2,1)S(1)}, u32[]{:S(2)}, u32[]{:S(2)}) collective-permute-start(bf16[128,2048]{1,0:T(8,128)(2,1)} %collective-permute-done.11.refs_3_), channel_id=1, source_target_pairs={{0,4},{1,5},{4,8},{5,9},{8,12},{9,13},{12,14},{13,15},{14,10},{15,... | collective-permute-start | bytes 1572872 | tf_op jit(solution)/shard_map/ppermute | solution.py:40
  62.2 15.0 %collective-permute-start.17 = (bf16[128,2048]{1,0:T(8,128)(2,1)}, bf16[128,2048]{1,0:T(8,128)(2,1)S(1)}, u32[]{:S(2)}, u32[]{:S(2)}) collective-permute-start(bf16[128,2048]{1,0:T(8,128)(2,1)} %collective-permute-done.12.refs_4_), channel_id=1, source_target_pairs={{0,2},{1,3},{4,0},{5,1},{8,4},{9,5},{12,8},{13,9},{14,12},{15,13},... | collective-permute-start | bytes 1572872 | tf_op jit(solution)/shard_map/ppermute | solution.py:40
  63.4 1.2 %copy-start = (bf16[256,2048]{1,0:T(8,128)(2,1)S(1)}, bf16[256,2048]{1,0:T(8,128)(2,1)}, u32[]{:S(2)}) copy-start(bf16[256,2048]{1,0:T(8,128)(2,1)} %shard_map.69.refs_5_.refs_2_.refs_1_) | copy-start | bytes 3145732
  68.4 10.8 %collective-permute-start.14 = (bf16[128,512]{1,0:T(8,128)(2,1)S(1)}, bf16[128,512]{1,0:T(8,128)(2,1)S(1)}, u32[]{:S(2)}, u32[]{:S(2)}) collective-permute-start(bf16[128,512]{1,0:T(8,128)(2,1)S(1)} %get-tuple-element.50), channel_id=1, source_target_pairs={{0,2},{1,3},{4,0},{5,1},{8,4},{9,5},{12,8},{13,9},{14,12},{15,13},... | collective-permute-start | bytes 393224 | tf_op jit(solution)/shard_map/ppermute | solution.py:40
  68.7 10.5 %collective-permute-start.15 = (bf16[128,512]{1,0:T(8,128)(2,1)S(1)}, bf16[128,512]{1,0:T(8,128)(2,1)S(1)}, u32[]{:S(2)}, u32[]{:S(2)}) collective-permute-start(bf16[128,512]{1,0:T(8,128)(2,1)S(1)} %get-tuple-element.51), channel_id=1, source_target_pairs={{0,4},{1,5},{4,8},{5,9},{8,12},{9,13},{12,14},{13,15},{14,10},{15,... | collective-permute-start | bytes 393224 | tf_op jit(solution)/shard_map/ppermute | solution.py:40
  79.2 6.5 %copy-start.10 = (bf16[128,512]{1,0:T(8,128)(2,1)}, bf16[128,512]{1,0:T(8,128)(2,1)S(1)}, u32[]{:S(2)}) copy-start(bf16[128,512]{1,0:T(8,128)(2,1)S(1)} %collective-permute-done.15.refs_7_) | copy-start | bytes 393220
  79.3 8.2 %collective-permute-start.20 = (bf16[64,2048]{1,0:T(8,128)(2,1)S(1)}, bf16[64,2048]{1,0:T(8,128)(2,1)S(1)}, u32[]{:S(2)}, u32[]{:S(2)}) collective-permute-start(bf16[64,2048]{1,0:T(8,128)(2,1)S(1)} %slice.6), channel_id=1, source_target_pairs={{0,4},{1,5},{4,8},{5,9},{8,12},{9,13},{12,14},{13,15},{14,10},{15,... | collective-permute-start | bytes 786440 | tf_op jit(solution)/shard_map/ppermute | solution.py:40
  79.6 14.1 %collective-permute-start.21 = (bf16[64,2048]{1,0:T(8,128)(2,1)S(1)}, bf16[64,2048]{1,0:T(8,128)(2,1)S(1)}, u32[]{:S(2)}, u32[]{:S(2)}) collective-permute-start(bf16[64,2048]{1,0:T(8,128)(2,1)S(1)} %slice.7), channel_id=1, source_target_pairs={{0,2},{1,3},{4,0},{5,1},{8,4},{9,5},{12,8},{13,9},{14,12},{15,13},... | collective-permute-start | bytes 786440 | tf_op jit(solution)/shard_map/ppermute | solution.py:40
  81.4 21.6 %collective-permute-start.18 = (bf16[128,512]{1,0:T(8,128)(2,1)}, bf16[128,512]{1,0:T(8,128)(2,1)}, u32[]{:S(2)}, u32[]{:S(2)}) collective-permute-start(bf16[128,512]{1,0:T(8,128)(2,1)} %get-tuple-element.53), channel_id=1, source_target_pairs={{0,6},{1,7},{4,2},{5,3},{8,0},{9,1},{12,4},{13,5},{14,8},{15,9},{1... | collective-permute-start | bytes 393224 | tf_op jit(solution)/shard_map/ppermute | solution.py:40
  81.6 12.1 %copy-start.1 = (bf16[256,2048]{1,0:T(8,128)(2,1)S(1)}, bf16[256,2048]{1,0:T(8,128)(2,1)}, u32[]{:S(2)}) copy-start(bf16[256,2048]{1,0:T(8,128)(2,1)} %shard_map.69.refs_5_.refs_2_.refs_1_) | copy-start | bytes 3145732
  81.6 21.4 %collective-permute-start.24 = (bf16[128,512]{1,0:T(8,128)(2,1)}, bf16[128,512]{1,0:T(8,128)(2,1)}, u32[]{:S(2)}, u32[]{:S(2)}) collective-permute-start(bf16[128,512]{1,0:T(8,128)(2,1)} %get-tuple-element.58), channel_id=1, source_target_pairs={{0,8},{1,9},{4,12},{5,13},{8,14},{9,15},{12,10},{13,11},{14,6},{15... | collective-permute-start | bytes 393224 | tf_op jit(solution)/shard_map/ppermute | solution.py:40
  85.7 11.0 %copy-start.3 = (bf16[16,144,128]{2,1,0:T(8,128)(2,1)S(1)}, bf16[16,144,128]{2,1,0:T(8,128)(2,1)}, u32[]{:S(2)}) copy-start(bf16[16,144,128]{2,1,0:T(8,128)(2,1)} %copy-done.2) | copy-start | bytes 1769476
  85.7 11.0 %copy-start.5 = (bf16[4096,128]{1,0:T(8,128)(2,1)S(1)}, bf16[4096,128]{1,0:T(8,128)(2,1)}, u32[]{:S(2)}) copy-start(bf16[4096,128]{1,0:T(8,128)(2,1)} %copy-done.4) | copy-start | bytes 3145732
  85.7 11.1 %copy-start.7 = (bf16[4096,128]{1,0:T(8,128)(2,1)S(1)}, bf16[4096,128]{1,0:T(8,128)(2,1)}, u32[]{:S(2)}) copy-start(bf16[4096,128]{1,0:T(8,128)(2,1)} %copy-done.6) | copy-start | bytes 3145732
  85.7 11.1 %copy-start.12 = (s32[2]{0:T(128)S(1)}, s32[2]{0:T(128)}, u32[]{:S(2)}) copy-start(s32[2]{0:T(128)} %pad_add_fusion.place_ref) | copy-start | bytes 28
  85.8 17.2 %collective-permute-start.19 = (bf16[128,512]{1,0:T(8,128)(2,1)}, bf16[128,512]{1,0:T(8,128)(2,1)}, u32[]{:S(2)}, u32[]{:S(2)}) collective-permute-start(bf16[128,512]{1,0:T(8,128)(2,1)} %get-tuple-element.56), channel_id=1, source_target_pairs={{0,10},{1,11},{4,6},{5,7},{8,2},{9,3},{12,0},{13,1},{14,4},{15,5},... | collective-permute-start | bytes 393224 | tf_op jit(solution)/shard_map/ppermute | solution.py:40
  87.4 16.5 %collective-permute-start.23 = (bf16[128,512]{1,0:T(8,128)(2,1)}, bf16[128,512]{1,0:T(8,128)(2,1)}, u32[]{:S(2)}, u32[]{:S(2)}) collective-permute-start(bf16[128,512]{1,0:T(8,128)(2,1)} %get-tuple-element.57), channel_id=1, source_target_pairs={{0,12},{1,13},{4,14},{5,15},{8,10},{9,11},{12,6},{13,7},{14,2},{15... | collective-permute-start | bytes 393224 | tf_op jit(solution)/shard_map/ppermute | solution.py:40
  95.2 8.7 %collective-permute-start.22 = (bf16[128,512]{1,0:T(8,128)(2,1)}, bf16[128,512]{1,0:T(8,128)(2,1)}, u32[]{:S(2)}, u32[]{:S(2)}) collective-permute-start(bf16[128,512]{1,0:T(8,128)(2,1)} %shard_map.72), channel_id=1, source_target_pairs={{0,14},{1,15},{4,10},{5,11},{8,6},{9,7},{12,2},{13,3},{14,0},{15,1... | collective-permute-start | bytes 393224 | tf_op jit(solution)/shard_map/ppermute | solution.py:40
  96.8 7.1 %copy-start.11 = (bf16[128,512]{1,0:T(8,128)(2,1)S(1)}, bf16[128,512]{1,0:T(8,128)(2,1)}, u32[]{:S(2)}) copy-start(bf16[128,512]{1,0:T(8,128)(2,1)} %copy-done.10) | copy-start | bytes 393220

commit v5 on v4

--- a/solution.py
+++ b/solution.py
@@ -39,14 +39,22 @@
             pairs += [(chip * CORES + c, target * CORES + c) for c in range(CORES)]
         return lax.ppermute(part, "rows", pairs)
 
+    def move(self, part, by, cross=0):
+        pairs = []
+        for z in range(self.line):
+            for y in range(SIDES):
+                source = (z * SIDES + y) * CORES
+                target = ((z + by) % self.line * SIDES + (y ^ cross)) * CORES
+                pairs += [(source + c, target + c) for c in range(CORES)]
+        return lax.ppermute(part, "rows", pairs)
+
     def to_core(self, part):
         devices = self.count * CORES
         return lax.ppermute(part, "rows", [(i, i ^ 1) for i in range(devices)])
 
     def opposite(self, ahead, behind):
         half = ahead.shape[0] // 2
-        first = self.turn(ahead[:half], 1)
-        return jnp.concatenate([first, self.turn(behind[half:], -1)], axis=0)
+        return [self.turn(ahead[:half], 1), self.turn(behind[half:], -1)]
 
 
 def flip_kernel(pos_ref, cross_ref, out_ref):
@@ -85,15 +93,13 @@
 
 
 def each_tile(line, place_ref, near_ref, far_ref, pos_ref, add):
-    spot, core = place_ref[0], place_ref[1]
+    core = place_ref[1]
     count = line * SIDES
     per_shard = near_ref.shape[0] // (count * TILE)
 
     @pl.loop(0, count)
     def _(s):
-        step = (s + 1) // 2
-        at = lax.rem(spot + jnp.where(s == 2 * step, step, count - step), count)
-        chip = jnp.where(at < line, at * SIDES, (2 * line - 1 - at) * SIDES + 1)
+        chip = place_ref[2 + s]
         for turn, ref in enumerate((near_ref, far_ref)):
             source = chip * CORES + (core if turn == 0 else 1 - core)
             for t in range(per_shard):
@@ -228,9 +234,11 @@
     lefts, (near_ref, far_ref), outs = refs[:many], refs[many : many + 2], refs[many + 2 : -1]
     all_ref = refs[-1]
     size = near_ref.shape[0]
-    rows = lefts[0].shape[0]
-    for k, left_ref in enumerate(lefts):
-        all_ref[k * rows : (k + 1) * rows, :] = left_ref[...]
+    at = 0
+    for left_ref in lefts:
+        all_ref[at : at + left_ref.shape[0], :] = left_ref[...]
+        at += left_ref.shape[0]
+    rows = outs[0].shape[0]
     for at, ref in ((0, near_ref), (size, far_ref)):
         value = (-contract_last(all_ref[...], ref[...])).astype(jnp.bfloat16)
         for k, out_ref in enumerate(outs):
@@ -238,17 +246,20 @@
 
 
 def products(lefts, near, far):
+    lefts = [left if isinstance(left, list) else [left] for left in lefts]
+    parts = [part for left in lefts for part in left]
     size = 2 * near.shape[0]
-    rows, width = lefts[0].shape
+    rows = sum(part.shape[0] for part in lefts[0])
+    width = near.shape[1]
     return pl.pallas_call(
-        functools.partial(products_kernel, len(lefts)),
+        functools.partial(products_kernel, len(parts)),
         out_shape=(jax.ShapeDtypeStruct((rows, size), jnp.bfloat16),) * len(lefts),
-        in_specs=[WHOLE] * (len(lefts) + 2),
+        in_specs=[WHOLE] * (len(parts) + 2),
         out_specs=(WHOLE,) * len(lefts),
         scratch_shapes=[pltpu.VMEM((len(lefts) * rows, width), jnp.bfloat16)],
         compiler_params=pltpu.CompilerParams(vmem_limit_bytes=12 * 1024 * 1024),
         cost_estimate=pl.CostEstimate(flops=0, bytes_accessed=size, transcendentals=0),
-    )(*lefts, near, far)
+    )(*parts, near, far)
 
 
 def finish_kernel(line, place_ref, *refs):
@@ -301,7 +312,12 @@
     far_side = chip % SIDES == 1
     spot = jnp.where(far_side, ring.count - 1 - chip // SIDES, chip // SIDES)
 
-    place = jnp.stack([spot, core]).astype(jnp.int32)
+    half = ring.line // 2
+    shifts = [0] + [sign * k for k in range(1, half) for sign in (1, -1)] + [half]
+    along = (chip // SIDES + jnp.asarray(shifts * SIDES, jnp.int32)) % ring.line
+    sides = jnp.asarray([side for side in range(SIDES) for _ in shifts], jnp.int32)
+    chips = along * SIDES + (sides ^ (chip % SIDES))
+    place = jnp.concatenate([spot[None], core[None], chips]).astype(jnp.int32)
 
     size = lax.axis_size("tm")
     steps = ring.count // 2
@@ -310,27 +326,26 @@
     second = [ring.turn(wahead[1], 1), ring.turn(wbehind[1], -1)]
     following = lax.ppermute(diag, "tm", [(i + 1, i) for i in range(size - 1)])
     flipped = flip(tile_pos[0], cross)
-    pieces = [plain]
-    ahead = behind = plain
-    across = [ring.turn(plain, steps)]
-    for step in range(1, steps - 0):
-        ahead, behind = ring.turn(ahead, 1), ring.turn(behind, -1)
-        beside = []
-        if step == 1:
-            across, ahead, behind = lax.optimization_barrier((across, ahead, behind))
-        if step == 3:
-            beside = [wahead[1], wbehind[1], following]
-        if step == 1:
-            ahead, behind, flipped, place, *beside = lax.optimization_barrier(
-                (ahead, behind, flipped, place, *beside)
-            )
-            cols = lax.all_to_all(flipped, "rows", 0, 0, tiled=True)
-        else:
-            ahead, behind, *beside = lax.optimization_barrier((ahead, behind, *beside))
-        if beside:
-            wahead[1], wbehind[1], following = beside
-        pieces += [ahead, behind]
-    pieces += across[1:] + across[:1]
+    pieces = {0: plain, 1: ring.move(plain, -1), -1: ring.move(plain, 1)}
+    sides = {0: ring.move(plain, 0, 1)}
+    pieces[1], pieces[-1], sides[0], flipped, place = lax.optimization_barrier(
+        (pieces[1], pieces[-1], sides[0], flipped, place)
+    )
+    cols = lax.all_to_all(flipped, "rows", 0, 0, tiled=True)
+    for k in range(2, half):
+        pieces[k], pieces[-k] = ring.move(pieces[k - 1], -1), ring.move(pieces[1 - k], 1)
+    pieces[half] = ring.move(pieces[half - 1], -1)
+    for k in shifts[1:-1]:
+        sides[k] = ring.move(pieces[k], 0, 1)
+    pieces[half], *back = lax.optimization_barrier(
+        (pieces[half], *[sides[k] for k in shifts[1:-1]])
+    )
+    sides.update(zip(shifts[1:-1], back))
+    sides[half] = ring.move(pieces[half], 0, 1)
+    sides[half], wahead[1], wbehind[1], following = lax.optimization_barrier(
+        (sides[half], wahead[1], wbehind[1], following)
+    )
+    pieces = [pieces[k] for k in shifts] + [sides[k] for k in shifts]
     wahead.append(second[0])
     wbehind.append(second[1])
     near = jnp.concatenate(pieces, axis=0)

time: 108 us -> 108 us (level); the launches traced: 107 us -> 106 us
  starting transfers between devices: 44.9 us -> 41.2 us
  local copies, waits for them, and re-layouts: 6.73 us -> 9.73 us
    ppermute x22 -> x15, starting transfers between devices: 40 us -> 21.5 us  [turn(): return lax.ppermute(part, 'rows', pairs)]
    ppermute x0 -> x7, starting transfers between devices: none -> 14.7 us  [move(): return lax.ppermute(part, 'rows', pairs)]
    ppermute x22 -> x15, waiting for transfers between devices: 30.1 us -> 19 us  [turn(): return lax.ppermute(part, 'rows', pairs)]
    ppermute x1, waiting for transfers between devices: 0.01 us -> 6.19 us  [shards(): following = lax.ppermute(diag, 'tm', [(i + 1, i) for i in range(size - 1)])]
    ppermute x0 -> x7, waiting for transfers between devices: none -> 3.51 us  [move(): return lax.ppermute(part, 'rows', pairs)]
    unnamed x35 -> x43, local copies, waits for them, and re-layouts: 5.9 us -> 8.9 us
  transfers between devices with their start and end apart: 26 -> 26, of which waited for: 13 -> 12; matrix products, arithmetic and copies ran while one was open for 2% -> 6% of each run, Pallas kernels for 18% -> 18%
where the time goes in v5:
time: 108 us; the launch traced here: 106 us
  starting transfers between devices  41.2 us (38%)
  waiting for transfers between devices  30.1 us (28%)
  Pallas kernels  22.7 us (21%)
  local copies, waits for them, and re-layouts  9.73 us (9%)
  other arithmetic  1.29 us (1%)
    ppermute x15, starting transfers between devices, turn(): return lax.ppermute(part, 'rows', pairs)  21.5 us
    ppermute x15, waiting for transfers between devices, turn(): return lax.ppermute(part, 'rows', pairs)  19 us
    ppermute x7, starting transfers between devices, move(): return lax.ppermute(part, 'rows', pairs)  14.7 us
    unnamed x43, local copies, waits for them, and re-layouts  8.9 us
    pallas_call x1, Pallas kernels, update(): pl.pallas_call(functools.partial(update_kernel, line, first), out_shape=j...  7.32 us
    pallas_call x3, Pallas kernels, products(): pl.pallas_call(functools.partial(products_kernel, len(parts)), out_shape=...  6.32 us
    ppermute x1, waiting for transfers between devices, shards(): following = lax.ppermute(diag, 'tm', [(i + 1, i) for i in range(size - 1)])  6.19 us
    pallas_call x1, Pallas kernels, factor_rows(): pl.pallas_call(functools.partial(factor_kernel, line, first), out_shape=j...  4.24 us
  transfers between devices with their start and end apart: 26, of which 12 were waited for; matrix products, arithmetic and copies ran while one was open for 6% of the time, Pallas kernels for 18%

profile of v5, /device:TPU:0, one launch (start us, length us, event | category | flops | bytes accessed | tf_op | source)
XLA Modules:
  0.0 105.8 jit_solution(4720553482779363360)
XLA Ops:
  0.6 5.1 %collective-permute-start = (bf16[512,128]{1,0:T(8,128)(2,1)}, bf16[512,128]{1,0:T(8,128)(2,1)S(1)}, u32[]{:S(2)}, u32[]{:S(2)}) collective-permute-start(bf16[512,128]{1,0:T(8,128)(2,1)} %bitcast.19), channel_id=1, source_target_pairs={{0,12},{1,13},{2,14},{3,15},{4,0},{5,1},{6,2},{7,3},{8,4},{9,5},{1... | collective-permute-start | bytes 393224 | tf_op jit(solution)/shard_map/ppermute | solution.py:49
  5.7 1.5 %collective-permute-start.2 = (bf16[512,128]{1,0:T(8,128)(2,1)}, bf16[512,128]{1,0:T(8,128)(2,1)S(1)}, u32[]{:S(2)}, u32[]{:S(2)}) collective-permute-start(bf16[512,128]{1,0:T(8,128)(2,1)} %bitcast.21), channel_id=1, source_target_pairs={{0,2},{1,3},{2,0},{3,1},{4,6},{5,7},{6,4},{7,5},{8,10},{9,11},{10,... | collective-permute-start | bytes 393224 | tf_op jit(solution)/shard_map/ppermute | solution.py:49
  7.3 2.0 %collective-permute-start.8 = (bf16[128,2048]{1,0:T(8,128)(2,1)}, bf16[128,2048]{1,0:T(8,128)(2,1)S(1)}, u32[]{:S(2)}, u32[]{:S(2)}) collective-permute-start(bf16[128,2048]{1,0:T(8,128)(2,1)} %bitcast.12), channel_id=1, source_target_pairs={{0,2},{1,3},{4,0},{5,1},{8,4},{9,5},{12,8},{13,9},{14,12},{15,13},... | collective-permute-start | bytes 1572872 | tf_op jit(solution)/shard_map/ppermute | solution.py:40
  9.3 0.7 fusion.2
  10.0 0.8 copy.9.pos_ref
  10.7 1.0 copy-done.8
  11.8 1.6 %shard_map.86 = bf16[16,144,128]{2,1,0:T(8,128)(2,1)} custom-call(s32[4,2]{1,0:T(4,128)S(1)} %copy.9.pos_ref, bf16[128,2048]{1,0:T(8,128)(2,1)S(1)} %bitcast.16), custom_call_target="tpu_custom_call" | custom-call | bytes 128 | tf_op jit(solution)/shard_map/pallas_call | solution.py:75
  14.0 3.9 %collective-permute-start.3 = (bf16[512,128]{1,0:T(8,128)(2,1)S(1)}, bf16[512,128]{1,0:T(8,128)(2,1)}, u32[]{:S(2)}, u32[]{:S(2)}) collective-permute-start(bf16[512,128]{1,0:T(8,128)(2,1)S(1)} %collective-permute-done), channel_id=1, source_target_pairs={{0,12},{1,13},{2,14},{3,15},{4,0},{5,1},{6,2},{7,3},{8,4},{9,5},{1... | collective-permute-start | bytes 393224 | tf_op jit(solution)/shard_map/ppermute | solution.py:49
  17.8 0.9 constant_dynamic-update-slice_fusion.7
  19.3 1.5 %collective-permute-start.5 = (bf16[512,128]{1,0:T(8,128)(2,1)}, bf16[512,128]{1,0:T(8,128)(2,1)}, u32[]{:S(2)}, u32[]{:S(2)}) collective-permute-start(bf16[512,128]{1,0:T(8,128)(2,1)} %collective-permute-done.1), channel_id=1, source_target_pairs={{0,2},{1,3},{2,0},{3,1},{4,6},{5,7},{6,4},{7,5},{8,10},{9,11},{10,... | collective-permute-start | bytes 393224 | tf_op jit(solution)/shard_map/ppermute | solution.py:49
  20.9 3.6 %all-to-all-start = ((bf16[16,144,128]{2,1,0:T(8,128)(2,1)}), bf16[16,144,128]{2,1,0:T(8,128)(2,1)S(1)}, u32[]{:S(2)}, u32[]{:S(2)}) async-start(bf16[16,144,128]{2,1,0:T(8,128)(2,1)} %shard_map.86), calls=%async_computation | async-start | bytes 1179648 | tf_op jit(solution)/shard_map/all_to_all | solution.py:334
  24.5 1.8 %collective-permute-done.3 = bf16[512,128]{1,0:T(8,128)(2,1)} collective-permute-done((bf16[512,128]{1,0:T(8,128)(2,1)S(1)}, bf16[512,128]{1,0:T(8,128)(2,1)}, u32[]{:S(2)}, u32[]{:S(2)}) %collective-permute-start.3) | collective-permute-done | bytes 131104 | tf_op jit(solution)/shard_map/ppermute | solution.py:49
  26.3 1.3 %collective-permute-start.9 = (bf16[128,2048]{1,0:T(8,128)(2,1)S(1)}, bf16[128,2048]{1,0:T(8,128)(2,1)S(1)}, u32[]{:S(2)}, u32[]{:S(2)}) collective-permute-start(bf16[128,2048]{1,0:T(8,128)(2,1)S(1)} %bitcast.18), channel_id=1, source_target_pairs={{16,0},{17,1},{18,2},{19,3},{20,4},{21,5},{22,6},{23,7},{24,8},{25... | collective-permute-start | bytes 1572872 | tf_op jit(solution)/shard_map/ppermute | solution.py:327
  27.6 0.9 constant_dynamic-update-slice_fusion.5
  28.5 2.2 %collective-permute-start.6 = (bf16[512,128]{1,0:T(8,128)(2,1)}, bf16[512,128]{1,0:T(8,128)(2,1)S(1)}, u32[]{:S(2)}, u32[]{:S(2)}) collective-permute-start(bf16[512,128]{1,0:T(8,128)(2,1)} %collective-permute-done.3), channel_id=1, source_target_pairs={{0,2},{1,3},{2,0},{3,1},{4,6},{5,7},{6,4},{7,5},{8,10},{9,11},{10,... | collective-permute-start | bytes 393224 | tf_op jit(solution)/shard_map/ppermute | solution.py:49
  30.7 1.0 constant_dynamic-update-slice_fusion.4
  31.7 0.9 constant_dynamic-update-slice_fusion.2
  32.6 0.9 constant_dynamic-update-slice_fusion.1
  33.5 1.7 %collective-permute-done.6 = bf16[512,128]{1,0:T(8,128)(2,1)S(1)} collective-permute-done((bf16[512,128]{1,0:T(8,128)(2,1)}, bf16[512,128]{1,0:T(8,128)(2,1)S(1)}, u32[]{:S(2)}, u32[]{:S(2)}) %collective-permute-start.6) | collective-permute-done | bytes 131104 | tf_op jit(solution)/shard_map/ppermute | solution.py:49
  35.2 6.2 %collective-permute-done.9.next_in = bf16[128,2048]{1,0:T(8,128)(2,1)S(1)} collective-permute-done((bf16[128,2048]{1,0:T(8,128)(2,1)S(1)}, bf16[128,2048]{1,0:T(8,128)(2,1)S(1)}, u32[]{:S(2)}, u32[]{:S(2)}) %collective-permute-start.9) | collective-permute-done | bytes 524320 | tf_op jit(solution)/shard_map/ppermute | solution.py:327
  41.5 1.2 %collective-permute-start.11 = (bf16[128,2048]{1,0:T(8,128)(2,1)}, bf16[128,2048]{1,0:T(8,128)(2,1)}, u32[]{:S(2)}, u32[]{:S(2)}) collective-permute-start(bf16[128,2048]{1,0:T(8,128)(2,1)} %copy-done.9), channel_id=1, source_target_pairs={{0,4},{1,5},{4,8},{5,9},{8,12},{9,13},{12,14},{13,15},{14,10},{15,... | collective-permute-start | bytes 1572872 | tf_op jit(solution)/shard_map/ppermute | solution.py:40
  42.7 0.9 collective-permute-start.12
  44.4 1.0 copy-done.5
  45.4 7.3 %shard_map.87.refs_5_.refs_2_ = bf16[256,2048]{1,0:T(8,128)(2,1)} custom-call(s32[10]{0:T(128)} %pad_add_fusion.place_ref, bf16[4096,128]{1,0:T(8,128)(2,1)} %copy-done.3, bf16[4096,128]{1,0:T(8,128)(2,1)} %copy-done.5, bf16[16,144,128]{2,1,0:T(8,128)(2,1)} %copy-done.1, bf16[128,2048]{1,0:T(8,128)(2,1)} %bitcast.17, bf16[128,2048]{1,0:T(8,128)(2,1)} %bitcast.15, ...), custom_call_target="tpu_custom_call" | custom-call | bytes 128 | tf_op jit(solution)/shard_map/pallas_call | solution.py:168
  52.8 3.4 %collective-permute-done.11.refs_3_ = bf16[128,2048]{1,0:T(8,128)(2,1)} collective-permute-done((bf16[128,2048]{1,0:T(8,128)(2,1)}, bf16[128,2048]{1,0:T(8,128)(2,1)}, u32[]{:S(2)}, u32[]{:S(2)}) %collective-permute-start.11) | collective-permute-done | bytes 524320 | tf_op jit(solution)/shard_map/ppermute | solution.py:40
  56.2 0.9 collective-permute-done.12.refs_4_
  57.0 1.6 %collective-permute-start.16 = (bf16[128,2048]{1,0:T(8,128)(2,1)}, bf16[128,2048]{1,0:T(8,128)(2,1)S(1)}, u32[]{:S(2)}, u32[]{:S(2)}) collective-permute-start(bf16[128,2048]{1,0:T(8,128)(2,1)} %collective-permute-done.11.refs_3_), channel_id=1, source_target_pairs={{0,4},{1,5},{4,8},{5,9},{8,12},{9,13},{12,14},{13,15},{14,10},{15,... | collective-permute-start | bytes 1572872 | tf_op jit(solution)/shard_map/ppermute | solution.py:40
  59.1 0.8 collective-permute-done.13.refs_6_.refs_3_
  59.9 1.2 %copy-done = bf16[256,2048]{1,0:T(8,128)(2,1)S(1)} copy-done((bf16[256,2048]{1,0:T(8,128)(2,1)S(1)}, bf16[256,2048]{1,0:T(8,128)(2,1)}, u32[]{:S(2)}) %copy-start) | copy-done | bytes 1048600
  61.1 3.4 %shard_map.88 = (bf16[128,512]{1,0:T(8,128)(2,1)S(1)}, bf16[128,512]{1,0:T(8,128)(2,1)S(1)}, bf16[128,512]{1,0:T(8,128)(2,1)S(1)}, bf16[128,512]{1,0:T(8,128)(2,1)}, bf16[128,512]{1,0:T(8,128)(2,1)}) custom-call(bf16[128,2048]{1,0:T(8,128)(2,1)S(1)} %bitcast.13, bf16[128,2048]{1,0:T(8,128)(2,1)S(1)} %copy-done.10, bf16[128,2048]{1,0:T(8,128)(2,1)S(1)} %copy-done.12, ...), custom_call_target="tpu_custom_call" | custom-call | bytes 512 | tf_op jit(solution)/shard_map/pallas_call | solution.py:254
  64.6 0.9 collective-permute-start.14
  65.4 1.1 %collective-permute-start.15 = (bf16[128,512]{1,0:T(8,128)(2,1)S(1)}, bf16[128,512]{1,0:T(8,128)(2,1)S(1)}, u32[]{:S(2)}, u32[]{:S(2)}) collective-permute-start(bf16[128,512]{1,0:T(8,128)(2,1)S(1)} %get-tuple-element.47), channel_id=1, source_target_pairs={{0,4},{1,5},{4,8},{5,9},{8,12},{9,13},{12,14},{13,15},{14,10},{15,... | collective-permute-start | bytes 393224 | tf_op jit(solution)/shard_map/ppermute | solution.py:40
  66.6 5.4 %collective-permute-done.16.refs_0_ = bf16[128,2048]{1,0:T(8,128)(2,1)S(1)} collective-permute-done((bf16[128,2048]{1,0:T(8,128)(2,1)}, bf16[128,2048]{1,0:T(8,128)(2,1)S(1)}, u32[]{:S(2)}, u32[]{:S(2)}) %collective-permute-start.16) | collective-permute-done | bytes 524320 | tf_op jit(solution)/shard_map/ppermute | solution.py:40
  72.0 1.6 %collective-permute-done.17.refs_1_ = bf16[128,2048]{1,0:T(8,128)(2,1)S(1)} collective-permute-done((bf16[128,2048]{1,0:T(8,128)(2,1)}, bf16[128,2048]{1,0:T(8,128)(2,1)S(1)}, u32[]{:S(2)}, u32[]{:S(2)}) %collective-permute-start.17) | collective-permute-done | bytes 524320 | tf_op jit(solution)/shard_map/ppermute | solution.py:40
  73.6 2.1 %collective-permute-done.14.refs_1_ = bf16[128,512]{1,0:T(8,128)(2,1)S(1)} collective-permute-done((bf16[128,512]{1,0:T(8,128)(2,1)S(1)}, bf16[128,512]{1,0:T(8,128)(2,1)S(1)}, u32[]{:S(2)}, u32[]{:S(2)}) %collective-permute-start.14) | collective-permute-done | bytes 131104 | tf_op jit(solution)/shard_map/ppermute | solution.py:40
  75.7 0.7 copy-done.13
  76.3 1.8 %collective-permute-start.20 = (bf16[64,2048]{1,0:T(8,128)(2,1)S(1)}, bf16[64,2048]{1,0:T(8,128)(2,1)S(1)}, u32[]{:S(2)}, u32[]{:S(2)}) collective-permute-start(bf16[64,2048]{1,0:T(8,128)(2,1)S(1)} %slice.6), channel_id=1, source_target_pairs={{0,4},{1,5},{4,8},{5,9},{8,12},{9,13},{12,14},{13,15},{14,10},{15,... | collective-permute-start | bytes 786440 | tf_op jit(solution)/shard_map/ppermute | solution.py:40
  78.5 0.8 collective-permute-start.18
  79.3 2.1 %collective-permute-start.24 = (bf16[128,512]{1,0:T(8,128)(2,1)}, bf16[128,512]{1,0:T(8,128)(2,1)}, u32[]{:S(2)}, u32[]{:S(2)}) collective-permute-start(bf16[128,512]{1,0:T(8,128)(2,1)} %get-tuple-element.54), channel_id=1, source_target_pairs={{0,8},{1,9},{4,12},{5,13},{8,14},{9,15},{12,10},{13,11},{14,6},{15... | collective-permute-start | bytes 393224 | tf_op jit(solution)/shard_map/ppermute | solution.py:40
  81.4 1.4 %shard_map.89 = (bf16[128,512]{1,0:T(8,128)(2,1)}, bf16[128,512]{1,0:T(8,128)(2,1)}) custom-call(bf16[128,2048]{1,0:T(8,128)(2,1)S(1)} %collective-permute-done.16.refs_0_, bf16[128,2048]{1,0:T(8,128)(2,1)S(1)} %collective-permute-done.17.refs_1_, bf16[256,2048]{1,0:T(8,128)(2,1)S(1)} %copy-done, bf16[256,2048]{1,0:T(8,128)(2,1)S(1)} %collective-permute-done.13.refs_6_.refs_3_), custom_call_target="tpu_custom_call" | custom-call | bytes 512 | tf_op jit(solution)/shard_map/pallas_call | solution.py:254
  82.8 1.1 collective-permute-start.19
  83.9 1.0 collective-permute-done.20.refs_0_
  84.9 4.7 %collective-permute-start.23 = (bf16[128,512]{1,0:T(8,128)(2,1)}, bf16[128,512]{1,0:T(8,128)(2,1)}, u32[]{:S(2)}, u32[]{:S(2)}) collective-permute-start(bf16[128,512]{1,0:T(8,128)(2,1)} %get-tuple-element.53), channel_id=1, source_target_pairs={{0,12},{1,13},{4,14},{5,15},{8,10},{9,11},{12,6},{13,7},{14,2},{15... | collective-permute-start | bytes 393224 | tf_op jit(solution)/shard_map/ppermute | solution.py:40
  89.6 1.5 %shard_map.90 = bf16[128,512]{1,0:T(8,128)(2,1)} custom-call(bf16[64,2048]{1,0:T(8,128)(2,1)S(1)} %collective-permute-done.20.refs_0_, bf16[64,2048]{1,0:T(8,128)(2,1)S(1)} %collective-permute-done.21.refs_1_, bf16[256,2048]{1,0:T(8,128)(2,1)S(1)} %copy-done, bf16[256,2048]{1,0:T(8,128)(2,1)S(1)} %collective-permute-done.13.refs_6_.refs_3_), custom_call_target="tpu_custom_call" | custom-call | bytes 512 | tf_op jit(solution)/shard_map/pallas_call | solution.py:254
  91.1 2.6 %collective-permute-start.22 = (bf16[128,512]{1,0:T(8,128)(2,1)}, bf16[128,512]{1,0:T(8,128)(2,1)}, u32[]{:S(2)}, u32[]{:S(2)}) collective-permute-start(bf16[128,512]{1,0:T(8,128)(2,1)} %shard_map.90), channel_id=1, source_target_pairs={{0,14},{1,15},{4,10},{5,11},{8,6},{9,7},{12,2},{13,3},{14,0},{15,1... | collective-permute-start | bytes 393224 | tf_op jit(solution)/shard_map/ppermute | solution.py:40
  93.7 4.2 %shard_map.91.refs_8_ = bf16[128,4096]{1,0:T(8,128)(2,1)S(1)} custom-call(s32[10]{0:T(128)S(1)} %copy-done.15, bf16[4096,128]{1,0:T(8,128)(2,1)S(1)} %copy-done.4, bf16[4096,128]{1,0:T(8,128)(2,1)S(1)} %copy-done.6, bf16[16,144,128]{2,1,0:T(8,128)(2,1)S(1)} %copy-done.2, bf16[128,2048]{1,0:T(8,128)(2,1)S(1)} %bitcast.14), custom_call_target="tpu_custom_call" | custom-call | bytes 128 | tf_op jit(solution)/shard_map/pallas_call | solution.py:218
  98.0 4.6 %collective-permute-done.18.refs_2_ = bf16[128,512]{1,0:T(8,128)(2,1)} collective-permute-done((bf16[128,512]{1,0:T(8,128)(2,1)}, bf16[128,512]{1,0:T(8,128)(2,1)}, u32[]{:S(2)}, u32[]{:S(2)}) %collective-permute-start.18) | collective-permute-done | bytes 131104 | tf_op jit(solution)/shard_map/ppermute | solution.py:40
  102.6 3.2 %shard_map.92 = (f32[128,4096]{1,0:T(8,128)}, f32[128,128]{1,0:T(8,128)}) custom-call(s32[10]{0:T(128)S(1)} %copy-done.15, bf16[128,512]{1,0:T(8,128)(2,1)S(1)} %get-tuple-element.45.refs_0_, bf16[128,512]{1,0:T(8,128)(2,1)S(1)} %collective-permute-done.14.refs_1_, bf16[128,512]{1,0:T(8,128)(2,1)} %collective-permute-done.18.refs_2_, ...), custom_call_target="tpu_custom_call" | custom-call | bytes 128 | tf_op jit(solution)/shard_map/pallas_call | solution.py:289
  (61 shorter events, 3.1 us)
Async XLA Ops:
  0.6 13.3 %collective-permute-start = (bf16[512,128]{1,0:T(8,128)(2,1)}, bf16[512,128]{1,0:T(8,128)(2,1)S(1)}, u32[]{:S(2)}, u32[]{:S(2)}) collective-permute-start(bf16[512,128]{1,0:T(8,128)(2,1)} %bitcast.19), channel_id=1, source_target_pairs={{0,12},{1,13},{2,14},{3,15},{4,0},{5,1},{6,2},{7,3},{8,4},{9,5},{1... | collective-permute-start | bytes 393224 | tf_op jit(solution)/shard_map/ppermute | solution.py:49
  5.7 8.2 %collective-permute-start.1 = (bf16[512,128]{1,0:T(8,128)(2,1)}, bf16[512,128]{1,0:T(8,128)(2,1)}, u32[]{:S(2)}, u32[]{:S(2)}) collective-permute-start(bf16[512,128]{1,0:T(8,128)(2,1)} %bitcast.20), channel_id=1, source_target_pairs={{0,4},{1,5},{2,6},{3,7},{4,8},{5,9},{6,10},{7,11},{8,12},{9,13},{1... | collective-permute-start | bytes 393224 | tf_op jit(solution)/shard_map/ppermute | solution.py:49
  5.7 8.2 %collective-permute-start.2 = (bf16[512,128]{1,0:T(8,128)(2,1)}, bf16[512,128]{1,0:T(8,128)(2,1)S(1)}, u32[]{:S(2)}, u32[]{:S(2)}) collective-permute-start(bf16[512,128]{1,0:T(8,128)(2,1)} %bitcast.21), channel_id=1, source_target_pairs={{0,2},{1,3},{2,0},{3,1},{4,6},{5,7},{6,4},{7,5},{8,10},{9,11},{10,... | collective-permute-start | bytes 393224 | tf_op jit(solution)/shard_map/ppermute | solution.py:49
  7.3 27.9 %collective-permute-start.7 = (bf16[128,2048]{1,0:T(8,128)(2,1)}, bf16[128,2048]{1,0:T(8,128)(2,1)S(1)}, u32[]{:S(2)}, u32[]{:S(2)}) collective-permute-start(bf16[128,2048]{1,0:T(8,128)(2,1)} %bitcast.11), channel_id=1, source_target_pairs={{0,4},{1,5},{4,8},{5,9},{8,12},{9,13},{12,14},{13,15},{14,10},{15,... | collective-permute-start | bytes 1572872 | tf_op jit(solution)/shard_map/ppermute | solution.py:40
  7.3 27.9 %collective-permute-start.8 = (bf16[128,2048]{1,0:T(8,128)(2,1)}, bf16[128,2048]{1,0:T(8,128)(2,1)S(1)}, u32[]{:S(2)}, u32[]{:S(2)}) collective-permute-start(bf16[128,2048]{1,0:T(8,128)(2,1)} %bitcast.12), channel_id=1, source_target_pairs={{0,2},{1,3},{4,0},{5,1},{8,4},{9,5},{12,8},{13,9},{14,12},{15,13},... | collective-permute-start | bytes 1572872 | tf_op jit(solution)/shard_map/ppermute | solution.py:40
  10.7 1.0 copy-start.8
  11.8 14.5 %copy-start.16 = (bf16[1,128,2048]{2,1,0:T(8,128)(2,1)S(1)}, bf16[1,128,2048]{2,1,0:T(8,128)(2,1)}, u32[]{:S(2)}) copy-start(bf16[1,128,2048]{2,1,0:T(8,128)(2,1)} %param.10) | copy-start | bytes 1572868
  14.0 12.3 %collective-permute-start.3 = (bf16[512,128]{1,0:T(8,128)(2,1)S(1)}, bf16[512,128]{1,0:T(8,128)(2,1)}, u32[]{:S(2)}, u32[]{:S(2)}) collective-permute-start(bf16[512,128]{1,0:T(8,128)(2,1)S(1)} %collective-permute-done), channel_id=1, source_target_pairs={{0,12},{1,13},{2,14},{3,15},{4,0},{5,1},{6,2},{7,3},{8,4},{9,5},{1... | collective-permute-start | bytes 393224 | tf_op jit(solution)/shard_map/ppermute | solution.py:49
  18.8 9.8 %collective-permute-start.4 = (bf16[512,128]{1,0:T(8,128)(2,1)S(1)}, bf16[512,128]{1,0:T(8,128)(2,1)}, u32[]{:S(2)}, u32[]{:S(2)}) collective-permute-start(bf16[512,128]{1,0:T(8,128)(2,1)S(1)} %collective-permute-done), channel_id=1, source_target_pairs={{0,2},{1,3},{2,0},{3,1},{4,6},{5,7},{6,4},{7,5},{8,10},{9,11},{10,... | collective-permute-start | bytes 393224 | tf_op jit(solution)/shard_map/ppermute | solution.py:49
  19.3 9.2 %collective-permute-start.5 = (bf16[512,128]{1,0:T(8,128)(2,1)}, bf16[512,128]{1,0:T(8,128)(2,1)}, u32[]{:S(2)}, u32[]{:S(2)}) collective-permute-start(bf16[512,128]{1,0:T(8,128)(2,1)} %collective-permute-done.1), channel_id=1, source_target_pairs={{0,2},{1,3},{2,0},{3,1},{4,6},{5,7},{6,4},{7,5},{8,10},{9,11},{10,... | collective-permute-start | bytes 393224 | tf_op jit(solution)/shard_map/ppermute | solution.py:49
  20.9 22.8 %all-to-all-start = ((bf16[16,144,128]{2,1,0:T(8,128)(2,1)}), bf16[16,144,128]{2,1,0:T(8,128)(2,1)S(1)}, u32[]{:S(2)}, u32[]{:S(2)}) async-start(bf16[16,144,128]{2,1,0:T(8,128)(2,1)} %shard_map.86), calls=%async_computation | async-start | bytes 1179648 | tf_op jit(solution)/shard_map/all_to_all | solution.py:334
  26.3 15.1 %collective-permute-start.9 = (bf16[128,2048]{1,0:T(8,128)(2,1)S(1)}, bf16[128,2048]{1,0:T(8,128)(2,1)S(1)}, u32[]{:S(2)}, u32[]{:S(2)}) collective-permute-start(bf16[128,2048]{1,0:T(8,128)(2,1)S(1)} %bitcast.18), channel_id=1, source_target_pairs={{16,0},{17,1},{18,2},{19,3},{20,4},{21,5},{22,6},{23,7},{24,8},{25... | collective-permute-start | bytes 1572872 | tf_op jit(solution)/shard_map/ppermute | solution.py:327
  28.5 6.7 %collective-permute-start.6 = (bf16[512,128]{1,0:T(8,128)(2,1)}, bf16[512,128]{1,0:T(8,128)(2,1)S(1)}, u32[]{:S(2)}, u32[]{:S(2)}) collective-permute-start(bf16[512,128]{1,0:T(8,128)(2,1)} %collective-permute-done.3), channel_id=1, source_target_pairs={{0,2},{1,3},{2,0},{3,1},{4,6},{5,7},{6,4},{7,5},{8,10},{9,11},{10,... | collective-permute-start | bytes 393224 | tf_op jit(solution)/shard_map/ppermute | solution.py:49
  35.2 6.2 %copy-start.9 = (bf16[128,2048]{1,0:T(8,128)(2,1)}, bf16[128,2048]{1,0:T(8,128)(2,1)S(1)}, u32[]{:S(2)}) copy-start(bf16[128,2048]{1,0:T(8,128)(2,1)S(1)} %collective-permute-done.7.refs_1_) | copy-start | bytes 1572868
  35.2 6.2 %copy-start.11 = (bf16[128,2048]{1,0:T(8,128)(2,1)}, bf16[128,2048]{1,0:T(8,128)(2,1)S(1)}, u32[]{:S(2)}) copy-start(bf16[128,2048]{1,0:T(8,128)(2,1)S(1)} %collective-permute-done.8.refs_2_) | copy-start | bytes 1572868
  41.4 1.3 %copy-start.17 = (bf16[128,2048]{1,0:T(8,128)(2,1)}, bf16[128,2048]{1,0:T(8,128)(2,1)S(1)}, u32[]{:S(2)}) copy-start(bf16[128,2048]{1,0:T(8,128)(2,1)S(1)} %collective-permute-done.9.next_in) | copy-start | bytes 1572868
  41.4 2.8 %copy-start.3 = (bf16[4096,128]{1,0:T(8,128)(2,1)}, bf16[4096,128]{1,0:T(8,128)(2,1)S(1)}, u32[]{:S(2)}) copy-start(bf16[4096,128]{1,0:T(8,128)(2,1)S(1)} %constant_dynamic-update-slice_fusion.near_ref) | copy-start | bytes 3145732
  41.4 18.5 %copy-start.7 = (bf16[1,128,2048]{2,1,0:T(8,128)(2,1)S(1)}, bf16[1,128,2048]{2,1,0:T(8,128)(2,1)}, u32[]{:S(2)}) copy-start(bf16[1,128,2048]{2,1,0:T(8,128)(2,1)} %param.7) | copy-start | bytes 1572868
  41.5 2.7 %collective-permute-start.10 = (bf16[4096,128]{1,0:T(8,128)(2,1)S(1)}, bf16[4096,128]{1,0:T(8,128)(2,1)S(1)}, u32[]{:S(2)}, u32[]{:S(2)}) collective-permute-start(bf16[4096,128]{1,0:T(8,128)(2,1)S(1)} %constant_dynamic-update-slice_fusion.near_ref), channel_id=1, source_target_pairs={{0,1},{1,0},{2,3},{3,2},{4,5},{5,4},{6,7},{7,6},{8,9},{9,8},{10,11... | collective-permute-start | bytes 3145736 | tf_op jit(solution)/shard_map/ppermute | solution.py:53
  41.5 14.6 %collective-permute-start.11 = (bf16[128,2048]{1,0:T(8,128)(2,1)}, bf16[128,2048]{1,0:T(8,128)(2,1)}, u32[]{:S(2)}, u32[]{:S(2)}) collective-permute-start(bf16[128,2048]{1,0:T(8,128)(2,1)} %copy-done.9), channel_id=1, source_target_pairs={{0,4},{1,5},{4,8},{5,9},{8,12},{9,13},{12,14},{13,15},{14,10},{15,... | collective-permute-start | bytes 1572872 | tf_op jit(solution)/shard_map/ppermute | solution.py:40
  42.7 14.3 %collective-permute-start.12 = (bf16[128,2048]{1,0:T(8,128)(2,1)}, bf16[128,2048]{1,0:T(8,128)(2,1)}, u32[]{:S(2)}, u32[]{:S(2)}) collective-permute-start(bf16[128,2048]{1,0:T(8,128)(2,1)} %copy-done.11), channel_id=1, source_target_pairs={{0,2},{1,3},{4,0},{5,1},{8,4},{9,5},{12,8},{13,9},{14,12},{15,13},... | collective-permute-start | bytes 1572872 | tf_op jit(solution)/shard_map/ppermute | solution.py:40
  43.6 0.8 copy-start.1
  43.6 16.3 %copy-start.10 = (bf16[128,2048]{1,0:T(8,128)(2,1)S(1)}, bf16[128,2048]{1,0:T(8,128)(2,1)}, u32[]{:S(2)}) copy-start(bf16[128,2048]{1,0:T(8,128)(2,1)} %copy-done.9) | copy-start | bytes 1572868
  43.6 16.3 %copy-start.12 = (bf16[128,2048]{1,0:T(8,128)(2,1)S(1)}, bf16[128,2048]{1,0:T(8,128)(2,1)}, u32[]{:S(2)}) copy-start(bf16[128,2048]{1,0:T(8,128)(2,1)} %copy-done.11) | copy-start | bytes 1572868
  44.4 1.0 copy-start.5
  57.0 2.9 %collective-permute-start.13 = (bf16[256,2048]{1,0:T(8,128)(2,1)}, bf16[256,2048]{1,0:T(8,128)(2,1)S(1)}, u32[]{:S(2)}, u32[]{:S(2)}) collective-permute-start(bf16[256,2048]{1,0:T(8,128)(2,1)} %shard_map.87.refs_5_.refs_2_), channel_id=1, source_target_pairs={{0,1},{1,0},{2,3},{3,2},{4,5},{5,4},{6,7},{7,6},{8,9},{9,8},{10,11... | collective-permute-start | bytes 3145736 | tf_op jit(solution)/shard_map/ppermute | solution.py:53
  57.0 14.9 %collective-permute-start.16 = (bf16[128,2048]{1,0:T(8,128)(2,1)}, bf16[128,2048]{1,0:T(8,128)(2,1)S(1)}, u32[]{:S(2)}, u32[]{:S(2)}) collective-permute-start(bf16[128,2048]{1,0:T(8,128)(2,1)} %collective-permute-done.11.refs_3_), channel_id=1, source_target_pairs={{0,4},{1,5},{4,8},{5,9},{8,12},{9,13},{12,14},{13,15},{14,10},{15,... | collective-permute-start | bytes 1572872 | tf_op jit(solution)/shard_map/ppermute | solution.py:40
  58.6 15.0 %collective-permute-start.17 = (bf16[128,2048]{1,0:T(8,128)(2,1)}, bf16[128,2048]{1,0:T(8,128)(2,1)S(1)}, u32[]{:S(2)}, u32[]{:S(2)}) collective-permute-start(bf16[128,2048]{1,0:T(8,128)(2,1)} %collective-permute-done.12.refs_4_), channel_id=1, source_target_pairs={{0,2},{1,3},{4,0},{5,1},{8,4},{9,5},{12,8},{13,9},{14,12},{15,13},... | collective-permute-start | bytes 1572872 | tf_op jit(solution)/shard_map/ppermute | solution.py:40
  59.9 1.2 %copy-start = (bf16[256,2048]{1,0:T(8,128)(2,1)S(1)}, bf16[256,2048]{1,0:T(8,128)(2,1)}, u32[]{:S(2)}) copy-start(bf16[256,2048]{1,0:T(8,128)(2,1)} %shard_map.87.refs_5_.refs_2_) | copy-start | bytes 3145732
  64.6 11.1 %collective-permute-start.14 = (bf16[128,512]{1,0:T(8,128)(2,1)S(1)}, bf16[128,512]{1,0:T(8,128)(2,1)S(1)}, u32[]{:S(2)}, u32[]{:S(2)}) collective-permute-start(bf16[128,512]{1,0:T(8,128)(2,1)S(1)} %get-tuple-element.46), channel_id=1, source_target_pairs={{0,2},{1,3},{4,0},{5,1},{8,4},{9,5},{12,8},{13,9},{14,12},{15,13},... | collective-permute-start | bytes 393224 | tf_op jit(solution)/shard_map/ppermute | solution.py:40
  65.4 10.2 %collective-permute-start.15 = (bf16[128,512]{1,0:T(8,128)(2,1)S(1)}, bf16[128,512]{1,0:T(8,128)(2,1)S(1)}, u32[]{:S(2)}, u32[]{:S(2)}) collective-permute-start(bf16[128,512]{1,0:T(8,128)(2,1)S(1)} %get-tuple-element.47), channel_id=1, source_target_pairs={{0,4},{1,5},{4,8},{5,9},{8,12},{9,13},{12,14},{13,15},{14,10},{15,... | collective-permute-start | bytes 393224 | tf_op jit(solution)/shard_map/ppermute | solution.py:40
  75.7 0.7 copy-start.13
  76.3 8.6 %collective-permute-start.20 = (bf16[64,2048]{1,0:T(8,128)(2,1)S(1)}, bf16[64,2048]{1,0:T(8,128)(2,1)S(1)}, u32[]{:S(2)}, u32[]{:S(2)}) collective-permute-start(bf16[64,2048]{1,0:T(8,128)(2,1)S(1)} %slice.6), channel_id=1, source_target_pairs={{0,4},{1,5},{4,8},{5,9},{8,12},{9,13},{12,14},{13,15},{14,10},{15,... | collective-permute-start | bytes 786440 | tf_op jit(solution)/shard_map/ppermute | solution.py:40
  78.2 11.4 %collective-permute-start.21 = (bf16[64,2048]{1,0:T(8,128)(2,1)S(1)}, bf16[64,2048]{1,0:T(8,128)(2,1)S(1)}, u32[]{:S(2)}, u32[]{:S(2)}) collective-permute-start(bf16[64,2048]{1,0:T(8,128)(2,1)S(1)} %slice.7), channel_id=1, source_target_pairs={{0,2},{1,3},{4,0},{5,1},{8,4},{9,5},{12,8},{13,9},{14,12},{15,13},... | collective-permute-start | bytes 786440 | tf_op jit(solution)/shard_map/ppermute | solution.py:40
  78.5 24.1 %collective-permute-start.18 = (bf16[128,512]{1,0:T(8,128)(2,1)}, bf16[128,512]{1,0:T(8,128)(2,1)}, u32[]{:S(2)}, u32[]{:S(2)}) collective-permute-start(bf16[128,512]{1,0:T(8,128)(2,1)} %get-tuple-element.49), channel_id=1, source_target_pairs={{0,6},{1,7},{4,2},{5,3},{8,0},{9,1},{12,4},{13,5},{14,8},{15,9},{1... | collective-permute-start | bytes 393224 | tf_op jit(solution)/shard_map/ppermute | solution.py:40
  79.3 23.3 %collective-permute-start.24 = (bf16[128,512]{1,0:T(8,128)(2,1)}, bf16[128,512]{1,0:T(8,128)(2,1)}, u32[]{:S(2)}, u32[]{:S(2)}) collective-permute-start(bf16[128,512]{1,0:T(8,128)(2,1)} %get-tuple-element.54), channel_id=1, source_target_pairs={{0,8},{1,9},{4,12},{5,13},{8,14},{9,15},{12,10},{13,11},{14,6},{15... | collective-permute-start | bytes 393224 | tf_op jit(solution)/shard_map/ppermute | solution.py:40
  82.8 10.8 %copy-start.2 = (bf16[16,144,128]{2,1,0:T(8,128)(2,1)S(1)}, bf16[16,144,128]{2,1,0:T(8,128)(2,1)}, u32[]{:S(2)}) copy-start(bf16[16,144,128]{2,1,0:T(8,128)(2,1)} %copy-done.1) | copy-start | bytes 1769476
  82.8 10.8 %copy-start.4 = (bf16[4096,128]{1,0:T(8,128)(2,1)S(1)}, bf16[4096,128]{1,0:T(8,128)(2,1)}, u32[]{:S(2)}) copy-start(bf16[4096,128]{1,0:T(8,128)(2,1)} %copy-done.3) | copy-start | bytes 3145732
  82.8 10.8 %copy-start.6 = (bf16[4096,128]{1,0:T(8,128)(2,1)S(1)}, bf16[4096,128]{1,0:T(8,128)(2,1)}, u32[]{:S(2)}) copy-start(bf16[4096,128]{1,0:T(8,128)(2,1)} %copy-done.5) | copy-start | bytes 3145732
  82.8 10.9 %copy-start.15 = (s32[10]{0:T(128)S(1)}, s32[10]{0:T(128)}, u32[]{:S(2)}) copy-start(s32[10]{0:T(128)} %pad_add_fusion.place_ref) | copy-start | bytes 124
  82.8 19.7 %collective-permute-start.19 = (bf16[128,512]{1,0:T(8,128)(2,1)}, bf16[128,512]{1,0:T(8,128)(2,1)}, u32[]{:S(2)}, u32[]{:S(2)}) collective-permute-start(bf16[128,512]{1,0:T(8,128)(2,1)} %get-tuple-element.52), channel_id=1, source_target_pairs={{0,10},{1,11},{4,6},{5,7},{8,2},{9,3},{12,0},{13,1},{14,4},{15,5},... | collective-permute-start | bytes 393224 | tf_op jit(solution)/shard_map/ppermute | solution.py:40
  84.9 17.7 %collective-permute-start.23 = (bf16[128,512]{1,0:T(8,128)(2,1)}, bf16[128,512]{1,0:T(8,128)(2,1)}, u32[]{:S(2)}, u32[]{:S(2)}) collective-permute-start(bf16[128,512]{1,0:T(8,128)(2,1)} %get-tuple-element.53), channel_id=1, source_target_pairs={{0,12},{1,13},{4,14},{5,15},{8,10},{9,11},{12,6},{13,7},{14,2},{15... | collective-permute-start | bytes 393224 | tf_op jit(solution)/shard_map/ppermute | solution.py:40
  91.1 11.5 %collective-permute-start.22 = (bf16[128,512]{1,0:T(8,128)(2,1)}, bf16[128,512]{1,0:T(8,128)(2,1)}, u32[]{:S(2)}, u32[]{:S(2)}) collective-permute-start(bf16[128,512]{1,0:T(8,128)(2,1)} %shard_map.90), channel_id=1, source_target_pairs={{0,14},{1,15},{4,10},{5,11},{8,6},{9,7},{12,2},{13,3},{14,0},{15,1... | collective-permute-start | bytes 393224 | tf_op jit(solution)/shard_map/ppermute | solution.py:40
  93.7 8.9 %copy-start.14 = (bf16[128,512]{1,0:T(8,128)(2,1)S(1)}, bf16[128,512]{1,0:T(8,128)(2,1)}, u32[]{:S(2)}) copy-start(bf16[128,512]{1,0:T(8,128)(2,1)} %copy-done.13) | copy-start | bytes 393220

commit v6 on v5

--- a/solution.py
+++ b/solution.py
@@ -324,7 +324,7 @@
     plain = tiles.reshape(-1, TILE)
     wahead, wbehind = [wrows, ring.turn(wrows, 1)], [wrows, ring.turn(wrows, -1)]
     second = [ring.turn(wahead[1], 1), ring.turn(wbehind[1], -1)]
-    following = lax.ppermute(diag, "tm", [(i + 1, i) for i in range(size - 1)])
+    following = lax.ppermute(diag, "tm", [((i + 1) % size, i) for i in range(size)])
     flipped = flip(tile_pos[0], cross)
     pieces = {0: plain, 1: ring.move(plain, -1), -1: ring.move(plain, 1)}
     sides = {0: ring.move(plain, 0, 1)}
@@ -356,6 +356,7 @@
         first, marks = 0, cols[:, rows:, :]
         cols = cols[:, :rows, :].reshape(width // TILE, TILE // rows, rows, rows)
         cols = cols.transpose(0, 2, 1, 3).reshape(width // TILE, rows, TILE)
+    following = jnp.where(lax.axis_index("tm") == size - 1, jnp.zeros_like(diag), following)
     updated = update(ring.line, first, place, near, far, marks, diag, cross, cols, following)
     updated, wahead[2], wbehind[2] = lax.optimization_barrier((updated, wahead[2], wbehind[2]))
     for step in range(3, steps):

time: 108 us -> 105 us (0.972)
  local copies, waits for them, and re-layouts: 9.73 us -> 5.96 us
    unnamed x43 -> x33, local copies, waits for them, and re-layouts: 8.9 us -> 5.13 us
    ppermute x7, waiting for transfers between devices: 3.51 us -> 6.2 us  [move(): return lax.ppermute(part, 'rows', pairs)]
    ppermute x1, waiting for transfers between devices: 6.19 us -> 4.5 us  [shards(): lax.ppermute(diag, 'tm', [((i + 1) % size, i) for i in range(size)])]
    ppermute x15, waiting for transfers between devices: 19 us -> 17.7 us  [turn(): return lax.ppermute(part, 'rows', pairs)]
  transfers between devices with their start and end apart: 26 -> 26, of which waited for: 12 -> 12; matrix products, arithmetic and copies ran while one was open for 6% -> 4% of each run, Pallas kernels for 18% -> 19%
where the time goes in v6:
time: 105 us; the launch traced here: 103 us
  starting transfers between devices  41.9 us (40%)
  waiting for transfers between devices  29.3 us (28%)
  Pallas kernels  23 us (22%)
  local copies, waits for them, and re-layouts  5.96 us (6%)
  other arithmetic  2.17 us (2%)
    ppermute x15, starting transfers between devices, turn(): return lax.ppermute(part, 'rows', pairs)  21.6 us
    ppermute x15, waiting for transfers between devices, turn(): return lax.ppermute(part, 'rows', pairs)  17.7 us
    ppermute x7, starting transfers between devices, move(): return lax.ppermute(part, 'rows', pairs)  15.2 us
    pallas_call x1, Pallas kernels, update(): pl.pallas_call(functools.partial(update_kernel, line, first), out_shape=j...  7.31 us
    pallas_call x3, Pallas kernels, products(): pl.pallas_call(functools.partial(products_kernel, len(parts)), out_shape=...  6.62 us
    ppermute x7, waiting for transfers between devices, move(): return lax.ppermute(part, 'rows', pairs)  6.2 us
    unnamed x33, local copies, waits for them, and re-layouts  5.13 us
    ppermute x1, waiting for transfers between devices, shards(): lax.ppermute(diag, 'tm', [((i + 1) % size, i) for i in range(size)])  4.5 us
  transfers between devices with their start and end apart: 26, of which 12 were waited for; matrix products, arithmetic and copies ran while one was open for 4% of the time, Pallas kernels for 19%

profile of v6, /device:TPU:0, one launch (start us, length us, event | category | flops | bytes accessed | tf_op | source)
XLA Modules:
  0.0 103.2 jit_solution(6627341830922792728)
XLA Ops:
  0.6 5.1 %collective-permute-start = (bf16[512,128]{1,0:T(8,128)(2,1)}, bf16[512,128]{1,0:T(8,128)(2,1)S(1)}, u32[]{:S(2)}, u32[]{:S(2)}) collective-permute-start(bf16[512,128]{1,0:T(8,128)(2,1)} %bitcast.19), channel_id=1, source_target_pairs={{0,12},{1,13},{2,14},{3,15},{4,0},{5,1},{6,2},{7,3},{8,4},{9,5},{1... | collective-permute-start | bytes 393224 | tf_op jit(solution)/shard_map/ppermute | solution.py:49
  5.7 1.5 %collective-permute-start.2 = (bf16[512,128]{1,0:T(8,128)(2,1)}, bf16[512,128]{1,0:T(8,128)(2,1)S(1)}, u32[]{:S(2)}, u32[]{:S(2)}) collective-permute-start(bf16[512,128]{1,0:T(8,128)(2,1)} %bitcast.21), channel_id=1, source_target_pairs={{0,2},{1,3},{2,0},{3,1},{4,6},{5,7},{6,4},{7,5},{8,10},{9,11},{10,... | collective-permute-start | bytes 393224 | tf_op jit(solution)/shard_map/ppermute | solution.py:49
  7.3 2.0 %collective-permute-start.8 = (bf16[128,2048]{1,0:T(8,128)(2,1)}, bf16[128,2048]{1,0:T(8,128)(2,1)}, u32[]{:S(2)}, u32[]{:S(2)}) collective-permute-start(bf16[128,2048]{1,0:T(8,128)(2,1)} %bitcast.12), channel_id=1, source_target_pairs={{0,2},{1,3},{4,0},{5,1},{8,4},{9,5},{12,8},{13,9},{14,12},{15,13},... | collective-permute-start | bytes 1572872 | tf_op jit(solution)/shard_map/ppermute | solution.py:40
  9.3 0.7 fusion.2
  10.0 0.8 copy.9.pos_ref
  10.7 1.0 %copy-done.8 = bf16[1,128,2048]{2,1,0:T(8,128)(2,1)S(1)} copy-done((bf16[1,128,2048]{2,1,0:T(8,128)(2,1)S(1)}, bf16[1,128,2048]{2,1,0:T(8,128)(2,1)}, u32[]{:S(2)}) %copy-start.8) | copy-done | bytes 524312
  11.8 1.6 %shard_map.86 = bf16[16,144,128]{2,1,0:T(8,128)(2,1)} custom-call(s32[4,2]{1,0:T(4,128)S(1)} %copy.9.pos_ref, bf16[128,2048]{1,0:T(8,128)(2,1)S(1)} %bitcast.16), custom_call_target="tpu_custom_call" | custom-call | bytes 128 | tf_op jit(solution)/shard_map/pallas_call | solution.py:75
  13.4 0.6 pad_add_fusion.place_ref
  14.0 3.9 %collective-permute-start.3 = (bf16[512,128]{1,0:T(8,128)(2,1)S(1)}, bf16[512,128]{1,0:T(8,128)(2,1)S(1)}, u32[]{:S(2)}, u32[]{:S(2)}) collective-permute-start(bf16[512,128]{1,0:T(8,128)(2,1)S(1)} %collective-permute-done), channel_id=1, source_target_pairs={{0,12},{1,13},{2,14},{3,15},{4,0},{5,1},{6,2},{7,3},{8,4},{9,5},{1... | collective-permute-start | bytes 393224 | tf_op jit(solution)/shard_map/ppermute | solution.py:49
  17.9 0.9 constant_dynamic-update-slice_fusion.7
  18.8 0.6 collective-permute-start.4
  19.4 1.5 %collective-permute-start.5 = (bf16[512,128]{1,0:T(8,128)(2,1)S(1)}, bf16[512,128]{1,0:T(8,128)(2,1)S(1)}, u32[]{:S(2)}, u32[]{:S(2)}) collective-permute-start(bf16[512,128]{1,0:T(8,128)(2,1)S(1)} %collective-permute-done.1), channel_id=1, source_target_pairs={{0,2},{1,3},{2,0},{3,1},{4,6},{5,7},{6,4},{7,5},{8,10},{9,11},{10,... | collective-permute-start | bytes 393224 | tf_op jit(solution)/shard_map/ppermute | solution.py:49
  20.9 3.6 %all-to-all-start = ((bf16[16,144,128]{2,1,0:T(8,128)(2,1)}), bf16[16,144,128]{2,1,0:T(8,128)(2,1)S(1)}, u32[]{:S(2)}, u32[]{:S(2)}) async-start(bf16[16,144,128]{2,1,0:T(8,128)(2,1)} %shard_map.86), calls=%async_computation | async-start | bytes 1179648 | tf_op jit(solution)/shard_map/all_to_all | solution.py:334
  24.5 1.7 %collective-permute-done.3 = bf16[512,128]{1,0:T(8,128)(2,1)S(1)} collective-permute-done((bf16[512,128]{1,0:T(8,128)(2,1)S(1)}, bf16[512,128]{1,0:T(8,128)(2,1)S(1)}, u32[]{:S(2)}, u32[]{:S(2)}) %collective-permute-start.3) | collective-permute-done | bytes 131104 | tf_op jit(solution)/shard_map/ppermute | solution.py:49
  26.2 1.5 %collective-permute-start.9 = (bf16[128,2048]{1,0:T(8,128)(2,1)S(1)}, bf16[128,2048]{1,0:T(8,128)(2,1)S(1)}, u32[]{:S(2)}, u32[]{:S(2)}) collective-permute-start(bf16[128,2048]{1,0:T(8,128)(2,1)S(1)} %bitcast.18), channel_id=1, source_target_pairs={{16,0},{0,16},{17,1},{1,17},{18,2},{2,18},{19,3},{3,19},{20,4},{4,... | collective-permute-start | bytes 1572872 | tf_op jit(solution)/shard_map/ppermute | solution.py:327
  28.0 2.6 %collective-permute-start.6 = (bf16[512,128]{1,0:T(8,128)(2,1)S(1)}, bf16[512,128]{1,0:T(8,128)(2,1)S(1)}, u32[]{:S(2)}, u32[]{:S(2)}) collective-permute-start(bf16[512,128]{1,0:T(8,128)(2,1)S(1)} %collective-permute-done.3), channel_id=1, source_target_pairs={{0,2},{1,3},{2,0},{3,1},{4,6},{5,7},{6,4},{7,5},{8,10},{9,11},{10,... | collective-permute-start | bytes 393224 | tf_op jit(solution)/shard_map/ppermute | solution.py:49
  30.7 4.2 %collective-permute-done.6 = bf16[512,128]{1,0:T(8,128)(2,1)S(1)} collective-permute-done((bf16[512,128]{1,0:T(8,128)(2,1)S(1)}, bf16[512,128]{1,0:T(8,128)(2,1)S(1)}, u32[]{:S(2)}, u32[]{:S(2)}) %collective-permute-start.6) | collective-permute-done | bytes 131104 | tf_op jit(solution)/shard_map/ppermute | solution.py:49
  34.9 4.5 %collective-permute-done.9 = bf16[128,2048]{1,0:T(8,128)(2,1)S(1)} collective-permute-done((bf16[128,2048]{1,0:T(8,128)(2,1)S(1)}, bf16[128,2048]{1,0:T(8,128)(2,1)S(1)}, u32[]{:S(2)}, u32[]{:S(2)}) %collective-permute-start.9) | collective-permute-done | bytes 524320 | tf_op jit(solution)/shard_map/ppermute | solution.py:327
  39.5 1.2 %collective-permute-start.11 = (bf16[128,2048]{1,0:T(8,128)(2,1)}, bf16[128,2048]{1,0:T(8,128)(2,1)}, u32[]{:S(2)}, u32[]{:S(2)}) collective-permute-start(bf16[128,2048]{1,0:T(8,128)(2,1)} %collective-permute-done.7.refs_1_), channel_id=1, source_target_pairs={{0,4},{1,5},{4,8},{5,9},{8,12},{9,13},{12,14},{13,15},{14,10},{15,... | collective-permute-start | bytes 1572872 | tf_op jit(solution)/shard_map/ppermute | solution.py:40
  40.7 0.9 collective-permute-start.12
  41.6 0.9 broadcast_select_fusion.next_in
  42.5 0.8 copy-done.1
  43.3 1.0 copy-done.5
  44.3 7.3 %shard_map.87.refs_5_.refs_2_ = bf16[256,2048]{1,0:T(8,128)(2,1)} custom-call(s32[10]{0:T(128)} %pad_add_fusion.place_ref, bf16[4096,128]{1,0:T(8,128)(2,1)} %copy-done.3, bf16[4096,128]{1,0:T(8,128)(2,1)} %copy-done.5, bf16[16,144,128]{2,1,0:T(8,128)(2,1)} %copy-done.1, bf16[128,2048]{1,0:T(8,128)(2,1)} %bitcast.17, bf16[128,2048]{1,0:T(8,128)(2,1)} %bitcast.15, ...), custom_call_target="tpu_custom_call" | custom-call | bytes 128 | tf_op jit(solution)/shard_map/pallas_call | solution.py:168
  51.6 2.5 %collective-permute-done.11.refs_3_ = bf16[128,2048]{1,0:T(8,128)(2,1)} collective-permute-done((bf16[128,2048]{1,0:T(8,128)(2,1)}, bf16[128,2048]{1,0:T(8,128)(2,1)}, u32[]{:S(2)}, u32[]{:S(2)}) %collective-permute-start.11) | collective-permute-done | bytes 524320 | tf_op jit(solution)/shard_map/ppermute | solution.py:40
  54.2 0.8 collective-permute-done.12.refs_4_
  55.0 1.6 %collective-permute-start.16 = (bf16[128,2048]{1,0:T(8,128)(2,1)}, bf16[128,2048]{1,0:T(8,128)(2,1)S(1)}, u32[]{:S(2)}, u32[]{:S(2)}) collective-permute-start(bf16[128,2048]{1,0:T(8,128)(2,1)} %collective-permute-done.11.refs_3_), channel_id=1, source_target_pairs={{0,4},{1,5},{4,8},{5,9},{8,12},{9,13},{12,14},{13,15},{14,10},{15,... | collective-permute-start | bytes 1572872 | tf_op jit(solution)/shard_map/ppermute | solution.py:40
  56.6 0.5 collective-permute-start.17
  57.1 0.8 collective-permute-done.13.refs_6_.refs_3_
  57.9 1.2 %copy-done = bf16[256,2048]{1,0:T(8,128)(2,1)S(1)} copy-done((bf16[256,2048]{1,0:T(8,128)(2,1)S(1)}, bf16[256,2048]{1,0:T(8,128)(2,1)}, u32[]{:S(2)}) %copy-start) | copy-done | bytes 1048600
  59.1 3.7 %shard_map.88 = (bf16[128,512]{1,0:T(8,128)(2,1)S(1)}, bf16[128,512]{1,0:T(8,128)(2,1)S(1)}, bf16[128,512]{1,0:T(8,128)(2,1)S(1)}, bf16[128,512]{1,0:T(8,128)(2,1)}, bf16[128,512]{1,0:T(8,128)(2,1)}) custom-call(bf16[128,2048]{1,0:T(8,128)(2,1)S(1)} %bitcast.13, bf16[128,2048]{1,0:T(8,128)(2,1)} %collective-permute-done.7.refs_1_, ...), custom_call_target="tpu_custom_call" | custom-call | bytes 512 | tf_op jit(solution)/shard_map/pallas_call | solution.py:254
  62.9 0.9 collective-permute-start.14
  63.8 1.1 %collective-permute-start.15 = (bf16[128,512]{1,0:T(8,128)(2,1)S(1)}, bf16[128,512]{1,0:T(8,128)(2,1)S(1)}, u32[]{:S(2)}, u32[]{:S(2)}) collective-permute-start(bf16[128,512]{1,0:T(8,128)(2,1)S(1)} %get-tuple-element.47), channel_id=1, source_target_pairs={{0,4},{1,5},{4,8},{5,9},{8,12},{9,13},{12,14},{13,15},{14,10},{15,... | collective-permute-start | bytes 393224 | tf_op jit(solution)/shard_map/ppermute | solution.py:40
  64.9 5.1 %collective-permute-done.16.refs_0_ = bf16[128,2048]{1,0:T(8,128)(2,1)S(1)} collective-permute-done((bf16[128,2048]{1,0:T(8,128)(2,1)}, bf16[128,2048]{1,0:T(8,128)(2,1)S(1)}, u32[]{:S(2)}, u32[]{:S(2)}) %collective-permute-start.16) | collective-permute-done | bytes 524320 | tf_op jit(solution)/shard_map/ppermute | solution.py:40
  70.0 1.6 %collective-permute-done.17.refs_1_ = bf16[128,2048]{1,0:T(8,128)(2,1)S(1)} collective-permute-done((bf16[128,2048]{1,0:T(8,128)(2,1)}, bf16[128,2048]{1,0:T(8,128)(2,1)S(1)}, u32[]{:S(2)}, u32[]{:S(2)}) %collective-permute-start.17) | collective-permute-done | bytes 524320 | tf_op jit(solution)/shard_map/ppermute | solution.py:40
  71.5 2.1 %collective-permute-done.14.refs_1_ = bf16[128,512]{1,0:T(8,128)(2,1)S(1)} collective-permute-done((bf16[128,512]{1,0:T(8,128)(2,1)S(1)}, bf16[128,512]{1,0:T(8,128)(2,1)S(1)}, u32[]{:S(2)}, u32[]{:S(2)}) %collective-permute-start.14) | collective-permute-done | bytes 131104 | tf_op jit(solution)/shard_map/ppermute | solution.py:40
  73.7 1.8 %collective-permute-start.20 = (bf16[64,2048]{1,0:T(8,128)(2,1)S(1)}, bf16[64,2048]{1,0:T(8,128)(2,1)S(1)}, u32[]{:S(2)}, u32[]{:S(2)}) collective-permute-start(bf16[64,2048]{1,0:T(8,128)(2,1)S(1)} %slice.6), channel_id=1, source_target_pairs={{0,4},{1,5},{4,8},{5,9},{8,12},{9,13},{12,14},{13,15},{14,10},{15,... | collective-permute-start | bytes 786440 | tf_op jit(solution)/shard_map/ppermute | solution.py:40
  75.8 0.8 collective-permute-start.18
  76.6 2.1 %collective-permute-start.24 = (bf16[128,512]{1,0:T(8,128)(2,1)}, bf16[128,512]{1,0:T(8,128)(2,1)}, u32[]{:S(2)}, u32[]{:S(2)}) collective-permute-start(bf16[128,512]{1,0:T(8,128)(2,1)} %get-tuple-element.54), channel_id=1, source_target_pairs={{0,8},{1,9},{4,12},{5,13},{8,14},{9,15},{12,10},{13,11},{14,6},{15... | collective-permute-start | bytes 393224 | tf_op jit(solution)/shard_map/ppermute | solution.py:40
  78.8 1.4 %shard_map.89 = (bf16[128,512]{1,0:T(8,128)(2,1)}, bf16[128,512]{1,0:T(8,128)(2,1)}) custom-call(bf16[128,2048]{1,0:T(8,128)(2,1)S(1)} %collective-permute-done.16.refs_0_, bf16[128,2048]{1,0:T(8,128)(2,1)S(1)} %collective-permute-done.17.refs_1_, bf16[256,2048]{1,0:T(8,128)(2,1)S(1)} %copy-done, bf16[256,2048]{1,0:T(8,128)(2,1)S(1)} %collective-permute-done.13.refs_6_.refs_3_), custom_call_target="tpu_custom_call" | custom-call | bytes 512 | tf_op jit(solution)/shard_map/pallas_call | solution.py:254
  80.2 1.2 %collective-permute-start.19 = (bf16[128,512]{1,0:T(8,128)(2,1)}, bf16[128,512]{1,0:T(8,128)(2,1)}, u32[]{:S(2)}, u32[]{:S(2)}) collective-permute-start(bf16[128,512]{1,0:T(8,128)(2,1)} %get-tuple-element.52), channel_id=1, source_target_pairs={{0,10},{1,11},{4,6},{5,7},{8,2},{9,3},{12,0},{13,1},{14,4},{15,5},... | collective-permute-start | bytes 393224 | tf_op jit(solution)/shard_map/ppermute | solution.py:40
  81.4 0.8 collective-permute-done.20.refs_0_
  82.2 4.7 %collective-permute-start.23 = (bf16[128,512]{1,0:T(8,128)(2,1)}, bf16[128,512]{1,0:T(8,128)(2,1)}, u32[]{:S(2)}, u32[]{:S(2)}) collective-permute-start(bf16[128,512]{1,0:T(8,128)(2,1)} %get-tuple-element.53), channel_id=1, source_target_pairs={{0,12},{1,13},{4,14},{5,15},{8,10},{9,11},{12,6},{13,7},{14,2},{15... | collective-permute-start | bytes 393224 | tf_op jit(solution)/shard_map/ppermute | solution.py:40
  86.9 1.5 %shard_map.90 = bf16[128,512]{1,0:T(8,128)(2,1)} custom-call(bf16[64,2048]{1,0:T(8,128)(2,1)S(1)} %collective-permute-done.20.refs_0_, bf16[64,2048]{1,0:T(8,128)(2,1)S(1)} %collective-permute-done.21.refs_1_, bf16[256,2048]{1,0:T(8,128)(2,1)S(1)} %copy-done, bf16[256,2048]{1,0:T(8,128)(2,1)S(1)} %collective-permute-done.13.refs_6_.refs_3_), custom_call_target="tpu_custom_call" | custom-call | bytes 512 | tf_op jit(solution)/shard_map/pallas_call | solution.py:254
  88.4 2.5 %collective-permute-start.22 = (bf16[128,512]{1,0:T(8,128)(2,1)}, bf16[128,512]{1,0:T(8,128)(2,1)}, u32[]{:S(2)}, u32[]{:S(2)}) collective-permute-start(bf16[128,512]{1,0:T(8,128)(2,1)} %shard_map.90), channel_id=1, source_target_pairs={{0,14},{1,15},{4,10},{5,11},{8,6},{9,7},{12,2},{13,3},{14,0},{15,1... | collective-permute-start | bytes 393224 | tf_op jit(solution)/shard_map/ppermute | solution.py:40
  90.9 4.2 %shard_map.91.refs_8_ = bf16[128,4096]{1,0:T(8,128)(2,1)S(1)} custom-call(s32[10]{0:T(128)S(1)} %copy-done.11, bf16[4096,128]{1,0:T(8,128)(2,1)S(1)} %copy-done.4, bf16[4096,128]{1,0:T(8,128)(2,1)S(1)} %copy-done.6, bf16[16,144,128]{2,1,0:T(8,128)(2,1)S(1)} %copy-done.2, bf16[128,2048]{1,0:T(8,128)(2,1)S(1)} %bitcast.14), custom_call_target="tpu_custom_call" | custom-call | bytes 128 | tf_op jit(solution)/shard_map/pallas_call | solution.py:218
  95.1 4.8 %collective-permute-done.18.refs_2_ = bf16[128,512]{1,0:T(8,128)(2,1)} collective-permute-done((bf16[128,512]{1,0:T(8,128)(2,1)}, bf16[128,512]{1,0:T(8,128)(2,1)}, u32[]{:S(2)}, u32[]{:S(2)}) %collective-permute-start.18) | collective-permute-done | bytes 131104 | tf_op jit(solution)/shard_map/ppermute | solution.py:40
  99.9 3.2 %shard_map.92 = (f32[128,4096]{1,0:T(8,128)}, f32[128,128]{1,0:T(8,128)}) custom-call(s32[10]{0:T(128)S(1)} %copy-done.11, bf16[128,512]{1,0:T(8,128)(2,1)S(1)} %get-tuple-element.45.refs_0_, bf16[128,512]{1,0:T(8,128)(2,1)S(1)} %collective-permute-done.14.refs_1_, bf16[128,512]{1,0:T(8,128)(2,1)} %collective-permute-done.18.refs_2_, ...), custom_call_target="tpu_custom_call" | custom-call | bytes 128 | tf_op jit(solution)/shard_map/pallas_call | solution.py:289
  (52 shorter events, 0.9 us)
Async XLA Ops:
  0.6 13.4 %collective-permute-start = (bf16[512,128]{1,0:T(8,128)(2,1)}, bf16[512,128]{1,0:T(8,128)(2,1)S(1)}, u32[]{:S(2)}, u32[]{:S(2)}) collective-permute-start(bf16[512,128]{1,0:T(8,128)(2,1)} %bitcast.19), channel_id=1, source_target_pairs={{0,12},{1,13},{2,14},{3,15},{4,0},{5,1},{6,2},{7,3},{8,4},{9,5},{1... | collective-permute-start | bytes 393224 | tf_op jit(solution)/shard_map/ppermute | solution.py:49
  5.7 8.3 %collective-permute-start.1 = (bf16[512,128]{1,0:T(8,128)(2,1)}, bf16[512,128]{1,0:T(8,128)(2,1)S(1)}, u32[]{:S(2)}, u32[]{:S(2)}) collective-permute-start(bf16[512,128]{1,0:T(8,128)(2,1)} %bitcast.20), channel_id=1, source_target_pairs={{0,4},{1,5},{2,6},{3,7},{4,8},{5,9},{6,10},{7,11},{8,12},{9,13},{1... | collective-permute-start | bytes 393224 | tf_op jit(solution)/shard_map/ppermute | solution.py:49
  5.7 8.3 %collective-permute-start.2 = (bf16[512,128]{1,0:T(8,128)(2,1)}, bf16[512,128]{1,0:T(8,128)(2,1)S(1)}, u32[]{:S(2)}, u32[]{:S(2)}) collective-permute-start(bf16[512,128]{1,0:T(8,128)(2,1)} %bitcast.21), channel_id=1, source_target_pairs={{0,2},{1,3},{2,0},{3,1},{4,6},{5,7},{6,4},{7,5},{8,10},{9,11},{10,... | collective-permute-start | bytes 393224 | tf_op jit(solution)/shard_map/ppermute | solution.py:49
  7.3 27.7 %collective-permute-start.7 = (bf16[128,2048]{1,0:T(8,128)(2,1)}, bf16[128,2048]{1,0:T(8,128)(2,1)}, u32[]{:S(2)}, u32[]{:S(2)}) collective-permute-start(bf16[128,2048]{1,0:T(8,128)(2,1)} %bitcast.11), channel_id=1, source_target_pairs={{0,4},{1,5},{4,8},{5,9},{8,12},{9,13},{12,14},{13,15},{14,10},{15,... | collective-permute-start | bytes 1572872 | tf_op jit(solution)/shard_map/ppermute | solution.py:40
  7.3 27.7 %collective-permute-start.8 = (bf16[128,2048]{1,0:T(8,128)(2,1)}, bf16[128,2048]{1,0:T(8,128)(2,1)}, u32[]{:S(2)}, u32[]{:S(2)}) collective-permute-start(bf16[128,2048]{1,0:T(8,128)(2,1)} %bitcast.12), channel_id=1, source_target_pairs={{0,2},{1,3},{4,0},{5,1},{8,4},{9,5},{12,8},{13,9},{14,12},{15,13},... | collective-permute-start | bytes 1572872 | tf_op jit(solution)/shard_map/ppermute | solution.py:40
  10.7 1.0 %copy-start.8 = (bf16[1,128,2048]{2,1,0:T(8,128)(2,1)S(1)}, bf16[1,128,2048]{2,1,0:T(8,128)(2,1)}, u32[]{:S(2)}) copy-start(bf16[1,128,2048]{2,1,0:T(8,128)(2,1)} %param.11) | copy-start | bytes 1572868
  11.8 14.4 %copy-start.12 = (bf16[1,128,2048]{2,1,0:T(8,128)(2,1)S(1)}, bf16[1,128,2048]{2,1,0:T(8,128)(2,1)}, u32[]{:S(2)}) copy-start(bf16[1,128,2048]{2,1,0:T(8,128)(2,1)} %param.10) | copy-start | bytes 1572868
  14.0 12.2 %collective-permute-start.3 = (bf16[512,128]{1,0:T(8,128)(2,1)S(1)}, bf16[512,128]{1,0:T(8,128)(2,1)S(1)}, u32[]{:S(2)}, u32[]{:S(2)}) collective-permute-start(bf16[512,128]{1,0:T(8,128)(2,1)S(1)} %collective-permute-done), channel_id=1, source_target_pairs={{0,12},{1,13},{2,14},{3,15},{4,0},{5,1},{6,2},{7,3},{8,4},{9,5},{1... | collective-permute-start | bytes 393224 | tf_op jit(solution)/shard_map/ppermute | solution.py:49
  18.8 8.9 %collective-permute-start.4 = (bf16[512,128]{1,0:T(8,128)(2,1)S(1)}, bf16[512,128]{1,0:T(8,128)(2,1)S(1)}, u32[]{:S(2)}, u32[]{:S(2)}) collective-permute-start(bf16[512,128]{1,0:T(8,128)(2,1)S(1)} %collective-permute-done), channel_id=1, source_target_pairs={{0,2},{1,3},{2,0},{3,1},{4,6},{5,7},{6,4},{7,5},{8,10},{9,11},{10,... | collective-permute-start | bytes 393224 | tf_op jit(solution)/shard_map/ppermute | solution.py:49
  19.4 8.6 %collective-permute-start.5 = (bf16[512,128]{1,0:T(8,128)(2,1)S(1)}, bf16[512,128]{1,0:T(8,128)(2,1)S(1)}, u32[]{:S(2)}, u32[]{:S(2)}) collective-permute-start(bf16[512,128]{1,0:T(8,128)(2,1)S(1)} %collective-permute-done.1), channel_id=1, source_target_pairs={{0,2},{1,3},{2,0},{3,1},{4,6},{5,7},{6,4},{7,5},{8,10},{9,11},{10,... | collective-permute-start | bytes 393224 | tf_op jit(solution)/shard_map/ppermute | solution.py:49
  20.9 21.6 %all-to-all-start = ((bf16[16,144,128]{2,1,0:T(8,128)(2,1)}), bf16[16,144,128]{2,1,0:T(8,128)(2,1)S(1)}, u32[]{:S(2)}, u32[]{:S(2)}) async-start(bf16[16,144,128]{2,1,0:T(8,128)(2,1)} %shard_map.86), calls=%async_computation | async-start | bytes 1179648 | tf_op jit(solution)/shard_map/all_to_all | solution.py:334
  26.2 13.2 %collective-permute-start.9 = (bf16[128,2048]{1,0:T(8,128)(2,1)S(1)}, bf16[128,2048]{1,0:T(8,128)(2,1)S(1)}, u32[]{:S(2)}, u32[]{:S(2)}) collective-permute-start(bf16[128,2048]{1,0:T(8,128)(2,1)S(1)} %bitcast.18), channel_id=1, source_target_pairs={{16,0},{0,16},{17,1},{1,17},{18,2},{2,18},{19,3},{3,19},{20,4},{4,... | collective-permute-start | bytes 1572872 | tf_op jit(solution)/shard_map/ppermute | solution.py:327
  28.0 6.9 %collective-permute-start.6 = (bf16[512,128]{1,0:T(8,128)(2,1)S(1)}, bf16[512,128]{1,0:T(8,128)(2,1)S(1)}, u32[]{:S(2)}, u32[]{:S(2)}) collective-permute-start(bf16[512,128]{1,0:T(8,128)(2,1)S(1)} %collective-permute-done.3), channel_id=1, source_target_pairs={{0,2},{1,3},{2,0},{3,1},{4,6},{5,7},{6,4},{7,5},{8,10},{9,11},{10,... | collective-permute-start | bytes 393224 | tf_op jit(solution)/shard_map/ppermute | solution.py:49
  39.4 3.1 %copy-start.3 = (bf16[4096,128]{1,0:T(8,128)(2,1)}, bf16[4096,128]{1,0:T(8,128)(2,1)S(1)}, u32[]{:S(2)}) copy-start(bf16[4096,128]{1,0:T(8,128)(2,1)S(1)} %constant_dynamic-update-slice_fusion.near_ref) | copy-start | bytes 3145732
  39.5 3.0 %collective-permute-start.10 = (bf16[4096,128]{1,0:T(8,128)(2,1)S(1)}, bf16[4096,128]{1,0:T(8,128)(2,1)S(1)}, u32[]{:S(2)}, u32[]{:S(2)}) collective-permute-start(bf16[4096,128]{1,0:T(8,128)(2,1)S(1)} %constant_dynamic-update-slice_fusion.near_ref), channel_id=1, source_target_pairs={{0,1},{1,0},{2,3},{3,2},{4,5},{5,4},{6,7},{7,6},{8,9},{9,8},{10,11... | collective-permute-start | bytes 3145736 | tf_op jit(solution)/shard_map/ppermute | solution.py:53
  39.5 14.6 %collective-permute-start.11 = (bf16[128,2048]{1,0:T(8,128)(2,1)}, bf16[128,2048]{1,0:T(8,128)(2,1)}, u32[]{:S(2)}, u32[]{:S(2)}) collective-permute-start(bf16[128,2048]{1,0:T(8,128)(2,1)} %collective-permute-done.7.refs_1_), channel_id=1, source_target_pairs={{0,4},{1,5},{4,8},{5,9},{8,12},{9,13},{12,14},{13,15},{14,10},{15,... | collective-permute-start | bytes 1572872 | tf_op jit(solution)/shard_map/ppermute | solution.py:40
  40.7 14.3 %collective-permute-start.12 = (bf16[128,2048]{1,0:T(8,128)(2,1)}, bf16[128,2048]{1,0:T(8,128)(2,1)}, u32[]{:S(2)}, u32[]{:S(2)}) collective-permute-start(bf16[128,2048]{1,0:T(8,128)(2,1)} %collective-permute-done.8.refs_2_), channel_id=1, source_target_pairs={{0,2},{1,3},{4,0},{5,1},{8,4},{9,5},{12,8},{13,9},{14,12},{15,13},... | collective-permute-start | bytes 1572872 | tf_op jit(solution)/shard_map/ppermute | solution.py:40
  42.5 15.4 %copy-start.7 = (bf16[1,128,2048]{2,1,0:T(8,128)(2,1)S(1)}, bf16[1,128,2048]{2,1,0:T(8,128)(2,1)}, u32[]{:S(2)}) copy-start(bf16[1,128,2048]{2,1,0:T(8,128)(2,1)} %param.7) | copy-start | bytes 1572868
  42.5 0.8 copy-start.1
  43.3 1.0 copy-start.5
  55.0 2.9 %collective-permute-start.13 = (bf16[256,2048]{1,0:T(8,128)(2,1)}, bf16[256,2048]{1,0:T(8,128)(2,1)S(1)}, u32[]{:S(2)}, u32[]{:S(2)}) collective-permute-start(bf16[256,2048]{1,0:T(8,128)(2,1)} %shard_map.87.refs_5_.refs_2_), channel_id=1, source_target_pairs={{0,1},{1,0},{2,3},{3,2},{4,5},{5,4},{6,7},{7,6},{8,9},{9,8},{10,11... | collective-permute-start | bytes 3145736 | tf_op jit(solution)/shard_map/ppermute | solution.py:53
  55.0 14.9 %collective-permute-start.16 = (bf16[128,2048]{1,0:T(8,128)(2,1)}, bf16[128,2048]{1,0:T(8,128)(2,1)S(1)}, u32[]{:S(2)}, u32[]{:S(2)}) collective-permute-start(bf16[128,2048]{1,0:T(8,128)(2,1)} %collective-permute-done.11.refs_3_), channel_id=1, source_target_pairs={{0,4},{1,5},{4,8},{5,9},{8,12},{9,13},{12,14},{13,15},{14,10},{15,... | collective-permute-start | bytes 1572872 | tf_op jit(solution)/shard_map/ppermute | solution.py:40
  56.6 15.0 %collective-permute-start.17 = (bf16[128,2048]{1,0:T(8,128)(2,1)}, bf16[128,2048]{1,0:T(8,128)(2,1)S(1)}, u32[]{:S(2)}, u32[]{:S(2)}) collective-permute-start(bf16[128,2048]{1,0:T(8,128)(2,1)} %collective-permute-done.12.refs_4_), channel_id=1, source_target_pairs={{0,2},{1,3},{4,0},{5,1},{8,4},{9,5},{12,8},{13,9},{14,12},{15,13},... | collective-permute-start | bytes 1572872 | tf_op jit(solution)/shard_map/ppermute | solution.py:40
  57.9 1.2 %copy-start = (bf16[256,2048]{1,0:T(8,128)(2,1)S(1)}, bf16[256,2048]{1,0:T(8,128)(2,1)}, u32[]{:S(2)}) copy-start(bf16[256,2048]{1,0:T(8,128)(2,1)} %shard_map.87.refs_5_.refs_2_) | copy-start | bytes 3145732
  62.9 10.8 %collective-permute-start.14 = (bf16[128,512]{1,0:T(8,128)(2,1)S(1)}, bf16[128,512]{1,0:T(8,128)(2,1)S(1)}, u32[]{:S(2)}, u32[]{:S(2)}) collective-permute-start(bf16[128,512]{1,0:T(8,128)(2,1)S(1)} %get-tuple-element.46), channel_id=1, source_target_pairs={{0,2},{1,3},{4,0},{5,1},{8,4},{9,5},{12,8},{13,9},{14,12},{15,13},... | collective-permute-start | bytes 393224 | tf_op jit(solution)/shard_map/ppermute | solution.py:40
  63.8 9.9 %collective-permute-start.15 = (bf16[128,512]{1,0:T(8,128)(2,1)S(1)}, bf16[128,512]{1,0:T(8,128)(2,1)S(1)}, u32[]{:S(2)}, u32[]{:S(2)}) collective-permute-start(bf16[128,512]{1,0:T(8,128)(2,1)S(1)} %get-tuple-element.47), channel_id=1, source_target_pairs={{0,4},{1,5},{4,8},{5,9},{8,12},{9,13},{12,14},{13,15},{14,10},{15,... | collective-permute-start | bytes 393224 | tf_op jit(solution)/shard_map/ppermute | solution.py:40
  73.7 6.5 %copy-start.9 = (bf16[128,512]{1,0:T(8,128)(2,1)}, bf16[128,512]{1,0:T(8,128)(2,1)S(1)}, u32[]{:S(2)}) copy-start(bf16[128,512]{1,0:T(8,128)(2,1)S(1)} %collective-permute-done.15.refs_7_) | copy-start | bytes 393220
  73.7 8.6 %collective-permute-start.20 = (bf16[64,2048]{1,0:T(8,128)(2,1)S(1)}, bf16[64,2048]{1,0:T(8,128)(2,1)S(1)}, u32[]{:S(2)}, u32[]{:S(2)}) collective-permute-start(bf16[64,2048]{1,0:T(8,128)(2,1)S(1)} %slice.6), channel_id=1, source_target_pairs={{0,4},{1,5},{4,8},{5,9},{8,12},{9,13},{12,14},{13,15},{14,10},{15,... | collective-permute-start | bytes 786440 | tf_op jit(solution)/shard_map/ppermute | solution.py:40
  75.5 11.4 %collective-permute-start.21 = (bf16[64,2048]{1,0:T(8,128)(2,1)S(1)}, bf16[64,2048]{1,0:T(8,128)(2,1)S(1)}, u32[]{:S(2)}, u32[]{:S(2)}) collective-permute-start(bf16[64,2048]{1,0:T(8,128)(2,1)S(1)} %slice.7), channel_id=1, source_target_pairs={{0,2},{1,3},{4,0},{5,1},{8,4},{9,5},{12,8},{13,9},{14,12},{15,13},... | collective-permute-start | bytes 786440 | tf_op jit(solution)/shard_map/ppermute | solution.py:40
  75.8 24.1 %collective-permute-start.18 = (bf16[128,512]{1,0:T(8,128)(2,1)}, bf16[128,512]{1,0:T(8,128)(2,1)}, u32[]{:S(2)}, u32[]{:S(2)}) collective-permute-start(bf16[128,512]{1,0:T(8,128)(2,1)} %get-tuple-element.49), channel_id=1, source_target_pairs={{0,6},{1,7},{4,2},{5,3},{8,0},{9,1},{12,4},{13,5},{14,8},{15,9},{1... | collective-permute-start | bytes 393224 | tf_op jit(solution)/shard_map/ppermute | solution.py:40
  76.6 23.3 %collective-permute-start.24 = (bf16[128,512]{1,0:T(8,128)(2,1)}, bf16[128,512]{1,0:T(8,128)(2,1)}, u32[]{:S(2)}, u32[]{:S(2)}) collective-permute-start(bf16[128,512]{1,0:T(8,128)(2,1)} %get-tuple-element.54), channel_id=1, source_target_pairs={{0,8},{1,9},{4,12},{5,13},{8,14},{9,15},{12,10},{13,11},{14,6},{15... | collective-permute-start | bytes 393224 | tf_op jit(solution)/shard_map/ppermute | solution.py:40
  80.2 10.7 %copy-start.2 = (bf16[16,144,128]{2,1,0:T(8,128)(2,1)S(1)}, bf16[16,144,128]{2,1,0:T(8,128)(2,1)}, u32[]{:S(2)}) copy-start(bf16[16,144,128]{2,1,0:T(8,128)(2,1)} %copy-done.1) | copy-start | bytes 1769476
  80.2 10.7 %copy-start.4 = (bf16[4096,128]{1,0:T(8,128)(2,1)S(1)}, bf16[4096,128]{1,0:T(8,128)(2,1)}, u32[]{:S(2)}) copy-start(bf16[4096,128]{1,0:T(8,128)(2,1)} %copy-done.3) | copy-start | bytes 3145732
  80.2 10.7 %copy-start.6 = (bf16[4096,128]{1,0:T(8,128)(2,1)S(1)}, bf16[4096,128]{1,0:T(8,128)(2,1)}, u32[]{:S(2)}) copy-start(bf16[4096,128]{1,0:T(8,128)(2,1)} %copy-done.5) | copy-start | bytes 3145732
  80.2 10.7 %copy-start.11 = (s32[10]{0:T(128)S(1)}, s32[10]{0:T(128)}, u32[]{:S(2)}) copy-start(s32[10]{0:T(128)} %pad_add_fusion.place_ref) | copy-start | bytes 124
  80.2 19.7 %collective-permute-start.19 = (bf16[128,512]{1,0:T(8,128)(2,1)}, bf16[128,512]{1,0:T(8,128)(2,1)}, u32[]{:S(2)}, u32[]{:S(2)}) collective-permute-start(bf16[128,512]{1,0:T(8,128)(2,1)} %get-tuple-element.52), channel_id=1, source_target_pairs={{0,10},{1,11},{4,6},{5,7},{8,2},{9,3},{12,0},{13,1},{14,4},{15,5},... | collective-permute-start | bytes 393224 | tf_op jit(solution)/shard_map/ppermute | solution.py:40
  82.2 17.7 %collective-permute-start.23 = (bf16[128,512]{1,0:T(8,128)(2,1)}, bf16[128,512]{1,0:T(8,128)(2,1)}, u32[]{:S(2)}, u32[]{:S(2)}) collective-permute-start(bf16[128,512]{1,0:T(8,128)(2,1)} %get-tuple-element.53), channel_id=1, source_target_pairs={{0,12},{1,13},{4,14},{5,15},{8,10},{9,11},{12,6},{13,7},{14,2},{15... | collective-permute-start | bytes 393224 | tf_op jit(solution)/shard_map/ppermute | solution.py:40
  88.4 11.5 %collective-permute-start.22 = (bf16[128,512]{1,0:T(8,128)(2,1)}, bf16[128,512]{1,0:T(8,128)(2,1)}, u32[]{:S(2)}, u32[]{:S(2)}) collective-permute-start(bf16[128,512]{1,0:T(8,128)(2,1)} %shard_map.90), channel_id=1, source_target_pairs={{0,14},{1,15},{4,10},{5,11},{8,6},{9,7},{12,2},{13,3},{14,0},{15,1... | collective-permute-start | bytes 393224 | tf_op jit(solution)/shard_map/ppermute | solution.py:40
  90.9 9.0 %copy-start.10 = (bf16[128,512]{1,0:T(8,128)(2,1)S(1)}, bf16[128,512]{1,0:T(8,128)(2,1)}, u32[]{:S(2)}) copy-start(bf16[128,512]{1,0:T(8,128)(2,1)} %copy-done.9) | copy-start | bytes 393220
